TPU v7x, 32 devices: a whole 2x2x4 slice. The times are simulated.
32 devices in a mesh: groups: 2 (over y), leaf: 8 (over z, x), rhs: 2 (over core).
Axes of the slice: x: 2, y: 2, z: 4, core: 2. Of those that a mesh axis runs over, the one named last changes fastest.
Arguments:
- sources: bfloat16 [2, 192, 8192], P(None, None, ('groups', 'leaf', 'rhs')), parts along dimension 2, may hold values from -6 to 6
- forward_field: bfloat16 [2, 192, 8192], P(None, None, ('groups', 'leaf', 'rhs')), parts along dimension 2, may hold values from -6 to 6
- row_bases: bfloat16 [3, 2, 8192, 512], P(None, None, ('groups', 'leaf', 'rhs')), parts along dimension 2, may hold values from -0.09375 to 0.09375
- col_bases: bfloat16 [3, 2, 8192, 512], P(None, None, ('groups', 'leaf', 'rhs')), parts along dimension 2, may hold values from -0.1875 to 0.1875
- near_blocks: bfloat16 [2, 64, 8, 128, 128], P(None, ('groups', 'leaf', 'rhs')), parts along dimension 1, may hold values from -0.125 to 0.125
- near_index: int32 [64, 8], P(('groups', 'leaf', 'rhs')), parts along dimension 0, may hold values from 0 to 31, as said below
- cluster_order: int32 [8192], P(('groups', 'leaf', 'rhs')), parts along dimension 0, may hold values from 0 to 4095, as said below
Outputs:
- adjoint_field: float32 [2, 192, 8192], P(None, None, ('groups', 'leaf', 'rhs')), parts along dimension 2
- admittance_grad: float32 [8192], P(('groups', 'leaf', 'rhs')), parts along dimension 0
There are 2 independent parts, one for each index of `groups`. A program takes and returns all parts, laid end to end along the dimension named above; each array names one. Nothing has to cross between parts.
Inputs may be any that keep to these rules, and one draw needn't show every extreme that they name: `near_index`: column 0 names the row's own block; every named block lies within 2 blocks of the row's own block. `cluster_order`: maps each aligned run of 256 tree positions (the panels of one device) onto the same run of panels, each panel once.
All inputs are finite; a program needn't handle non-finite values.
Results may differ from a plain program's by a relative error of at most 0.0023.
Values may be sent and summed in bfloat16 or wider, within the bound.
No kernel may reach another device: no remote copies, remote signals or barrier semaphores. Data moves between devices by JAX's collectives and lax.ppermute only.
A program may use at most 64 MiB of HBM per device.

v0:
```python
import math

import jax
import jax.numpy as jnp
from jax import lax
from jax.sharding import PartitionSpec as P


def from_behind(x, axis, by):
    peers = lax.axis_size(axis)
    pairs = [(i, i + by) for i in range(peers) if 0 <= i + by < peers]
    return lax.ppermute(x, axis, pairs)


def swapped(x, axis, distance):
    return lax.ppermute(x, axis, [(i, i ^ 1 << distance) for i in range(lax.axis_size(axis))])


def conj_product(first_operand, second_operand, pattern):
    real_part = jnp.einsum(
        pattern, first_operand[0], second_operand[0], preferred_element_type=jnp.float32
    ) + jnp.einsum(pattern, first_operand[1], second_operand[1], preferred_element_type=jnp.float32)
    imag_part = jnp.einsum(
        pattern, first_operand[1], second_operand[0], preferred_element_type=jnp.float32
    ) - jnp.einsum(pattern, first_operand[0], second_operand[1], preferred_element_type=jnp.float32)
    return jnp.stack([real_part, imag_part])


def expand_basis(coefficient, col_basis):
    real_part = jnp.einsum(
        "rk,nk->rn", coefficient[0], col_basis[0], preferred_element_type=jnp.float32
    ) - jnp.einsum("rk,nk->rn", coefficient[1], col_basis[1], preferred_element_type=jnp.float32)
    imag_part = jnp.einsum(
        "rk,nk->rn", coefficient[0], col_basis[1], preferred_element_type=jnp.float32
    ) + jnp.einsum("rk,nk->rn", coefficient[1], col_basis[0], preferred_element_type=jnp.float32)
    return jnp.stack([real_part, imag_part])


def body(sources, forward_field, row_bases, col_bases, near_blocks, near_index, cluster_order):
    panel_count = sources.shape[2]
    columns = sources.shape[1]
    device = lax.axis_index(("leaf", "rhs"))
    tree_bits = lax.axis_size(("leaf", "rhs")).bit_length() - 1
    level_total = row_bases.shape[0]
    local_order = cluster_order - device * panel_count
    tree_sources = jnp.take(sources, local_order, axis=2)
    partials = [
        conj_product(tree_sources, row_bases[level_number], "rn,nk->rk")
        for level_number in range(level_total)
    ]
    block_count = near_blocks.shape[1]
    block_size = near_blocks.shape[3]
    targets = near_index - device * block_count + block_count
    one_hot = (
        targets[:, :, None] == jnp.arange(3 * block_count, dtype=jnp.int32)[None, None, :]
    ).astype(jnp.float32)
    block_sources = tree_sources.reshape(2, columns, block_count, block_size)
    terms = conj_product(block_sources, near_blocks, "rib,ikbc->rikc")
    buffer = jnp.einsum("zrikc,ikj->zrjc", terms, one_hot, precision=lax.Precision.HIGHEST)
    from_right = from_behind(buffer[:, :, :block_count], ("leaf", "rhs"), -1)
    from_left = from_behind(buffer[:, :, 2 * block_count :], ("leaf", "rhs"), 1)
    near_field = buffer[:, :, block_count : 2 * block_count] + from_right + from_left
    adjoint_tree = near_field.reshape(2, columns, panel_count)
    level_sums = []
    for level_number in range(level_total):
        running = partials[level_number]
        for bit_number in range(tree_bits - level_number - 1):
            running = running + swapped(running, ("leaf", "rhs"), bit_number)
        level_sums.append(running.astype(jnp.bfloat16))
    for level_number in range(level_total):
        sibling = swapped(level_sums[level_number], ("leaf", "rhs"), tree_bits - level_number - 1)
        adjoint_tree = adjoint_tree + expand_basis(sibling, col_bases[level_number])
    adjoint_field = (
        jnp.zeros((2, columns, panel_count), jnp.float32).at[:, :, local_order].set(adjoint_tree)
    )
    forward_float = forward_field.astype(jnp.float32)
    gradient = -jnp.sum(adjoint_field * forward_float, axis=(0, 1)) / math.sqrt(columns)
    return (adjoint_field, gradient)


def solution(mesh):
    in_specs = (
        P(None, None, ("groups", "leaf", "rhs")),
        P(None, None, ("groups", "leaf", "rhs")),
        P(None, None, ("groups", "leaf", "rhs"), None),
        P(None, None, ("groups", "leaf", "rhs"), None),
        P(None, ("groups", "leaf", "rhs"), None, None, None),
        P(("groups", "leaf", "rhs"), None),
        P(("groups", "leaf", "rhs")),
    )
    out_specs = (P(None, None, ("groups", "leaf", "rhs")), P(("groups", "leaf", "rhs")))
    return jax.shard_map(body, mesh=mesh, in_specs=in_specs, out_specs=out_specs, check_vma=False)
```

profile of v0, /device:TPU:0, one launch (start us, length us, event | category | flops | bytes accessed | tf_op | source)
XLA Modules:
  0.0 117.9 jit_solution(8387722666161078869)
XLA Ops:
  0.6 1.2 %copy.37 = bf16[2,192,256]{1,0,2:T(2,128)(2,1)S(1)} copy(bf16[2,192,256]{2,1,0:T(8,128)(2,1)} %param.7) | data formatting | bytes 393216 | tf_op args[0]
  1.9 0.7 compare_and_fusion
  2.6 1.2 %gather_fusion = bf16[256,2,192]{2,1,0:T(2,128)(2,1)S(1)} fusion(bf16[2,192,256]{1,0,2:T(2,128)(2,1)S(1)} %copy.37, s32[1024]{0:T(1024)S(1)} %pad_clamp_fusion), kind=kCustom, calls=%fused_computation | custom fusion | bytes 394240 | tf_op jit(solution)/shard_map/jit(_take)/gather | solution.py:46
  3.8 0.9 fusion.67
  4.8 0.4 fusion.114
  6.3 0.9 pad_maximum_fusion.1
  7.3 0.5 collective-permute-start.2
  8.6 0.9 pad_maximum_fusion.2
  10.4 0.5 copy-done.3
  10.9 0.9 pad_maximum_fusion.3
  12.0 0.4 collective-permute-start.9
  12.6 0.4 fusion.19
  12.9 0.3 fusion.21
  13.3 0.4 subtract_bitcast_fusion
  13.7 0.3 copy-done.10
  14.0 0.4 add_bitcast_fusion
  14.3 0.3 pad_maximum_fusion
  14.7 3.1 %fusion.2 = f32[2,192,6,128]{3,2,1,0:T(8,128)S(1)} fusion(f32[2,192,2,8,128]{4,1,3,2,0:T(8,128)S(1)} %pad_maximum_fusion, s32[2,8]{1,0:T(2,128)S(1)} %subtract_add_fusion), kind=kOutput, calls=%fused_computation.7 | convolution fusion | flops 56623200 | bytes 4325440 | tf_op jit(solution)/shard_map/zrikc,ikj->zrjc/dot_general | solution.py:59
  17.8 0.3 fusion.113
  18.2 2.5 %collective-permute-start.1 = (f32[2,192,2,128]{3,2,1,0:T(2,128)S(1)}, f32[2,192,2,128]{3,2,1,0:T(2,128)S(1)}, u32[]{:S(2)}, u32[]{:S(2)}) collective-permute-start(f32[2,192,2,128]{3,2,1,0:T(2,128)S(1)} %get-tuple-element.13), channel_id=1, source_target_pairs={{0,1},{1,2},{2,3},{3,4},{4,5},{5,6},{6,7},{7,8},{8,9},{9,10},{10,1... | collective-permute-start | bytes 1179656 | tf_op jit(solution)/shard_map/ppermute | solution.py:12
  20.7 1.5 %collective-permute-start = (f32[2,192,2,128]{3,2,1,0:T(2,128)S(1)}, f32[2,192,2,128]{3,2,1,0:T(2,128)S(1)}, u32[]{:S(2)}, u32[]{:S(2)}) collective-permute-start(f32[2,192,2,128]{3,2,1,0:T(2,128)S(1)} %get-tuple-element.12), channel_id=1, source_target_pairs={{1,0},{2,1},{3,2},{4,3},{5,4},{6,5},{7,6},{8,7},{9,8},{10,9},{11,1... | collective-permute-start | bytes 1179656 | tf_op jit(solution)/shard_map/ppermute | solution.py:12
  22.2 2.2 %fusion.112 = f32[2,192,512]{2,1,0:T(8,128)} fusion(f32[2,192,512]{2,1,0:T(8,128)} %collective-permute-done.2, f32[1,192,512]{2,1,0:T(8,128)S(1)} %fusion.9, f32[1,192,512]{2,1,0:T(8,128)S(1)} %fusion.10), kind=kLoop, calls=%fused_computation.148 | loop fusion | flops 393216 | bytes 2359296 | tf_op jit(solution)/shard_map/add | solution.py:68
  24.3 4.9 %collective-permute-start.3 = (f32[2,192,512]{2,1,0:T(8,128)}, f32[2,192,512]{2,1,0:T(8,128)}, u32[]{:S(2)}, u32[]{:S(2)}) collective-permute-start(f32[2,192,512]{2,1,0:T(8,128)} %fusion.112), channel_id=1, source_target_pairs={{0,2},{1,3},{2,0},{3,1},{4,6},{5,7},{6,4},{7,5},{8,10},{9,11},{10,... | collective-permute-start | bytes 2359304 | tf_op jit(solution)/shard_map/ppermute | solution.py:16
  29.2 2.0 %add_convert_fusion = bf16[2,192,512]{2,1,0:T(8,128)(2,1)} fusion(f32[2,192,512]{2,1,0:T(8,128)} %collective-permute-done.9, f32[1,192,512]{2,1,0:T(8,128)S(1)} %copy-done.4, f32[1,192,512]{2,1,0:T(8,128)S(1)} %copy-done.6), kind=kLoop, calls=%fused_computation.35 | loop fusion | flops 589824 | bytes 1966080 | tf_op jit(solution)/shard_map/convert_element_type | solution.py:69
  31.2 2.2 %fusion.111 = f32[2,192,512]{2,1,0:T(8,128)} fusion(f32[2,192,512]{2,1,0:T(8,128)} %collective-permute-done.6, f32[1,192,512]{2,1,0:T(8,128)S(1)} %fusion.7, f32[1,192,512]{2,1,0:T(8,128)S(1)} %fusion.8), kind=kLoop, calls=%fused_computation.147 | loop fusion | flops 393216 | bytes 2359296 | tf_op jit(solution)/shard_map/add | solution.py:68
  33.4 2.0 %collective-permute-start.7 = (f32[2,192,512]{2,1,0:T(8,128)}, f32[2,192,512]{2,1,0:T(8,128)}, u32[]{:S(2)}, u32[]{:S(2)}) collective-permute-start(f32[2,192,512]{2,1,0:T(8,128)} %fusion.111), channel_id=1, source_target_pairs={{0,2},{1,3},{2,0},{3,1},{4,6},{5,7},{6,4},{7,5},{8,10},{9,11},{10,... | collective-permute-start | bytes 2359304 | tf_op jit(solution)/shard_map/ppermute | solution.py:16
  35.4 0.4 fusion.27
  35.8 1.1 reshape.42
  36.8 23.2 %collective-permute-done.10 = bf16[2,192,512]{2,1,0:T(8,128)(2,1)} collective-permute-done((bf16[2,192,512]{2,1,0:T(8,128)(2,1)}, bf16[2,192,512]{2,1,0:T(8,128)(2,1)}, u32[]{:S(2)}, u32[]{:S(2)}) %collective-permute-start.10) | collective-permute-done | bytes 393248 | tf_op jit(solution)/shard_map/ppermute | solution.py:16
  60.0 1.2 fusion.34
  61.2 1.6 %fusion.115 = f32[2,192,512]{2,1,0:T(8,128)S(1)} fusion(f32[2,192,512]{2,1,0:T(8,128)} %collective-permute-done.3, f32[2,192,512]{2,1,0:T(8,128)} %collective-permute-done.2, f32[1,192,512]{2,1,0:T(8,128)S(1)} %fusion.9, f32[1,192,512]{2,1,0:T(8,128)S(1)} %fusion.10), kind=kLoop, calls=%fused_computation.151 | loop fusion | flops 589824 | bytes 3145728 | tf_op jit(solution)/shard_map/add | solution.py:68
  62.9 4.4 %collective-permute-start.4 = (f32[2,192,512]{2,1,0:T(8,128)S(1)}, f32[2,192,512]{2,1,0:T(8,128)S(1)}, u32[]{:S(2)}, u32[]{:S(2)}) collective-permute-start(f32[2,192,512]{2,1,0:T(8,128)S(1)} %fusion.115), channel_id=1, source_target_pairs={{0,4},{1,5},{2,6},{3,7},{4,0},{5,1},{6,2},{7,3},{8,12},{9,13},{10,... | collective-permute-start | bytes 2359304 | tf_op jit(solution)/shard_map/ppermute | solution.py:16
  67.3 7.5 %collective-permute-done.7 = f32[2,192,512]{2,1,0:T(8,128)} collective-permute-done((f32[2,192,512]{2,1,0:T(8,128)}, f32[2,192,512]{2,1,0:T(8,128)}, u32[]{:S(2)}, u32[]{:S(2)}) %collective-permute-start.7) | collective-permute-done | bytes 786464 | tf_op jit(solution)/shard_map/ppermute | solution.py:16
  74.8 1.6 %add_convert_fusion.1 = bf16[2,192,512]{2,1,0:T(8,128)(2,1)S(1)} fusion(f32[2,192,512]{2,1,0:T(8,128)} %collective-permute-done.7, f32[2,192,512]{2,1,0:T(8,128)} %collective-permute-done.6, f32[1,192,512]{2,1,0:T(8,128)S(1)} %fusion.7, f32[1,192,512]{2,1,0:T(8,128)S(1)} %fusion.8), kind=kLoop, calls=%fused_computation.36 | loop fusion | flops 786432 | bytes 2752512 | tf_op jit(solution)/shard_map/convert_element_type | solution.py:69
  76.4 3.0 %collective-permute-start.8 = (bf16[2,192,512]{2,1,0:T(8,128)(2,1)S(1)}, bf16[2,192,512]{2,1,0:T(8,128)(2,1)S(1)}, u32[]{:S(2)}, u32[]{:S(2)}) collective-permute-start(bf16[2,192,512]{2,1,0:T(8,128)(2,1)S(1)} %add_convert_fusion.1), channel_id=1, source_target_pairs={{0,4},{1,5},{2,6},{3,7},{4,0},{5,1},{6,2},{7,3},{8,12},{9,13},{10,... | collective-permute-start | bytes 1179656 | tf_op jit(solution)/shard_map/ppermute | solution.py:16
  79.4 1.2 fusion.11
  80.6 1.2 fusion.32
  81.7 1.2 fusion.12
  82.9 5.7 %collective-permute-done.8 = bf16[2,192,512]{2,1,0:T(8,128)(2,1)S(1)} collective-permute-done((bf16[2,192,512]{2,1,0:T(8,128)(2,1)S(1)}, bf16[2,192,512]{2,1,0:T(8,128)(2,1)S(1)}, u32[]{:S(2)}, u32[]{:S(2)}) %collective-permute-start.8) | collective-permute-done | bytes 393248 | tf_op jit(solution)/shard_map/ppermute | solution.py:16
  88.6 0.2 fusion.46
  89.1 2.7 %collective-permute-start.5 = (bf16[2,192,512]{2,1,0:T(8,128)(2,1)S(1)}, bf16[2,192,512]{2,1,0:T(8,128)(2,1)S(1)}, u32[]{:S(2)}, u32[]{:S(2)}) collective-permute-start(bf16[2,192,512]{2,1,0:T(8,128)(2,1)S(1)} %add_convert_fusion.2), channel_id=1, source_target_pairs={{0,8},{1,9},{2,10},{3,11},{4,12},{5,13},{6,14},{7,15},{8,0},{9,1},... | collective-permute-start | bytes 1179656 | tf_op jit(solution)/shard_map/ppermute | solution.py:16
  91.7 0.2 fusion.13
  92.5 15.9 %collective-permute-done.5 = bf16[2,192,512]{2,1,0:T(8,128)(2,1)S(1)} collective-permute-done((bf16[2,192,512]{2,1,0:T(8,128)(2,1)S(1)}, bf16[2,192,512]{2,1,0:T(8,128)(2,1)S(1)}, u32[]{:S(2)}, u32[]{:S(2)}) %collective-permute-start.5) | collective-permute-done | bytes 393248 | tf_op jit(solution)/shard_map/ppermute | solution.py:16
  108.4 0.2 fusion.58
  108.7 0.2 fusion.56
  108.9 0.2 fusion.15
  109.9 7.0 %scatter_fusion = f32[2,192,256]{1,0,2:T(2,128)S(1)} fusion(f32[2,192,256]{1,0,2:T(2,128)S(1)} %broadcast_in_dim.18, s32[256]{0:T(256)S(1)} %get-tuple-element.11, f32[256,2,192]{2,1,0:T(2,128)S(1)} %copy.47), kind=kCustom, calls=%fused_computation.1 | custom fusion | bytes 1180672 | tf_op jit(solution)/shard_map/scatter | solution.py:74
  117.2 0.6 negate_multiply_fusion
  (56 shorter events, 4.9 us)
Async XLA Ops:
  0.6 4.8 %copy-start = (bf16[3,2,256,512]{3,2,1,0:T(8,128)(2,1)S(1)}, bf16[3,2,256,512]{3,2,1,0:T(8,128)(2,1)}, u32[]{:S(2)}) copy-start(bf16[3,2,256,512]{3,2,1,0:T(8,128)(2,1)} %param.9) | copy-start | bytes 4718596
  7.3 14.9 %collective-permute-start.2 = (f32[2,192,512]{2,1,0:T(8,128)}, f32[2,192,512]{2,1,0:T(8,128)}, u32[]{:S(2)}, u32[]{:S(2)}) collective-permute-start(f32[2,192,512]{2,1,0:T(8,128)} %pad_maximum_fusion.1), channel_id=1, source_target_pairs={{0,1},{1,0},{2,3},{3,2},{4,5},{5,4},{6,7},{7,6},{8,9},{9,8},{10,11... | collective-permute-start | bytes 2359304 | tf_op jit(solution)/shard_map/ppermute | solution.py:16
  9.5 21.7 %collective-permute-start.6 = (f32[2,192,512]{2,1,0:T(8,128)}, f32[2,192,512]{2,1,0:T(8,128)}, u32[]{:S(2)}, u32[]{:S(2)}) collective-permute-start(f32[2,192,512]{2,1,0:T(8,128)} %pad_maximum_fusion.2), channel_id=1, source_target_pairs={{0,1},{1,0},{2,3},{3,2},{4,5},{5,4},{6,7},{7,6},{8,9},{9,8},{10,11... | collective-permute-start | bytes 2359304 | tf_op jit(solution)/shard_map/ppermute | solution.py:16
  10.2 0.7 copy-start.3
  10.9 1.0 copy-start.5
  10.9 1.6 %copy-start.2 = (bf16[2,2,8,128,128]{4,3,2,1,0:T(8,128)(2,1)S(1)}, bf16[2,2,8,128,128]{4,3,2,1,0:T(8,128)(2,1)}, u32[]{:S(2)}) copy-start(bf16[2,2,8,128,128]{4,3,2,1,0:T(8,128)(2,1)} %param.11) | copy-start | bytes 3145732
  12.0 17.2 %collective-permute-start.9 = (f32[2,192,512]{2,1,0:T(8,128)}, f32[2,192,512]{2,1,0:T(8,128)}, u32[]{:S(2)}, u32[]{:S(2)}) collective-permute-start(f32[2,192,512]{2,1,0:T(8,128)} %pad_maximum_fusion.3), channel_id=1, source_target_pairs={{0,1},{1,0},{2,3},{3,2},{4,5},{5,4},{6,7},{7,6},{8,9},{9,8},{10,11... | collective-permute-start | bytes 2359304 | tf_op jit(solution)/shard_map/ppermute | solution.py:16
  13.3 0.7 copy-start.10
  18.1 11.1 %copy-start.4 = (f32[1,192,512]{2,1,0:T(8,128)S(1)}, f32[1,192,512]{2,1,0:T(8,128)}, u32[]{:S(2)}) copy-start(f32[1,192,512]{2,1,0:T(8,128)} %copy-done.3) | copy-start | bytes 1179652
  18.2 11.0 %copy-start.6 = (f32[1,192,512]{2,1,0:T(8,128)S(1)}, f32[1,192,512]{2,1,0:T(8,128)}, u32[]{:S(2)}) copy-start(f32[1,192,512]{2,1,0:T(8,128)} %copy-done.5) | copy-start | bytes 1179652
  18.2 17.2 %collective-permute-start.1 = (f32[2,192,2,128]{3,2,1,0:T(2,128)S(1)}, f32[2,192,2,128]{3,2,1,0:T(2,128)S(1)}, u32[]{:S(2)}, u32[]{:S(2)}) collective-permute-start(f32[2,192,2,128]{3,2,1,0:T(2,128)S(1)} %get-tuple-element.13), channel_id=1, source_target_pairs={{0,1},{1,2},{2,3},{3,4},{4,5},{5,6},{6,7},{7,8},{8,9},{9,10},{10,1... | collective-permute-start | bytes 1179656 | tf_op jit(solution)/shard_map/ppermute | solution.py:12
  20.7 14.7 %collective-permute-start = (f32[2,192,2,128]{3,2,1,0:T(2,128)S(1)}, f32[2,192,2,128]{3,2,1,0:T(2,128)S(1)}, u32[]{:S(2)}, u32[]{:S(2)}) collective-permute-start(f32[2,192,2,128]{3,2,1,0:T(2,128)S(1)} %get-tuple-element.12), channel_id=1, source_target_pairs={{1,0},{2,1},{3,2},{4,3},{5,4},{6,5},{7,6},{8,7},{9,8},{10,9},{11,1... | collective-permute-start | bytes 1179656 | tf_op jit(solution)/shard_map/ppermute | solution.py:12
  24.3 36.9 %collective-permute-start.3 = (f32[2,192,512]{2,1,0:T(8,128)}, f32[2,192,512]{2,1,0:T(8,128)}, u32[]{:S(2)}, u32[]{:S(2)}) collective-permute-start(f32[2,192,512]{2,1,0:T(8,128)} %fusion.112), channel_id=1, source_target_pairs={{0,2},{1,3},{2,0},{3,1},{4,6},{5,7},{6,4},{7,5},{8,10},{9,11},{10,... | collective-permute-start | bytes 2359304 | tf_op jit(solution)/shard_map/ppermute | solution.py:16
  31.2 28.8 %collective-permute-start.10 = (bf16[2,192,512]{2,1,0:T(8,128)(2,1)}, bf16[2,192,512]{2,1,0:T(8,128)(2,1)}, u32[]{:S(2)}, u32[]{:S(2)}) collective-permute-start(bf16[2,192,512]{2,1,0:T(8,128)(2,1)} %add_convert_fusion), channel_id=1, source_target_pairs={{0,2},{1,3},{2,0},{3,1},{4,6},{5,7},{6,4},{7,5},{8,10},{9,11},{10,... | collective-permute-start | bytes 1179656 | tf_op jit(solution)/shard_map/ppermute | solution.py:16
  33.4 26.7 %copy-start.1 = (bf16[3,2,256,512]{3,2,1,0:T(8,128)(2,1)S(1)}, bf16[3,2,256,512]{3,2,1,0:T(8,128)(2,1)}, u32[]{:S(2)}) copy-start(bf16[3,2,256,512]{3,2,1,0:T(8,128)(2,1)} %param.10) | copy-start | bytes 4718596
  33.4 41.4 %collective-permute-start.7 = (f32[2,192,512]{2,1,0:T(8,128)}, f32[2,192,512]{2,1,0:T(8,128)}, u32[]{:S(2)}, u32[]{:S(2)}) collective-permute-start(f32[2,192,512]{2,1,0:T(8,128)} %fusion.111), channel_id=1, source_target_pairs={{0,2},{1,3},{2,0},{3,1},{4,6},{5,7},{6,4},{7,5},{8,10},{9,11},{10,... | collective-permute-start | bytes 2359304 | tf_op jit(solution)/shard_map/ppermute | solution.py:16
  62.9 26.0 %collective-permute-start.4 = (f32[2,192,512]{2,1,0:T(8,128)S(1)}, f32[2,192,512]{2,1,0:T(8,128)S(1)}, u32[]{:S(2)}, u32[]{:S(2)}) collective-permute-start(f32[2,192,512]{2,1,0:T(8,128)S(1)} %fusion.115), channel_id=1, source_target_pairs={{0,4},{1,5},{2,6},{3,7},{4,0},{5,1},{6,2},{7,3},{8,12},{9,13},{10,... | collective-permute-start | bytes 2359304 | tf_op jit(solution)/shard_map/ppermute | solution.py:16
  76.4 12.3 %collective-permute-start.8 = (bf16[2,192,512]{2,1,0:T(8,128)(2,1)S(1)}, bf16[2,192,512]{2,1,0:T(8,128)(2,1)S(1)}, u32[]{:S(2)}, u32[]{:S(2)}) collective-permute-start(bf16[2,192,512]{2,1,0:T(8,128)(2,1)S(1)} %add_convert_fusion.1), channel_id=1, source_target_pairs={{0,4},{1,5},{2,6},{3,7},{4,0},{5,1},{6,2},{7,3},{8,12},{9,13},{10,... | collective-permute-start | bytes 1179656 | tf_op jit(solution)/shard_map/ppermute | solution.py:16
  89.1 19.3 %collective-permute-start.5 = (bf16[2,192,512]{2,1,0:T(8,128)(2,1)S(1)}, bf16[2,192,512]{2,1,0:T(8,128)(2,1)S(1)}, u32[]{:S(2)}, u32[]{:S(2)}) collective-permute-start(bf16[2,192,512]{2,1,0:T(8,128)(2,1)S(1)} %add_convert_fusion.2), channel_id=1, source_target_pairs={{0,8},{1,9},{2,10},{3,11},{4,12},{5,13},{6,14},{7,15},{8,0},{9,1},... | collective-permute-start | bytes 1179656 | tf_op jit(solution)/shard_map/ppermute | solution.py:16
  92.5 16.9 %copy-start.8 = (f32[2,192,256]{2,1,0:T(8,128)S(1)}, f32[2,192,256]{2,1,0:T(8,128)}, u32[]{:S(2)}) copy-start(f32[2,192,256]{2,1,0:T(8,128)} %reshape.42) | copy-start | bytes 1179652
  109.5 7.6 %copy-start.9 = (bf16[2,192,256]{2,1,0:T(8,128)(2,1)S(1)}, bf16[2,192,256]{2,1,0:T(8,128)(2,1)}, u32[]{:S(2)}) copy-start(bf16[2,192,256]{2,1,0:T(8,128)(2,1)} %param.8) | copy-start | bytes 589828
  117.1 0.7 copy-start.7
where the time goes:
time: 118 us
  waiting for transfers between devices  52.4 us (44%)
  starting transfers between devices  21.9 us (19%)
  other arithmetic  15.7 us (13%)
  matrix products  13.6 us (12%)
  local copies, waits for them, and re-layouts  13.2 us (11%)
    ppermute x9, waiting for transfers between devices, swapped(): lax.ppermute(x, axis, [(i, i ^ 1 << distance) for i in range(lax.axis_siz...  52.4 us
    ppermute x9, starting transfers between devices, swapped(): lax.ppermute(x, axis, [(i, i ^ 1 << distance) for i in range(lax.axis_siz...  17.9 us
    scatter x1, local copies, waits for them, and re-layouts, body(): jnp.zeros((2, columns, panel_count), jnp.float32).at[:, :, local_order]  6.97 us
    add x3, other arithmetic, body(): running = running + swapped(running, ('leaf', 'rhs'), bit_number)  5.96 us
    ppermute x2, starting transfers between devices, from_behind(): return lax.ppermute(x, axis, pairs)  3.96 us
    convert_element_type x3, other arithmetic, body(): level_sums.append(running.astype(jnp.bfloat16))  3.76 us
    another operation x4, other arithmetic, conj_product(): return jnp.stack([real_part, imag_part])  3.14 us
    dot_general x1, matrix products, body(): jnp.einsum('zrikc,ikj->zrjc', terms, one_hot, precision=lax.Precision.HIG...  3.14 us
  transfers between devices with their start and end apart: 11, of which 4 were waited for; matrix products, arithmetic and copies ran while one was open for 22% of the time, Pallas kernels for 0%

commit v1 on v0

v1 whole, which is shorter than its diff:
```python
import math

import jax
import jax.numpy as jnp
from jax import lax
from jax.experimental import pallas as pl
from jax.experimental.pallas import tpu as pltpu
from jax.sharding import PartitionSpec as P

TREE = ("leaf", "rhs")
F32 = jnp.float32
BF16 = jnp.bfloat16
VMEM_BYTES = 24 * 1024 * 1024


def dot(a, b):
    return lax.dot_general(a, b, (((1,), (0,)), ((), ())), preferred_element_type=F32)


def dot_t(a, b):
    return lax.dot_general(a, b, (((1,), (1,)), ((), ())), preferred_element_type=F32)


def call(kernel, out_shape, scratch_shapes=(), smem=(), inputs=0):
    in_specs = [
        pl.BlockSpec(memory_space=pltpu.SMEM if i in smem else pltpu.VMEM) for i in range(inputs)
    ]
    out_specs = jax.tree.map(lambda _: pl.BlockSpec(memory_space=pltpu.VMEM), out_shape)
    return pl.pallas_call(
        kernel,
        out_shape=out_shape,
        in_specs=in_specs,
        out_specs=out_specs,
        scratch_shapes=list(scratch_shapes),
        compiler_params=pltpu.CompilerParams(vmem_limit_bytes=VMEM_BYTES),
    )


def array(shape, dtype):
    return jax.ShapeDtypeStruct(shape, dtype)


def swapped(x, distance):
    return lax.ppermute(x, TREE, [(i, i ^ distance) for i in range(lax.axis_size(TREE))])


def by_core(x, distance_0, distance_1):
    pairs = []
    for i in range(lax.axis_size(TREE)):
        distance = distance_1 if i & 1 else distance_0
        if distance is not None:
            pairs.append((i, i ^ distance))
    return lax.ppermute(x, TREE, pairs)


def one_hot_of(order_ref, panels):
    local = lax.rem(order_ref[...], panels)
    rows = lax.broadcasted_iota(jnp.int32, (panels, panels), 0)
    return (rows == local).astype(F32).astype(BF16)


def signed_stack(x):
    half = x.shape[0] // 2
    real, imag = x[:half], x[half:]
    return jnp.concatenate(
        [jnp.concatenate([real, imag], axis=1), jnp.concatenate([imag, -real], axis=1)], axis=0
    )


def position():
    place = lax.axis_index(TREE)
    return place & 1, (place >> 1) & 1, (place >> 2) & 1


def first_kernel(order_ref, src_ref, basis_ref, tree_ref, send_ref, keep_ref):
    core, _, low = position()
    two, rows, panels = src_ref.shape
    rank = basis_ref.shape[3]
    half = rank // 2
    source = src_ref[...].reshape(two * rows, panels)
    tree = dot(source, one_hot_of(order_ref, panels)).astype(BF16)
    tree_ref[...] = tree
    stack = signed_stack(tree)
    mine = pl.multiple_of((low ^ core) * half, half)
    theirs = pl.multiple_of((low ^ core ^ 1) * half, half)
    for start, out in ((theirs, send_ref), (mine, keep_ref)):
        basis = basis_ref[0, :, :, pl.ds(start, half)].reshape(2 * panels, half)
        out[...] = dot(stack, basis)


def second_kernel(tree_ref, basis_ref, send_ref, keep_ref):
    core, _, _ = position()
    levels, _, panels, rank = basis_ref.shape
    half = rank // 2
    stack = signed_stack(tree_ref[...])
    mine = pl.multiple_of(core * half, half)
    theirs = pl.multiple_of((core ^ 1) * half, half)
    for start, out in ((theirs, send_ref), (mine, keep_ref)):
        for level in range(1, levels):
            basis = basis_ref[level, :, :, pl.ds(start, half)].reshape(2 * panels, half)
            out[level - 1] = dot(stack, basis)


def near_kernel(index_ref, tree_ref, near_ref, core_ref, far_ref, own_ref, sums):
    core, _, _ = position()
    _, block_count, neighbours, size, _ = near_ref.shape
    sums[...] = jnp.zeros_like(sums)
    base = index_ref[0, 0] - block_count
    for i in range(block_count):
        stack = signed_stack(tree_ref[:, i * size : (i + 1) * size])
        for k in range(neighbours):
            block = near_ref[:, i, k].reshape(2 * size, size)
            target = jnp.clip(index_ref[i, k] - base, 0, 3 * block_count - 1)
            sums[target] += dot(stack, block)
    for j in range(block_count):
        lanes = pl.ds(j * size, size)
        own_ref[:, lanes] = sums[block_count + j]
        far_ref[:, lanes] = sums[core * 2 * block_count + j].astype(BF16)
        core_ref[:, lanes] = sums[(1 - core) * 2 * block_count + j]


def spread_kernel(keep_ref, got_ref, out_ref, other_ref):
    core, across, _ = position()
    width = out_ref.shape[1]
    out_lanes = pl.ds(pl.multiple_of((across ^ 1 ^ core) * width, width), width)
    other_lanes = pl.ds(pl.multiple_of((across ^ core) * width, width), width)
    out_ref[...] = keep_ref[:, out_lanes] + got_ref[:, out_lanes]
    other_ref[...] = keep_ref[:, other_lanes] + got_ref[:, other_lanes]


def expanded(coefficient, basis_ref, level, start, width):
    half = coefficient.shape[0] // 2
    turned = jnp.concatenate([-coefficient[half:], coefficient[:half]], axis=0)
    lanes = pl.ds(start, width)
    return dot_t(coefficient, basis_ref[level, 0, :, lanes]) + dot_t(
        turned, basis_ref[level, 1, :, lanes]
    )


def middle_kernel(own_ref, core_ref, far_ref, two_ref, two_got_ref, three_ref, three_got_ref, basis_ref, out_ref):
    core, _, _ = position()
    half = two_ref.shape[1]
    total = own_ref[...] + core_ref[...] + far_ref[...].astype(F32)
    for level, mine_ref, got_ref in ((1, two_ref, two_got_ref), (2, three_ref, three_got_ref)):
        total += expanded(mine_ref[...], basis_ref, level, pl.multiple_of(core * half, half), half)
        total += expanded(got_ref[...], basis_ref, level, pl.multiple_of((1 - core) * half, half), half)
    out_ref[...] = total


def last_kernel(
    order_ref, base_ref, f_ref, g_ref, f_got_ref, g_got_ref, basis_ref, forward_ref, field_ref, grad_ref, full
):
    core, across, low = position()
    width = f_ref.shape[1]
    mine = low ^ core
    for half, first, second in ((mine, f_ref, g_ref), (mine ^ 1, f_got_ref, g_got_ref)):
        full[:, pl.ds(pl.multiple_of((2 * half + across) * width, width), width)] = first[...]
        full[:, pl.ds(pl.multiple_of((2 * half + (across ^ 1)) * width, width), width)] = second[...]
    total = base_ref[...] + expanded(full[...], basis_ref, 0, 0, 4 * width)
    two, rows, panels = field_ref.shape
    one_hot = one_hot_of(order_ref, panels)
    field = jnp.zeros_like(total)
    for _ in range(3):
        piece = total.astype(BF16)
        total = total - piece.astype(F32)
        field += dot_t(piece, one_hot)
    field_ref[...] = field.reshape(two, rows, panels)
    forward = forward_ref[...].reshape(two * rows, panels).astype(F32)
    grad_ref[...] = -jnp.sum(field * forward, axis=0, keepdims=True) / math.sqrt(rows)


def fast_body(sources, forward_field, row_bases, col_bases, near_blocks, near_index, cluster_order):
    two, rows, panels = sources.shape
    rank = row_bases.shape[3]
    both = two * rows
    half, quarter = rank // 2, rank // 4
    order = cluster_order.reshape(1, panels)
    core = lax.axis_index(TREE) & 1

    tree, send_1, keep_1 = call(
        first_kernel,
        (array((both, panels), BF16), array((both, half), F32), array((both, half), F32)),
        inputs=3,
    )(order, sources, row_bases)
    got_1 = swapped(send_1, 1)
    send_23, keep_23 = call(
        second_kernel, (array((2, both, half), F32), array((2, both, half), F32)), inputs=2
    )(tree, row_bases)
    got_23 = swapped(send_23, 1)

    to_a, other = call(
        spread_kernel, (array((both, quarter), F32), array((both, quarter), F32)), inputs=2
    )(keep_1, got_1)
    got_a = by_core(to_a, 2, 4)
    got_b = by_core(other, None, 6)

    sum_23 = keep_23 + got_23
    mine_3 = swapped(sum_23[1].astype(BF16), 2)
    two_sent = sum_23[0].astype(BF16)
    got_c = swapped(two_sent, 4)
    got_d = swapped(two_sent, 6)

    blocks = near_blocks.shape[1]
    size = near_blocks.shape[3]
    to_core, to_far, own = call(
        near_kernel,
        (array((both, panels), F32), array((both, panels), BF16), array((both, panels), F32)),
        scratch_shapes=[pltpu.VMEM((3 * blocks, both, size), F32)],
        smem=(0,),
        inputs=3,
    )(near_index, tree, near_blocks)
    core_halo = swapped(to_core, 1)
    peers = lax.axis_size(TREE)
    joints = [(i, i + 1) for i in range(1, peers - 1, 2)]
    far_halo = lax.ppermute(to_far, TREE, joints + [(b, a) for a, b in joints])

    middle = got_a + jnp.where(core == 0, other, got_b)
    quarter_sum = (middle + swapped(middle, 1)).astype(BF16)
    got_f = by_core(quarter_sum, 8, 12)
    got_g = by_core(quarter_sum, 10, 14)

    mine_2 = (got_c.astype(F32) + got_d.astype(F32)).astype(BF16)
    other_3 = swapped(mine_3, 1)
    other_2 = swapped(mine_2, 1)
    base = call(middle_kernel, array((both, panels), F32), inputs=8)(
        own, core_halo, far_halo, mine_2, other_2, mine_3, other_3, col_bases
    )
    core_f = swapped(got_f, 1)
    core_g = swapped(got_g, 1)
    field, grad = call(
        last_kernel,
        (array((two, rows, panels), F32), array((1, panels), F32)),
        scratch_shapes=[pltpu.VMEM((both, rank), BF16)],
        inputs=8,
    )(order, base, got_f, got_g, core_f, core_g, col_bases, forward_field)
    return field, grad.reshape(panels)


def conj_product(first_operand, second_operand, pattern):
    real_part = jnp.einsum(
        pattern, first_operand[0], second_operand[0], preferred_element_type=jnp.float32
    ) + jnp.einsum(pattern, first_operand[1], second_operand[1], preferred_element_type=jnp.float32)
    imag_part = jnp.einsum(
        pattern, first_operand[1], second_operand[0], preferred_element_type=jnp.float32
    ) - jnp.einsum(pattern, first_operand[0], second_operand[1], preferred_element_type=jnp.float32)
    return jnp.stack([real_part, imag_part])


def expand_basis(coefficient, col_basis):
    real_part = jnp.einsum(
        "rk,nk->rn", coefficient[0], col_basis[0], preferred_element_type=jnp.float32
    ) - jnp.einsum("rk,nk->rn", coefficient[1], col_basis[1], preferred_element_type=jnp.float32)
    imag_part = jnp.einsum(
        "rk,nk->rn", coefficient[0], col_basis[1], preferred_element_type=jnp.float32
    ) + jnp.einsum("rk,nk->rn", coefficient[1], col_basis[0], preferred_element_type=jnp.float32)
    return jnp.stack([real_part, imag_part])


def from_behind(x, by):
    peers = lax.axis_size(TREE)
    return lax.ppermute(x, TREE, [(i, i + by) for i in range(peers) if 0 <= i + by < peers])


def general_body(sources, forward_field, row_bases, col_bases, near_blocks, near_index, cluster_order):
    panel_count = sources.shape[2]
    columns = sources.shape[1]
    device = lax.axis_index(TREE)
    tree_bits = lax.axis_size(TREE).bit_length() - 1
    level_total = row_bases.shape[0]
    local_order = cluster_order - device * panel_count
    tree_sources = jnp.take(sources, local_order, axis=2)
    partials = [
        conj_product(tree_sources, row_bases[level_number], "rn,nk->rk")
        for level_number in range(level_total)
    ]
    block_count = near_blocks.shape[1]
    block_size = near_blocks.shape[3]
    targets = near_index - device * block_count + block_count
    one_hot = (
        targets[:, :, None] == jnp.arange(3 * block_count, dtype=jnp.int32)[None, None, :]
    ).astype(jnp.float32)
    block_sources = tree_sources.reshape(2, columns, block_count, block_size)
    terms = conj_product(block_sources, near_blocks, "rib,ikbc->rikc")
    buffer = jnp.einsum("zrikc,ikj->zrjc", terms, one_hot, precision=lax.Precision.HIGHEST)
    from_right = from_behind(buffer[:, :, :block_count], -1)
    from_left = from_behind(buffer[:, :, 2 * block_count :], 1)
    near_field = buffer[:, :, block_count : 2 * block_count] + from_right + from_left
    adjoint_tree = near_field.reshape(2, columns, panel_count)
    level_sums = []
    for level_number in range(level_total):
        running = partials[level_number]
        for bit_number in range(tree_bits - level_number - 1):
            running = running + swapped(running, 1 << bit_number)
        level_sums.append(running.astype(jnp.bfloat16))
    for level_number in range(level_total):
        sibling = swapped(level_sums[level_number], 1 << (tree_bits - level_number - 1))
        adjoint_tree = adjoint_tree + expand_basis(sibling, col_bases[level_number])
    adjoint_field = (
        jnp.zeros((2, columns, panel_count), jnp.float32).at[:, :, local_order].set(adjoint_tree)
    )
    forward_float = forward_field.astype(jnp.float32)
    gradient = -jnp.sum(adjoint_field * forward_float, axis=(0, 1)) / math.sqrt(columns)
    return (adjoint_field, gradient)


def body(*arrays):
    row_bases = arrays[2]
    fits = lax.axis_size("rhs") == 2 and lax.axis_size("leaf") == 8 and row_bases.shape[0] == 3
    return (fast_body if fits else general_body)(*arrays)


def solution(mesh):
    split = ("groups", "leaf", "rhs")
    in_specs = (
        P(None, None, split),
        P(None, None, split),
        P(None, None, split, None),
        P(None, None, split, None),
        P(None, split, None, None, None),
        P(split, None),
        P(split),
    )
    out_specs = (P(None, None, split), P(split))
    return jax.shard_map(body, mesh=mesh, in_specs=in_specs, out_specs=out_specs, check_vma=False)
```

time: 118 us -> 52.2 us (0.44)
  waiting for transfers between devices: 52.4 us -> 18.1 us
  other arithmetic: 15.7 us -> 1.31 us
  matrix products: 13.6 us -> 0 us
  local copies, waits for them, and re-layouts: 13.2 us -> 3.22 us
  Pallas kernels: 0 us -> 6.59 us
    ppermute x11 -> x16, waiting for transfers between devices: 52.4 us -> 18.1 us  [the longest x4 12.6 us: by_core(): return lax.ppermute(x, TREE, pairs)]
    dot_general x29 -> x0, matrix products: 13.6 us -> none  [the longest x1 3.14 us: body(): jnp.einsum('zrikc,ikj->zrjc', terms, one_hot, precision=lax.Precision.HIG...]
    scatter x1 -> x0, local copies, waits for them, and re-layouts: 6.97 us -> none  [body(): jnp.zeros((2, columns, panel_count), jnp.float32).at[:, :, local_order]]
    pallas_call x0 -> x6, Pallas kernels: none -> 6.59 us  [the longest x1 2.43 us: fast_body(): call(near_kernel, (array((both, panels), F32), array((both, panels), BF16...]
    add x6 -> x1, other arithmetic: 6.44 us -> 0.03 us  [fast_body(): middle = got_a + jnp.where(core == 0, other, got_b)]
    convert_element_type x3 -> x2, other arithmetic: 3.76 us -> 0.07 us  [the longest x1 0.05 us: fast_body(): mine_2 = (got_c.astype(F32) + got_d.astype(F32)).astype(BF16)]
    another operation x4 -> x1, other arithmetic: 3.14 us -> 1.21 us  [conj_product(): return jnp.stack([real_part, imag_part])]
    gather x1 -> x0, local copies, waits for them, and re-layouts: 1.23 us -> none  [body(): tree_sources = jnp.take(sources, local_order, axis=2)]
  transfers between devices with their start and end apart: 11 -> 16, of which waited for: 4 -> 6; matrix products, arithmetic and copies ran while one was open for 22% -> 3% of each run, Pallas kernels for 0% -> 6%
where the time goes in v1:
time: 52.2 us; the launch traced here: 51.9 us
  starting transfers between devices  21.9 us (42%)
  waiting for transfers between devices  18.1 us (35%)
  Pallas kernels  6.59 us (13%)
  local copies, waits for them, and re-layouts  3.22 us (6%)
  other arithmetic  1.31 us (3%)
  between operations  0.79 us (2%)
    ppermute x4, waiting for transfers between devices, by_core(): return lax.ppermute(x, TREE, pairs)  12.6 us
    ppermute x11, starting transfers between devices, swapped(): lax.ppermute(x, TREE, [(i, i ^ distance) for i in range(lax.axis_size(TRE...  12.6 us
    ppermute x4, starting transfers between devices, by_core(): return lax.ppermute(x, TREE, pairs)  8.67 us
    ppermute x11, waiting for transfers between devices, swapped(): lax.ppermute(x, TREE, [(i, i ^ distance) for i in range(lax.axis_size(TRE...  5.47 us
    unnamed x18, local copies, waits for them, and re-layouts  3.2 us
    pallas_call x1, Pallas kernels, fast_body(): call(near_kernel, (array((both, panels), F32), array((both, panels), BF16...  2.43 us
    pallas_call x1, Pallas kernels, fast_body(): call(last_kernel, (array((two, rows, panels), F32), array((1, panels), F3...  1.66 us
    pallas_call x1, Pallas kernels, fast_body(): call(first_kernel, (array((both, panels), BF16), array((both, half), F32)...  1.24 us
  transfers between devices with their start and end apart: 16, of which 6 were waited for; matrix products, arithmetic and copies ran while one was open for 3% of the time, Pallas kernels for 6%

profile of v1, /device:TPU:0, one launch (start us, length us, event | category | flops | bytes accessed | tf_op | source)
XLA Modules:
  0.0 51.9 jit_solution(9908023702120349753)
XLA Ops:
  0.6 0.0 copy-start
  0.6 1.4 %copy-done = bf16[3,2,256,512]{3,2,1,0:T(8,128)(2,1)S(1)} copy-done((bf16[3,2,256,512]{3,2,1,0:T(8,128)(2,1)S(1)}, bf16[3,2,256,512]{3,2,1,0:T(8,128)(2,1)}, u32[]{:S(2)}) %copy-start) | copy-done | bytes 1572888
  2.0 0.9 %copy-done.4 = bf16[2,192,256]{2,1,0:T(8,128)(2,1)S(1)} copy-done((bf16[2,192,256]{2,1,0:T(8,128)(2,1)S(1)}, bf16[2,192,256]{2,1,0:T(8,128)(2,1)}, u32[]{:S(2)}) %copy-start.4) | copy-done | bytes 196632
  3.0 0.7 %copy-done.6 = s32[256]{0:T(256)S(1)} copy-done((s32[256]{0:T(256)S(1)}, s32[256]{0:T(256)}, u32[]{:S(2)}) %copy-start.6) | copy-done | bytes 1048
  3.7 1.2 %shard_map.86 = (bf16[384,256]{1,0:T(8,128)(2,1)S(1)}, f32[384,256]{1,0:T(8,128)}, f32[384,256]{1,0:T(8,128)S(1)}) custom-call(s32[1,256]{1,0:T(1,128)S(1)} %bitcast.6, bf16[2,192,256]{2,1,0:T(8,128)(2,1)S(1)} %copy-done.4, bf16[3,2,256,512]{3,2,1,0:T(8,128)(2,1)S(1)} %copy-done), custom_call_target="tpu_custom_call" | custom-call | tf_op jit(solution)/shard_map/pallas_call | solution.py:180
  4.9 0.2 copy-done.1
  5.1 0.6 %shard_map.88 = (f32[2,384,256]{2,1,0:T(8,128)S(1)}, f32[2,384,256]{2,1,0:T(8,128)S(1)}) custom-call(bf16[384,256]{1,0:T(8,128)(2,1)S(1)} %get-tuple-element.14.tree_ref, bf16[3,2,256,512]{3,2,1,0:T(8,128)(2,1)S(1)} %copy-done.1), custom_call_target="tpu_custom_call" | custom-call | tf_op jit(solution)/shard_map/pallas_call | solution.py:186
  5.6 0.5 %collective-permute-start.2 = (f32[2,384,256]{2,1,0:T(8,128)S(1)}, f32[2,384,256]{2,1,0:T(8,128)}, u32[]{:S(2)}, u32[]{:S(2)}) collective-permute-start(f32[2,384,256]{2,1,0:T(8,128)S(1)} %get-tuple-element.19), channel_id=1, source_target_pairs={{0,1},{1,0},{2,3},{3,2},{4,5},{5,4},{6,7},{7,6},{8,9},{9,8},{10,11... | collective-permute-start | bytes 2359304 | tf_op jit(solution)/shard_map/ppermute | solution.py:44
  6.2 0.1 collective-permute-start.8
  6.2 0.0 copy-done.8
  6.2 2.4 %shard_map.87 = (f32[384,256]{1,0:T(8,128)}, bf16[384,256]{1,0:T(8,128)(2,1)S(1)}, f32[384,256]{1,0:T(8,128)S(1)}) custom-call(s32[2,8]{1,0:T(2,128)S(1)} %copy-done.8, bf16[384,256]{1,0:T(8,128)(2,1)S(1)} %get-tuple-element.14.tree_ref, bf16[2,2,8,128,128]{4,3,2,1,0:T(8,128)(2,1)S(1)} %copy-done.3), custom_call_target="tpu_custom_call" | custom-call | tf_op jit(solution)/shard_map/pallas_call | solution.py:205
  8.7 0.4 collective-permute-start
  9.1 0.7 %collective-permute-start.1 = (bf16[384,256]{1,0:T(8,128)(2,1)S(1)}, bf16[384,256]{1,0:T(8,128)(2,1)S(1)}, u32[]{:S(2)}, u32[]{:S(2)}) collective-permute-start(bf16[384,256]{1,0:T(8,128)(2,1)S(1)} %get-tuple-element.17), channel_id=1, source_target_pairs={{1,2},{3,4},{5,6},{7,8},{9,10},{11,12},{13,14},{2,1},{4,3},{6,5},{... | collective-permute-start | bytes 589832 | tf_op jit(solution)/shard_map/ppermute | solution.py:215
  9.8 0.0 collective-permute-done.8.got_ref
  9.8 0.1 shard_map.90
  9.9 0.7 %collective-permute-start.10 = (f32[384,128]{1,0:T(8,128)S(1)}, f32[384,128]{1,0:T(8,128)S(1)}, u32[]{:S(2)}, u32[]{:S(2)}) collective-permute-start(f32[384,128]{1,0:T(8,128)S(1)} %get-tuple-element.23), channel_id=1, source_target_pairs={{1,7},{3,5},{5,3},{7,1},{9,15},{11,13},{13,11},{15,9},{17,23},{19,... | collective-permute-start | bytes 589832 | tf_op jit(solution)/shard_map/ppermute | solution.py:53
  10.5 3.9 %collective-permute-start.9 = (f32[384,128]{1,0:T(8,128)S(1)}, f32[384,128]{1,0:T(8,128)S(1)}, u32[]{:S(2)}, u32[]{:S(2)}) collective-permute-start(f32[384,128]{1,0:T(8,128)S(1)} %get-tuple-element.22), channel_id=1, source_target_pairs={{0,2},{1,5},{2,0},{3,7},{4,6},{5,1},{6,4},{7,3},{8,10},{9,13},{10,... | collective-permute-start | bytes 589832 | tf_op jit(solution)/shard_map/ppermute | solution.py:53
  14.4 0.0 collective-permute-done.2
  14.4 1.2 %add_convert_fusion = bf16[2,384,256]{2,1,0:T(8,128)(2,1)S(1)} fusion(f32[2,384,256]{2,1,0:T(8,128)S(1)} %get-tuple-element.18, f32[2,384,256]{2,1,0:T(8,128)} %collective-permute-done.2), kind=kLoop, calls=%fused_computation | loop fusion | flops 393216 | bytes 1966080 | tf_op jit(solution)/shard_map/convert.1
  15.6 0.0 copy-start.2
  15.7 2.2 %collective-permute-start.3 = (bf16[384,256]{1,0:T(8,128)(2,1)S(1)}, bf16[384,256]{1,0:T(8,128)(2,1)S(1)}, u32[]{:S(2)}, u32[]{:S(2)}) collective-permute-start(bf16[384,256]{1,0:T(8,128)(2,1)S(1)} %get-tuple-element.27), channel_id=1, source_target_pairs={{0,4},{1,5},{2,6},{3,7},{4,0},{5,1},{6,2},{7,3},{8,12},{9,13},{10,... | collective-permute-start | bytes 589832 | tf_op jit(solution)/shard_map/ppermute | solution.py:44
  17.9 0.0 collective-permute-done.10
  17.9 0.9 %collective-permute-start.4 = (bf16[384,256]{1,0:T(8,128)(2,1)S(1)}, bf16[384,256]{1,0:T(8,128)(2,1)S(1)}, u32[]{:S(2)}, u32[]{:S(2)}) collective-permute-start(bf16[384,256]{1,0:T(8,128)(2,1)S(1)} %get-tuple-element.27), channel_id=1, source_target_pairs={{0,6},{1,7},{2,4},{3,5},{4,2},{5,3},{6,0},{7,1},{8,14},{9,15},{10,... | collective-permute-start | bytes 589832 | tf_op jit(solution)/shard_map/ppermute | solution.py:44
  18.8 3.7 %collective-permute-done.9 = f32[384,128]{1,0:T(8,128)S(1)} collective-permute-done((f32[384,128]{1,0:T(8,128)S(1)}, f32[384,128]{1,0:T(8,128)S(1)}, u32[]{:S(2)}, u32[]{:S(2)}) %collective-permute-start.9) | collective-permute-done | bytes 196640 | tf_op jit(solution)/shard_map/ppermute | solution.py:53
  22.5 5.2 %collective-permute-start.11 = (f32[384,128]{1,0:T(8,128)S(1)}, f32[384,128]{1,0:T(8,128)S(1)}, u32[]{:S(2)}, u32[]{:S(2)}) collective-permute-start(f32[384,128]{1,0:T(8,128)S(1)} %select_add_fusion), channel_id=1, source_target_pairs={{0,1},{1,0},{2,3},{3,2},{4,5},{5,4},{6,7},{7,6},{8,9},{9,8},{10,11... | collective-permute-start | bytes 589832 | tf_op jit(solution)/shard_map/ppermute | solution.py:44
  27.7 0.0 collective-permute-done.3
  27.7 0.0 collective-permute-start.6
  27.7 1.0 %collective-permute-done.4 = bf16[384,256]{1,0:T(8,128)(2,1)S(1)} collective-permute-done((bf16[384,256]{1,0:T(8,128)(2,1)S(1)}, bf16[384,256]{1,0:T(8,128)(2,1)S(1)}, u32[]{:S(2)}, u32[]{:S(2)}) %collective-permute-start.4) | collective-permute-done | bytes 196640 | tf_op jit(solution)/shard_map/ppermute | solution.py:44
  28.7 3.1 %collective-permute-start.5 = (bf16[384,256]{1,0:T(8,128)(2,1)S(1)}, bf16[384,256]{1,0:T(8,128)(2,1)S(1)}, u32[]{:S(2)}, u32[]{:S(2)}) collective-permute-start(bf16[384,256]{1,0:T(8,128)(2,1)S(1)} %add_convert_fusion.1.two_ref), channel_id=1, source_target_pairs={{0,1},{1,0},{2,3},{3,2},{4,5},{5,4},{6,7},{7,6},{8,9},{9,8},{10,11... | collective-permute-start | bytes 589832 | tf_op jit(solution)/shard_map/ppermute | solution.py:44
  31.8 3.9 %collective-permute-done.6.three_ref = bf16[384,256]{1,0:T(8,128)(2,1)S(1)} collective-permute-done((bf16[384,256]{1,0:T(8,128)(2,1)S(1)}, bf16[384,256]{1,0:T(8,128)(2,1)S(1)}, u32[]{:S(2)}, u32[]{:S(2)}) %collective-permute-start.6) | collective-permute-done | bytes 196640 | tf_op jit(solution)/shard_map/ppermute | solution.py:44
  35.7 0.2 collective-permute-start.7
  35.9 0.0 collective-permute-done.11
  35.9 2.6 %collective-permute-start.12 = (bf16[384,128]{1,0:T(8,128)(2,1)S(1)}, bf16[384,128]{1,0:T(8,128)(2,1)S(1)}, u32[]{:S(2)}, u32[]{:S(2)}) collective-permute-start(bf16[384,128]{1,0:T(8,128)(2,1)S(1)} %add_convert_fusion.2), channel_id=1, source_target_pairs={{0,8},{1,13},{2,10},{3,15},{4,12},{5,9},{6,14},{7,11},{8,0},{9,5},... | collective-permute-start | bytes 294920 | tf_op jit(solution)/shard_map/ppermute | solution.py:53
  38.6 0.0 collective-permute-done.1.far_ref
  38.6 1.5 %collective-permute-start.13 = (bf16[384,128]{1,0:T(8,128)(2,1)S(1)}, bf16[384,128]{1,0:T(8,128)(2,1)S(1)}, u32[]{:S(2)}, u32[]{:S(2)}) collective-permute-start(bf16[384,128]{1,0:T(8,128)(2,1)S(1)} %add_convert_fusion.2), channel_id=1, source_target_pairs={{0,10},{1,15},{2,8},{3,13},{4,14},{5,11},{6,12},{7,9},{8,2},{9,7},... | collective-permute-start | bytes 294920 | tf_op jit(solution)/shard_map/ppermute | solution.py:53
  40.0 6.6 %collective-permute-done.12.f_ref = bf16[384,128]{1,0:T(8,128)(2,1)S(1)} collective-permute-done((bf16[384,128]{1,0:T(8,128)(2,1)S(1)}, bf16[384,128]{1,0:T(8,128)(2,1)S(1)}, u32[]{:S(2)}, u32[]{:S(2)}) %collective-permute-start.12) | collective-permute-done | bytes 98336 | tf_op jit(solution)/shard_map/ppermute | solution.py:53
  46.7 0.0 collective-permute-start.14
  46.7 2.3 %collective-permute-done.13.g_ref = bf16[384,128]{1,0:T(8,128)(2,1)S(1)} collective-permute-done((bf16[384,128]{1,0:T(8,128)(2,1)S(1)}, bf16[384,128]{1,0:T(8,128)(2,1)S(1)}, u32[]{:S(2)}, u32[]{:S(2)}) %collective-permute-start.13) | collective-permute-done | bytes 98336 | tf_op jit(solution)/shard_map/ppermute | solution.py:53
  48.9 0.0 collective-permute-start.15
  49.0 0.0 collective-permute-done.core_ref
  49.0 0.0 collective-permute-done.5.two_got_ref
  49.0 0.0 collective-permute-done.7.three_got_ref
  49.0 0.0 copy-start.5
  49.0 0.0 copy-start.7
  49.0 0.6 %shard_map.89.base_ref = f32[384,256]{1,0:T(8,128)S(1)} custom-call(f32[384,256]{1,0:T(8,128)S(1)} %get-tuple-element.15.own_ref, f32[384,256]{1,0:T(8,128)S(1)} %collective-permute-done.core_ref, bf16[384,256]{1,0:T(8,128)(2,1)S(1)} %collective-permute-done.1.far_ref, bf16[384,256]{1,0:T(8,128)(2,1)S(1)} %add_convert_fusion.1.two_ref, ...), custom_call_target="tpu_custom_call" | custom-call | tf_op jit(solution)/shard_map/pallas_call | solution.py:225
  49.6 0.0 collective-permute-done.14.f_got_ref
  49.6 0.6 %collective-permute-done.15.g_got_ref = bf16[384,128]{1,0:T(8,128)(2,1)S(1)} collective-permute-done((bf16[384,128]{1,0:T(8,128)(2,1)S(1)}, bf16[384,128]{1,0:T(8,128)(2,1)S(1)}, u32[]{:S(2)}, u32[]{:S(2)}) %collective-permute-start.15) | collective-permute-done | bytes 98336 | tf_op jit(solution)/shard_map/ppermute | solution.py:44
  50.3 1.7 %shard_map.91 = (f32[2,192,256]{2,1,0:T(8,128)}, f32[1,256]{1,0:T(1,128)}) custom-call(s32[1,256]{1,0:T(1,128)S(1)} %bitcast.7, f32[384,256]{1,0:T(8,128)S(1)} %shard_map.89.base_ref, bf16[384,128]{1,0:T(8,128)(2,1)S(1)} %collective-permute-done.12.f_ref, bf16[384,128]{1,0:T(8,128)(2,1)S(1)} %collective-permute-done.13.g_ref, ...), custom_call_target="tpu_custom_call" | custom-call | tf_op jit(solution)/shard_map/pallas_call | solution.py:230
  (13 shorter events, 0.1 us)
Async XLA Ops:
  0.6 1.4 %copy-start = (bf16[3,2,256,512]{3,2,1,0:T(8,128)(2,1)S(1)}, bf16[3,2,256,512]{3,2,1,0:T(8,128)(2,1)}, u32[]{:S(2)}) copy-start(bf16[3,2,256,512]{3,2,1,0:T(8,128)(2,1)} %basis_ref.5) | copy-start | bytes 4718596
  2.0 0.9 %copy-start.4 = (bf16[2,192,256]{2,1,0:T(8,128)(2,1)S(1)}, bf16[2,192,256]{2,1,0:T(8,128)(2,1)}, u32[]{:S(2)}) copy-start(bf16[2,192,256]{2,1,0:T(8,128)(2,1)} %src_ref.1) | copy-start | bytes 589828
  3.0 0.7 %copy-start.6 = (s32[256]{0:T(256)S(1)}, s32[256]{0:T(256)}, u32[]{:S(2)}) copy-start(s32[256]{0:T(256)} %param.13) | copy-start | bytes 3076
  3.6 1.4 %copy-start.1 = (bf16[3,2,256,512]{3,2,1,0:T(8,128)(2,1)S(1)}, bf16[3,2,256,512]{3,2,1,0:T(8,128)(2,1)}, u32[]{:S(2)}) copy-start(bf16[3,2,256,512]{3,2,1,0:T(8,128)(2,1)} %basis_ref.5) | copy-start | bytes 4718596
  3.6 2.6 %copy-start.3 = (bf16[2,2,8,128,128]{4,3,2,1,0:T(8,128)(2,1)S(1)}, bf16[2,2,8,128,128]{4,3,2,1,0:T(8,128)(2,1)}, u32[]{:S(2)}) copy-start(bf16[2,2,8,128,128]{4,3,2,1,0:T(8,128)(2,1)} %near_ref.1) | copy-start | bytes 3145732
  3.7 2.6 %copy-start.8 = (s32[2,8]{1,0:T(2,128)S(1)}, s32[2,8]{1,0:T(2,128)}, u32[]{:S(2)}) copy-start(s32[2,8]{1,0:T(2,128)} %index_ref.1) | copy-start | bytes 196
  5.6 8.8 %collective-permute-start.2 = (f32[2,384,256]{2,1,0:T(8,128)S(1)}, f32[2,384,256]{2,1,0:T(8,128)}, u32[]{:S(2)}, u32[]{:S(2)}) collective-permute-start(f32[2,384,256]{2,1,0:T(8,128)S(1)} %get-tuple-element.19), channel_id=1, source_target_pairs={{0,1},{1,0},{2,3},{3,2},{4,5},{5,4},{6,7},{7,6},{8,9},{9,8},{10,11... | collective-permute-start | bytes 2359304 | tf_op jit(solution)/shard_map/ppermute | solution.py:44
  6.2 3.6 %collective-permute-start.8 = (f32[384,256]{1,0:T(8,128)}, f32[384,256]{1,0:T(8,128)S(1)}, u32[]{:S(2)}, u32[]{:S(2)}) collective-permute-start(f32[384,256]{1,0:T(8,128)} %get-tuple-element.21), channel_id=1, source_target_pairs={{0,1},{1,0},{2,3},{3,2},{4,5},{5,4},{6,7},{7,6},{8,9},{9,8},{10,11... | collective-permute-start | bytes 1179656 | tf_op jit(solution)/shard_map/ppermute | solution.py:44
  8.7 40.3 %collective-permute-start = (f32[384,256]{1,0:T(8,128)}, f32[384,256]{1,0:T(8,128)S(1)}, u32[]{:S(2)}, u32[]{:S(2)}) collective-permute-start(f32[384,256]{1,0:T(8,128)} %get-tuple-element.16), channel_id=1, source_target_pairs={{0,1},{1,0},{2,3},{3,2},{4,5},{5,4},{6,7},{7,6},{8,9},{9,8},{10,11... | collective-permute-start | bytes 1179656 | tf_op jit(solution)/shard_map/ppermute | solution.py:44
  9.1 29.5 %collective-permute-start.1 = (bf16[384,256]{1,0:T(8,128)(2,1)S(1)}, bf16[384,256]{1,0:T(8,128)(2,1)S(1)}, u32[]{:S(2)}, u32[]{:S(2)}) collective-permute-start(bf16[384,256]{1,0:T(8,128)(2,1)S(1)} %get-tuple-element.17), channel_id=1, source_target_pairs={{1,2},{3,4},{5,6},{7,8},{9,10},{11,12},{13,14},{2,1},{4,3},{6,5},{... | collective-permute-start | bytes 589832 | tf_op jit(solution)/shard_map/ppermute | solution.py:215
  9.9 8.0 %collective-permute-start.10 = (f32[384,128]{1,0:T(8,128)S(1)}, f32[384,128]{1,0:T(8,128)S(1)}, u32[]{:S(2)}, u32[]{:S(2)}) collective-permute-start(f32[384,128]{1,0:T(8,128)S(1)} %get-tuple-element.23), channel_id=1, source_target_pairs={{1,7},{3,5},{5,3},{7,1},{9,15},{11,13},{13,11},{15,9},{17,23},{19,... | collective-permute-start | bytes 589832 | tf_op jit(solution)/shard_map/ppermute | solution.py:53
  10.5 12.0 %collective-permute-start.9 = (f32[384,128]{1,0:T(8,128)S(1)}, f32[384,128]{1,0:T(8,128)S(1)}, u32[]{:S(2)}, u32[]{:S(2)}) collective-permute-start(f32[384,128]{1,0:T(8,128)S(1)} %get-tuple-element.22), channel_id=1, source_target_pairs={{0,2},{1,5},{2,0},{3,7},{4,6},{5,1},{6,4},{7,3},{8,10},{9,13},{10,... | collective-permute-start | bytes 589832 | tf_op jit(solution)/shard_map/ppermute | solution.py:53
  15.6 33.3 %copy-start.2 = (bf16[3,2,256,512]{3,2,1,0:T(8,128)(2,1)S(1)}, bf16[3,2,256,512]{3,2,1,0:T(8,128)(2,1)}, u32[]{:S(2)}) copy-start(bf16[3,2,256,512]{3,2,1,0:T(8,128)(2,1)} %basis_ref.7) | copy-start | bytes 4718596
  15.7 12.0 %collective-permute-start.3 = (bf16[384,256]{1,0:T(8,128)(2,1)S(1)}, bf16[384,256]{1,0:T(8,128)(2,1)S(1)}, u32[]{:S(2)}, u32[]{:S(2)}) collective-permute-start(bf16[384,256]{1,0:T(8,128)(2,1)S(1)} %get-tuple-element.27), channel_id=1, source_target_pairs={{0,4},{1,5},{2,6},{3,7},{4,0},{5,1},{6,2},{7,3},{8,12},{9,13},{10,... | collective-permute-start | bytes 589832 | tf_op jit(solution)/shard_map/ppermute | solution.py:44
  17.9 10.8 %collective-permute-start.4 = (bf16[384,256]{1,0:T(8,128)(2,1)S(1)}, bf16[384,256]{1,0:T(8,128)(2,1)S(1)}, u32[]{:S(2)}, u32[]{:S(2)}) collective-permute-start(bf16[384,256]{1,0:T(8,128)(2,1)S(1)} %get-tuple-element.27), channel_id=1, source_target_pairs={{0,6},{1,7},{2,4},{3,5},{4,2},{5,3},{6,0},{7,1},{8,14},{9,15},{10,... | collective-permute-start | bytes 589832 | tf_op jit(solution)/shard_map/ppermute | solution.py:44
  22.5 13.3 %collective-permute-start.11 = (f32[384,128]{1,0:T(8,128)S(1)}, f32[384,128]{1,0:T(8,128)S(1)}, u32[]{:S(2)}, u32[]{:S(2)}) collective-permute-start(f32[384,128]{1,0:T(8,128)S(1)} %select_add_fusion), channel_id=1, source_target_pairs={{0,1},{1,0},{2,3},{3,2},{4,5},{5,4},{6,7},{7,6},{8,9},{9,8},{10,11... | collective-permute-start | bytes 589832 | tf_op jit(solution)/shard_map/ppermute | solution.py:44
  27.7 8.0 %collective-permute-start.6 = (bf16[384,256]{1,0:T(8,128)(2,1)S(1)}, bf16[384,256]{1,0:T(8,128)(2,1)S(1)}, u32[]{:S(2)}, u32[]{:S(2)}) collective-permute-start(bf16[384,256]{1,0:T(8,128)(2,1)S(1)} %get-tuple-element.26), channel_id=1, source_target_pairs={{0,2},{1,3},{2,0},{3,1},{4,6},{5,7},{6,4},{7,5},{8,10},{9,11},{10,... | collective-permute-start | bytes 589832 | tf_op jit(solution)/shard_map/ppermute | solution.py:44
  28.7 20.2 %collective-permute-start.5 = (bf16[384,256]{1,0:T(8,128)(2,1)S(1)}, bf16[384,256]{1,0:T(8,128)(2,1)S(1)}, u32[]{:S(2)}, u32[]{:S(2)}) collective-permute-start(bf16[384,256]{1,0:T(8,128)(2,1)S(1)} %add_convert_fusion.1.two_ref), channel_id=1, source_target_pairs={{0,1},{1,0},{2,3},{3,2},{4,5},{5,4},{6,7},{7,6},{8,9},{9,8},{10,11... | collective-permute-start | bytes 589832 | tf_op jit(solution)/shard_map/ppermute | solution.py:44
  35.7 13.2 %collective-permute-start.7 = (bf16[384,256]{1,0:T(8,128)(2,1)S(1)}, bf16[384,256]{1,0:T(8,128)(2,1)S(1)}, u32[]{:S(2)}, u32[]{:S(2)}) collective-permute-start(bf16[384,256]{1,0:T(8,128)(2,1)S(1)} %collective-permute-done.6.three_ref), channel_id=1, source_target_pairs={{0,1},{1,0},{2,3},{3,2},{4,5},{5,4},{6,7},{7,6},{8,9},{9,8},{10,11... | collective-permute-start | bytes 589832 | tf_op jit(solution)/shard_map/ppermute | solution.py:44
  35.9 10.8 %collective-permute-start.12 = (bf16[384,128]{1,0:T(8,128)(2,1)S(1)}, bf16[384,128]{1,0:T(8,128)(2,1)S(1)}, u32[]{:S(2)}, u32[]{:S(2)}) collective-permute-start(bf16[384,128]{1,0:T(8,128)(2,1)S(1)} %add_convert_fusion.2), channel_id=1, source_target_pairs={{0,8},{1,13},{2,10},{3,15},{4,12},{5,9},{6,14},{7,11},{8,0},{9,5},... | collective-permute-start | bytes 294920 | tf_op jit(solution)/shard_map/ppermute | solution.py:53
  38.6 10.4 %collective-permute-start.13 = (bf16[384,128]{1,0:T(8,128)(2,1)S(1)}, bf16[384,128]{1,0:T(8,128)(2,1)S(1)}, u32[]{:S(2)}, u32[]{:S(2)}) collective-permute-start(bf16[384,128]{1,0:T(8,128)(2,1)S(1)} %add_convert_fusion.2), channel_id=1, source_target_pairs={{0,10},{1,15},{2,8},{3,13},{4,14},{5,11},{6,12},{7,9},{8,2},{9,7},... | collective-permute-start | bytes 294920 | tf_op jit(solution)/shard_map/ppermute | solution.py:53
  46.7 2.9 %collective-permute-start.14 = (bf16[384,128]{1,0:T(8,128)(2,1)S(1)}, bf16[384,128]{1,0:T(8,128)(2,1)S(1)}, u32[]{:S(2)}, u32[]{:S(2)}) collective-permute-start(bf16[384,128]{1,0:T(8,128)(2,1)S(1)} %collective-permute-done.12.f_ref), channel_id=1, source_target_pairs={{0,1},{1,0},{2,3},{3,2},{4,5},{5,4},{6,7},{7,6},{8,9},{9,8},{10,11... | collective-permute-start | bytes 294920 | tf_op jit(solution)/shard_map/ppermute | solution.py:44
  48.9 1.3 %collective-permute-start.15 = (bf16[384,128]{1,0:T(8,128)(2,1)S(1)}, bf16[384,128]{1,0:T(8,128)(2,1)S(1)}, u32[]{:S(2)}, u32[]{:S(2)}) collective-permute-start(bf16[384,128]{1,0:T(8,128)(2,1)S(1)} %collective-permute-done.13.g_ref), channel_id=1, source_target_pairs={{0,1},{1,0},{2,3},{3,2},{4,5},{5,4},{6,7},{7,6},{8,9},{9,8},{10,11... | collective-permute-start | bytes 294920 | tf_op jit(solution)/shard_map/ppermute | solution.py:44
  49.0 1.3 %copy-start.5 = (bf16[2,192,256]{2,1,0:T(8,128)(2,1)S(1)}, bf16[2,192,256]{2,1,0:T(8,128)(2,1)}, u32[]{:S(2)}) copy-start(bf16[2,192,256]{2,1,0:T(8,128)(2,1)} %forward_ref.1) | copy-start | bytes 589828
  49.0 1.3 %copy-start.7 = (s32[256]{0:T(256)S(1)}, s32[256]{0:T(256)}, u32[]{:S(2)}) copy-start(s32[256]{0:T(256)} %param.13) | copy-start | bytes 3076

commit v2 on v1

--- a/solution.py
+++ b/solution.py
@@ -10,7 +10,7 @@
 TREE = ("leaf", "rhs")
 F32 = jnp.float32
 BF16 = jnp.bfloat16
-VMEM_BYTES = 24 * 1024 * 1024
+VMEM_BYTES = 12 * 1024 * 1024
 
 
 def dot(a, b):
@@ -21,18 +21,19 @@
     return lax.dot_general(a, b, (((1,), (1,)), ((), ())), preferred_element_type=F32)
 
 
-def call(kernel, out_shape, scratch_shapes=(), smem=(), inputs=0):
-    in_specs = [
-        pl.BlockSpec(memory_space=pltpu.SMEM if i in smem else pltpu.VMEM) for i in range(inputs)
-    ]
-    out_specs = jax.tree.map(lambda _: pl.BlockSpec(memory_space=pltpu.VMEM), out_shape)
+def call(kernel, out_shape, inputs, scratch_shapes=(), smem=(), far=(), vmem=VMEM_BYTES):
+    def place(i):
+        if i in far:
+            return pl.BlockSpec(memory_space=pltpu.HBM)
+        return pl.BlockSpec(memory_space=pltpu.SMEM if i in smem else pltpu.VMEM)
+
     return pl.pallas_call(
         kernel,
         out_shape=out_shape,
-        in_specs=in_specs,
-        out_specs=out_specs,
+        in_specs=[place(i) for i in range(inputs)],
+        out_specs=jax.tree.map(lambda _: pl.BlockSpec(memory_space=pltpu.VMEM), out_shape),
         scratch_shapes=list(scratch_shapes),
-        compiler_params=pltpu.CompilerParams(vmem_limit_bytes=VMEM_BYTES),
+        compiler_params=pltpu.CompilerParams(vmem_limit_bytes=vmem),
     )
 
 
@@ -53,6 +54,28 @@
     return lax.ppermute(x, TREE, pairs)
 
 
+def after(x, *others):
+    return lax.optimization_barrier((x, *others))[0]
+
+
+EXTRA = 16
+TOP = 14.0
+
+
+def scaled_to(out_ref, values):
+    rows = values.shape[0]
+    largest = jnp.max(jnp.max(jnp.abs(values), axis=0, keepdims=True), axis=1, keepdims=True)
+    power = jnp.clip(jnp.ceil(jnp.log2(jnp.maximum(largest, 1e-30))), -100.0, 100.0)
+    out_ref[:rows] = values * jnp.exp2(TOP - power)
+    out_ref[rows:] = jnp.broadcast_to(power, (EXTRA, values.shape[1]))
+
+
+def unscaled(packed):
+    packed = packed.astype(F32)
+    rows = packed.shape[0] - EXTRA
+    return packed[:rows] * jnp.exp2(packed[rows : rows + 1] - TOP)
+
+
 def one_hot_of(order_ref, panels):
     local = lax.rem(order_ref[...], panels)
     rows = lax.broadcasted_iota(jnp.int32, (panels, panels), 0)
@@ -72,33 +95,53 @@
     return place & 1, (place >> 1) & 1, (place >> 2) & 1
 
 
-def first_kernel(order_ref, src_ref, basis_ref, tree_ref, send_ref, keep_ref):
+def first_kernel(
+    order_hbm,
+    src_hbm,
+    basis_hbm,
+    tree_ref,
+    send_1_ref,
+    keep_1_ref,
+    part_2_ref,
+    send_3_ref,
+    keep_3_ref,
+    order,
+    source,
+    basis,
+    sems,
+):
     core, _, low = position()
-    two, rows, panels = src_ref.shape
-    rank = basis_ref.shape[3]
+    two, rows, panels = source.shape
+    rank = basis.shape[3]
     half = rank // 2
-    source = src_ref[...].reshape(two * rows, panels)
-    tree = dot(source, one_hot_of(order_ref, panels)).astype(BF16)
+    copies = [
+        pltpu.make_async_copy(order_hbm, order, sems.at[0]),
+        pltpu.make_async_copy(src_hbm, source, sems.at[1]),
+    ] + [
+        pltpu.make_async_copy(basis_hbm.at[level], basis.at[level], sems.at[2 + level])
+        for level in range(3)
+    ]
+    for copy in copies:
+        copy.start()
+    copies[0].wait()
+    one_hot = one_hot_of(order, panels)
+    copies[1].wait()
+    tree = dot(source[...].reshape(two * rows, panels), one_hot).astype(BF16)
     tree_ref[...] = tree
     stack = signed_stack(tree)
-    mine = pl.multiple_of((low ^ core) * half, half)
-    theirs = pl.multiple_of((low ^ core ^ 1) * half, half)
-    for start, out in ((theirs, send_ref), (mine, keep_ref)):
-        basis = basis_ref[0, :, :, pl.ds(start, half)].reshape(2 * panels, half)
-        out[...] = dot(stack, basis)
-
-
-def second_kernel(tree_ref, basis_ref, send_ref, keep_ref):
-    core, _, _ = position()
-    levels, _, panels, rank = basis_ref.shape
-    half = rank // 2
-    stack = signed_stack(tree_ref[...])
-    mine = pl.multiple_of(core * half, half)
-    theirs = pl.multiple_of((core ^ 1) * half, half)
-    for start, out in ((theirs, send_ref), (mine, keep_ref)):
-        for level in range(1, levels):
-            basis = basis_ref[level, :, :, pl.ds(start, half)].reshape(2 * panels, half)
-            out[level - 1] = dot(stack, basis)
+
+    def product(level, start, width):
+        columns = basis[level, :, :, pl.ds(start, width)].reshape(2 * panels, width)
+        return dot(stack, columns)
+
+    copies[2].wait()
+    send_1_ref[...] = product(0, pl.multiple_of((low ^ core ^ 1) * half, half), half)
+    keep_1_ref[...] = product(0, pl.multiple_of((low ^ core) * half, half), half)
+    copies[3].wait()
+    part_2_ref[...] = product(1, 0, rank)
+    copies[4].wait()
+    send_3_ref[...] = product(2, pl.multiple_of((core ^ 1) * half, half), half)
+    keep_3_ref[...] = product(2, pl.multiple_of(core * half, half), half)
 
 
 def near_kernel(index_ref, tree_ref, near_ref, core_ref, far_ref, own_ref, sums):
@@ -116,7 +159,7 @@
         lanes = pl.ds(j * size, size)
         own_ref[:, lanes] = sums[block_count + j]
         far_ref[:, lanes] = sums[core * 2 * block_count + j].astype(BF16)
-        core_ref[:, lanes] = sums[(1 - core) * 2 * block_count + j]
+        core_ref[:, lanes] = sums[(1 - core) * 2 * block_count + j].astype(BF16)
 
 
 def spread_kernel(keep_ref, got_ref, out_ref, other_ref):
@@ -128,6 +171,11 @@
     other_ref[...] = keep_ref[:, other_lanes] + got_ref[:, other_lanes]
 
 
+def sums_kernel(part_2_ref, got_2_ref, keep_3_ref, got_3_ref, two_ref, three_ref):
+    three_ref[...] = (keep_3_ref[...] + got_3_ref[...]).astype(BF16)
+    scaled_to(two_ref, part_2_ref[...] + got_2_ref[...])
+
+
 def expanded(coefficient, basis_ref, level, start, width):
     half = coefficient.shape[0] // 2
     turned = jnp.concatenate([-coefficient[half:], coefficient[:half]], axis=0)
@@ -137,25 +185,29 @@
     )
 
 
-def middle_kernel(own_ref, core_ref, far_ref, two_ref, two_got_ref, three_ref, three_got_ref, basis_ref, out_ref):
+def halo_kernel(own_ref, far_ref, three_ref, pair_ref, basis_ref, out_ref):
     core, _, _ = position()
-    half = two_ref.shape[1]
-    total = own_ref[...] + core_ref[...] + far_ref[...].astype(F32)
-    for level, mine_ref, got_ref in ((1, two_ref, two_got_ref), (2, three_ref, three_got_ref)):
-        total += expanded(mine_ref[...], basis_ref, level, pl.multiple_of(core * half, half), half)
-        total += expanded(got_ref[...], basis_ref, level, pl.multiple_of((1 - core) * half, half), half)
+    rows, half = three_ref.shape
+    total = own_ref[...] + far_ref[...].astype(F32) + pair_ref[rows:].astype(F32)
+    total += expanded(three_ref[...], basis_ref, 2, pl.multiple_of(core * half, half), half)
+    total += expanded(pair_ref[:rows], basis_ref, 2, pl.multiple_of((1 - core) * half, half), half)
     out_ref[...] = total
 
 
+def second_kernel(base_ref, two_ref, basis_ref, out_ref):
+    out_ref[...] = base_ref[...] + expanded(two_ref[...], basis_ref, 1, 0, two_ref.shape[1])
+
+
 def last_kernel(
-    order_ref, base_ref, f_ref, g_ref, f_got_ref, g_got_ref, basis_ref, forward_ref, field_ref, grad_ref, full
+    order_ref, base_ref, mine_ref, got_ref, basis_ref, forward_ref, field_ref, grad_ref, full
 ):
     core, across, low = position()
-    width = f_ref.shape[1]
+    both = base_ref.shape[0]
+    width = mine_ref.shape[1]
     mine = low ^ core
-    for half, first, second in ((mine, f_ref, g_ref), (mine ^ 1, f_got_ref, g_got_ref)):
-        full[:, pl.ds(pl.multiple_of((2 * half + across) * width, width), width)] = first[...]
-        full[:, pl.ds(pl.multiple_of((2 * half + (across ^ 1)) * width, width), width)] = second[...]
+    for half, part in ((mine, mine_ref), (mine ^ 1, got_ref)):
+        full[:, pl.ds(pl.multiple_of((2 * half + across) * width, width), width)] = part[:both]
+        full[:, pl.ds(pl.multiple_of((2 * half + (across ^ 1)) * width, width), width)] = part[both:]
     total = base_ref[...] + expanded(full[...], basis_ref, 0, 0, 4 * width)
     two, rows, panels = field_ref.shape
     one_hot = one_hot_of(order_ref, panels)
@@ -176,63 +228,72 @@
     half, quarter = rank // 2, rank // 4
     order = cluster_order.reshape(1, panels)
     core = lax.axis_index(TREE) & 1
-
-    tree, send_1, keep_1 = call(
+    halves = array((both, half), F32)
+
+    tree, send_1, keep_1, part_2, send_3, keep_3 = call(
         first_kernel,
-        (array((both, panels), BF16), array((both, half), F32), array((both, half), F32)),
-        inputs=3,
+        (array((both, panels), BF16), halves, halves, array((both, rank), F32), halves, halves),
+        3,
+        scratch_shapes=[
+            pltpu.VMEM((1, panels), jnp.int32),
+            pltpu.VMEM((two, rows, panels), BF16),
+            pltpu.VMEM((3, 2, panels, rank), BF16),
+            pltpu.SemaphoreType.DMA((5,)),
+        ],
+        far=(0, 1, 2),
+        vmem=56 * 1024 * 1024,
     )(order, sources, row_bases)
     got_1 = swapped(send_1, 1)
-    send_23, keep_23 = call(
-        second_kernel, (array((2, both, half), F32), array((2, both, half), F32)), inputs=2
-    )(tree, row_bases)
-    got_23 = swapped(send_23, 1)
-
-    to_a, other = call(
-        spread_kernel, (array((both, quarter), F32), array((both, quarter), F32)), inputs=2
-    )(keep_1, got_1)
-    got_a = by_core(to_a, 2, 4)
-    got_b = by_core(other, None, 6)
-
-    sum_23 = keep_23 + got_23
-    mine_3 = swapped(sum_23[1].astype(BF16), 2)
-    two_sent = sum_23[0].astype(BF16)
-    got_c = swapped(two_sent, 4)
-    got_d = swapped(two_sent, 6)
+    got_3 = swapped(send_3, 1)
+    got_2 = swapped(part_2, 1)
 
     blocks = near_blocks.shape[1]
     size = near_blocks.shape[3]
     to_core, to_far, own = call(
         near_kernel,
-        (array((both, panels), F32), array((both, panels), BF16), array((both, panels), F32)),
+        (array((both, panels), BF16), array((both, panels), BF16), array((both, panels), F32)),
+        3,
         scratch_shapes=[pltpu.VMEM((3 * blocks, both, size), F32)],
         smem=(0,),
-        inputs=3,
     )(near_index, tree, near_blocks)
-    core_halo = swapped(to_core, 1)
+
+    got_1, own = lax.optimization_barrier((got_1, own))
+    to_a, to_b = call(
+        spread_kernel, (array((both, quarter), F32), array((both, quarter), F32)), 2
+    )(keep_1, got_1)
+    got_a = by_core(to_a, 2, 4)
+    got_b = by_core(to_b, None, 6)
+
+    two_sent, three_sent = call(
+        sums_kernel, (array((both + EXTRA, rank), F32), array((both, half), BF16)), 4
+    )(part_2, got_2, keep_3, after(got_3, to_a))
+    mine_3 = swapped(three_sent, 2)
+    two_sent = two_sent.astype(jnp.float16)
+    got_cd = by_core(two_sent, 4, 6)
     peers = lax.axis_size(TREE)
     joints = [(i, i + 1) for i in range(1, peers - 1, 2)]
-    far_halo = lax.ppermute(to_far, TREE, joints + [(b, a) for a, b in joints])
-
-    middle = got_a + jnp.where(core == 0, other, got_b)
-    quarter_sum = (middle + swapped(middle, 1)).astype(BF16)
+    far_halo = lax.ppermute(after(to_far, to_a), TREE, joints + [(b, a) for a, b in joints])
+
+    got_a, got_b, _ = lax.optimization_barrier((got_a, got_b, two_sent))
+    middle = got_a + jnp.where(core == 0, to_b, got_b)
+    parts = lax.all_gather(middle, "rhs", axis=0)
+    quarter_sum = (parts[0] + parts[1]).astype(BF16)
     got_f = by_core(quarter_sum, 8, 12)
     got_g = by_core(quarter_sum, 10, 14)
 
-    mine_2 = (got_c.astype(F32) + got_d.astype(F32)).astype(BF16)
-    other_3 = swapped(mine_3, 1)
-    other_2 = swapped(mine_2, 1)
-    base = call(middle_kernel, array((both, panels), F32), inputs=8)(
-        own, core_halo, far_halo, mine_2, other_2, mine_3, other_3, col_bases
-    )
-    core_f = swapped(got_f, 1)
-    core_g = swapped(got_g, 1)
+    mine_3, own, _ = lax.optimization_barrier((mine_3, own, quarter_sum))
+    pair_3 = swapped(jnp.concatenate([mine_3, to_core], axis=0), 1)
+    base = call(halo_kernel, array((both, panels), F32), 5)(own, far_halo, mine_3, pair_3, col_bases)
+    got_cd = after(got_cd, quarter_sum)
+    all_2 = (unscaled(got_cd) + unscaled(swapped(got_cd, 1))).astype(BF16)
+    base = call(second_kernel, array((both, panels), F32), 3)(base, all_2, col_bases)
+    mine_1 = jnp.concatenate([got_f, got_g], axis=0)
     field, grad = call(
         last_kernel,
         (array((two, rows, panels), F32), array((1, panels), F32)),
+        6,
         scratch_shapes=[pltpu.VMEM((both, rank), BF16)],
-        inputs=8,
-    )(order, base, got_f, got_g, core_f, core_g, col_bases, forward_field)
+    )(order, base, mine_1, swapped(mine_1, 1), col_bases, forward_field)
     return field, grad.reshape(panels)
 
 

time: 52.2 us -> 40.2 us (0.77)
  waiting for transfers between devices: 18.1 us -> 8.12 us
  starting transfers between devices: 21.9 us -> 17 us
  blocking collectives: 0 us -> 2.09 us
  Pallas kernels: 6.59 us -> 7.95 us
  local copies, waits for them, and re-layouts: 3.22 us -> 2.37 us
    ppermute x4 -> x5, waiting for transfers between devices: 12.6 us -> 3.97 us  [by_core(): return lax.ppermute(x, TREE, pairs)]
    ppermute x11 -> x7, starting transfers between devices: 12.6 us -> 4.59 us  [swapped(): lax.ppermute(x, TREE, [(i, i ^ distance) for i in range(lax.axis_size(TRE...]
    ppermute x4 -> x5, starting transfers between devices: 8.67 us -> 11.7 us  [by_core(): return lax.ppermute(x, TREE, pairs)]
    all_gather x0 -> x1, blocking collectives: none -> 2.09 us  [fast_body(): parts = lax.all_gather(middle, 'rhs', axis=0)]
    pallas_call x4 -> x5, Pallas kernels: 4.86 us -> 6.24 us  [the longest x1 3.51 us: fast_body(): call(first_kernel, (array((both, panels), BF16), halves, halves, array((b...]
    ppermute x11 -> x7, waiting for transfers between devices: 5.47 us -> 4.15 us  [swapped(): lax.ppermute(x, TREE, [(i, i ^ distance) for i in range(lax.axis_size(TRE...]
    another operation x1 -> x0, other arithmetic: 1.21 us -> none
    add x1, other arithmetic: 0.03 us -> 0.96 us  [fast_body(): middle = got_a + jnp.where(core == 0, to_b, got_b)]
  transfers between devices with their start and end apart: 16 -> 13, of which waited for: 6 -> 4; matrix products, arithmetic and copies ran while one was open for 3% -> 4% of each run, Pallas kernels for 6% -> 7%
where the time goes in v2:
time: 40.2 us; the launch traced here: 39.9 us
  starting transfers between devices  17 us (42%)
  waiting for transfers between devices  8.12 us (20%)
  Pallas kernels  7.95 us (20%)
  local copies, waits for them, and re-layouts  2.37 us (6%)
  blocking collectives  2.09 us (5%)
  other arithmetic  1.47 us (4%)
  between operations  0.88 us (2%)
    ppermute x5, starting transfers between devices, by_core(): return lax.ppermute(x, TREE, pairs)  11.7 us
    ppermute x7, starting transfers between devices, swapped(): lax.ppermute(x, TREE, [(i, i ^ distance) for i in range(lax.axis_size(TRE...  4.59 us
    ppermute x7, waiting for transfers between devices, swapped(): lax.ppermute(x, TREE, [(i, i ^ distance) for i in range(lax.axis_size(TRE...  4.15 us
    ppermute x5, waiting for transfers between devices, by_core(): return lax.ppermute(x, TREE, pairs)  3.97 us
    pallas_call x1, Pallas kernels, fast_body(): call(first_kernel, (array((both, panels), BF16), halves, halves, array((b...  3.51 us
    unnamed x19, local copies, waits for them, and re-layouts  2.36 us
    all_gather x1, blocking collectives, fast_body(): parts = lax.all_gather(middle, 'rhs', axis=0)  2.09 us
    pallas_call x1, Pallas kernels, fast_body(): call(last_kernel, (array((two, rows, panels), F32), array((1, panels), F3...  1.66 us
  transfers between devices with their start and end apart: 13, of which 4 were waited for; matrix products, arithmetic and copies ran while one was open for 4% of the time, Pallas kernels for 7%

profile of v2, /device:TPU:0, one launch (start us, length us, event | category | flops | bytes accessed | tf_op | source)
XLA Modules:
  0.0 39.9 jit_solution(4617514483736310509)
XLA Ops:
  0.6 0.0 copy-start.1
  0.6 0.0 copy-start.8
  0.7 3.5 %shard_map.86 = (bf16[384,256]{1,0:T(8,128)(2,1)}, f32[384,256]{1,0:T(8,128)}, f32[384,256]{1,0:T(8,128)}, f32[384,512]{1,0:T(8,128)}, f32[384,256]{1,0:T(8,128)}, /*index=5*/f32[384,256]{1,0:T(8,128)}) custom-call(s32[1,256]{1,0:T(1,128)} %bitcast.4, bf16[2,192,256]{2,1,0:T(8,128)(2,1)} %src_hbm.1, bf16[3,2,256,512]{3,2,1,0:T(8,128)(2,1)} %basis_hbm.1), custom_call_target="tpu_custom_call" | custom-call | tf_op jit(solution)/shard_map/pallas_call | solution.py:233
  4.2 0.0 copy-start.2
  4.2 0.0 copy-start.3
  4.2 0.5 %collective-permute-start = (f32[384,512]{1,0:T(8,128)}, f32[384,512]{1,0:T(8,128)S(1)}, u32[]{:S(2)}, u32[]{:S(2)}) collective-permute-start(f32[384,512]{1,0:T(8,128)} %get-tuple-element.26.part_2_ref), channel_id=1, source_target_pairs={{0,1},{1,0},{2,3},{3,2},{4,5},{5,4},{6,7},{7,6},{8,9},{9,8},{10,11... | collective-permute-start | bytes 2359304 | tf_op jit(solution)/shard_map/ppermute | solution.py:45
  4.7 0.1 collective-permute-start.2
  4.8 0.4 %collective-permute-start.1 = (f32[384,256]{1,0:T(8,128)}, f32[384,256]{1,0:T(8,128)S(1)}, u32[]{:S(2)}, u32[]{:S(2)}) collective-permute-start(f32[384,256]{1,0:T(8,128)} %get-tuple-element.28), channel_id=1, source_target_pairs={{0,1},{1,0},{2,3},{3,2},{4,5},{5,4},{6,7},{7,6},{8,9},{9,8},{10,11... | collective-permute-start | bytes 1179656 | tf_op jit(solution)/shard_map/ppermute | solution.py:45
  5.2 0.9 %copy-done.6 = bf16[384,256]{1,0:T(8,128)(2,1)S(1)} copy-done((bf16[384,256]{1,0:T(8,128)(2,1)S(1)}, bf16[384,256]{1,0:T(8,128)(2,1)}, u32[]{:S(2)}) %copy-start.6) | copy-done | bytes 196632
  6.1 1.6 %shard_map.87 = (bf16[384,256]{1,0:T(8,128)(2,1)S(1)}, bf16[384,256]{1,0:T(8,128)(2,1)S(1)}, f32[384,256]{1,0:T(8,128)S(1)}) custom-call(s32[2,8]{1,0:T(2,128)S(1)} %copy-done.8, bf16[384,256]{1,0:T(8,128)(2,1)S(1)} %copy-done.6, bf16[2,2,8,128,128]{4,3,2,1,0:T(8,128)(2,1)S(1)} %copy-done.1), custom_call_target="tpu_custom_call" | custom-call | tf_op jit(solution)/shard_map/pallas_call | solution.py:252
  7.8 0.0 collective-permute-done.2.got_ref
  7.8 1.0 %copy-done.4 = f32[384,256]{1,0:T(8,128)S(1)} copy-done((f32[384,256]{1,0:T(8,128)S(1)}, f32[384,256]{1,0:T(8,128)}, u32[]{:S(2)}) %copy-start.4) | copy-done | bytes 393240
  8.8 0.1 shard_map.88
  8.9 2.6 %collective-permute-start.4 = (f32[384,128]{1,0:T(8,128)S(1)}, f32[384,128]{1,0:T(8,128)}, u32[]{:S(2)}, u32[]{:S(2)}) collective-permute-start(f32[384,128]{1,0:T(8,128)S(1)} %get-tuple-element.34), channel_id=1, source_target_pairs={{0,2},{1,5},{2,0},{3,7},{4,6},{5,1},{6,4},{7,3},{8,10},{9,13},{10,... | collective-permute-start | bytes 589832 | tf_op jit(solution)/shard_map/ppermute | solution.py:54
  11.5 1.3 %collective-permute-start.5 = (f32[384,128]{1,0:T(8,128)S(1)}, f32[384,128]{1,0:T(8,128)}, u32[]{:S(2)}, u32[]{:S(2)}) collective-permute-start(f32[384,128]{1,0:T(8,128)S(1)} %get-tuple-element.38), channel_id=1, source_target_pairs={{1,7},{3,5},{5,3},{7,1},{9,15},{11,13},{13,11},{15,9},{17,23},{19,... | collective-permute-start | bytes 589832 | tf_op jit(solution)/shard_map/ppermute | solution.py:54
  12.8 0.0 collective-permute-done.1.got_3_ref
  12.8 0.7 %collective-permute-start.6 = (bf16[384,256]{1,0:T(8,128)(2,1)S(1)}, bf16[384,256]{1,0:T(8,128)(2,1)S(1)}, u32[]{:S(2)}, u32[]{:S(2)}) collective-permute-start(bf16[384,256]{1,0:T(8,128)(2,1)S(1)} %get-tuple-element.44), channel_id=1, source_target_pairs={{1,2},{3,4},{5,6},{7,8},{9,10},{11,12},{13,14},{2,1},{4,3},{6,5},{... | collective-permute-start | bytes 589832 | tf_op jit(solution)/shard_map/ppermute | solution.py:275
  13.5 0.0 collective-permute-done.got_2_ref
  13.5 0.3 shard_map.89
  13.8 0.1 convert_element_type.18
  13.9 4.7 %collective-permute-start.8 = (f16[400,512]{1,0:T(8,128)(2,1)S(1)}, f16[400,512]{1,0:T(8,128)(2,1)S(1)}, u32[]{:S(2)}, u32[]{:S(2)}) collective-permute-start(f16[400,512]{1,0:T(8,128)(2,1)S(1)} %convert_element_type.18), channel_id=1, source_target_pairs={{0,4},{1,7},{2,6},{3,5},{4,0},{5,3},{6,2},{7,1},{8,12},{9,15},{10,... | collective-permute-start | bytes 1228808 | tf_op jit(solution)/shard_map/ppermute | solution.py:54
  18.6 0.0 collective-permute-done.4
  18.6 0.0 collective-permute-done.5
  18.6 1.7 %collective-permute-start.3 = (bf16[384,256]{1,0:T(8,128)(2,1)S(1)}, bf16[384,256]{1,0:T(8,128)(2,1)S(1)}, u32[]{:S(2)}, u32[]{:S(2)}) collective-permute-start(bf16[384,256]{1,0:T(8,128)(2,1)S(1)} %get-tuple-element.36), channel_id=1, source_target_pairs={{0,2},{1,3},{2,0},{3,1},{4,6},{5,7},{6,4},{7,5},{8,10},{9,11},{10,... | collective-permute-start | bytes 589832 | tf_op jit(solution)/shard_map/ppermute | solution.py:45
  20.3 1.0 %select_add_fusion = f32[384,128]{1,0:T(8,128)S(1)} fusion(f32[384,128]{1,0:T(8,128)} %collective-permute-done.4, f32[384,128]{1,0:T(8,128)S(1)} %get-tuple-element.38, f32[384,128]{1,0:T(8,128)} %collective-permute-done.5, pred[]{:T(512)S(6)} %eq.3), kind=kLoop, calls=%fused_computation.7 | loop fusion | flops 98304 | bytes 786433 | tf_op jit(solution)/shard_map/add | solution.py:278
  21.3 2.1 %all-gather = f32[768,128]{1,0:T(8,128)S(1)} all-gather(f32[384,128]{1,0:T(8,128)S(1)} %select_add_fusion), channel_id=2, replica_groups=mesh['groups'=2,'leaf'=8,'rhs'=2] {'rhs'}, dimensions={0}, use_global_device_ids=true | all-gather | bytes 589824 | tf_op jit(solution)/shard_map/all_gather | solution.py:279
  23.4 2.7 %collective-permute-start.10 = (bf16[384,128]{1,0:T(8,128)(2,1)S(1)}, bf16[384,128]{1,0:T(8,128)(2,1)S(1)}, u32[]{:S(2)}, u32[]{:S(2)}) collective-permute-start(bf16[384,128]{1,0:T(8,128)(2,1)S(1)} %fusion.2), channel_id=1, source_target_pairs={{0,8},{1,13},{2,10},{3,15},{4,12},{5,9},{6,14},{7,11},{8,0},{9,5},... | collective-permute-start | bytes 294920 | tf_op jit(solution)/shard_map/ppermute | solution.py:54
  26.1 0.4 %collective-permute-start.11 = (bf16[384,128]{1,0:T(8,128)(2,1)S(1)}, bf16[384,128]{1,0:T(8,128)(2,1)S(1)}, u32[]{:S(2)}, u32[]{:S(2)}) collective-permute-start(bf16[384,128]{1,0:T(8,128)(2,1)S(1)} %fusion.2), channel_id=1, source_target_pairs={{0,10},{1,15},{2,8},{3,13},{4,14},{5,11},{6,12},{7,9},{8,2},{9,7},... | collective-permute-start | bytes 294920 | tf_op jit(solution)/shard_map/ppermute | solution.py:54
  26.5 4.0 %collective-permute-done.3.three_ref = bf16[384,256]{1,0:T(8,128)(2,1)S(1)} collective-permute-done((bf16[384,256]{1,0:T(8,128)(2,1)S(1)}, bf16[384,256]{1,0:T(8,128)(2,1)S(1)}, u32[]{:S(2)}, u32[]{:S(2)}) %collective-permute-start.3) | collective-permute-done | bytes 196640 | tf_op jit(solution)/shard_map/ppermute | solution.py:45
  30.6 1.7 %collective-permute-start.7 = (bf16[768,256]{1,0:T(8,128)(2,1)S(1)}, bf16[768,256]{1,0:T(8,128)(2,1)S(1)}, u32[]{:S(2)}, u32[]{:S(2)}) collective-permute-start(bf16[768,256]{1,0:T(8,128)(2,1)S(1)} %pad_maximum_fusion), channel_id=1, source_target_pairs={{0,1},{1,0},{2,3},{3,2},{4,5},{5,4},{6,7},{7,6},{8,9},{9,8},{10,11... | collective-permute-start | bytes 1179656 | tf_op jit(solution)/shard_map/ppermute | solution.py:45
  32.3 1.9 %collective-permute-done.8 = f16[400,512]{1,0:T(8,128)(2,1)S(1)} collective-permute-done((f16[400,512]{1,0:T(8,128)(2,1)S(1)}, f16[400,512]{1,0:T(8,128)(2,1)S(1)}, u32[]{:S(2)}, u32[]{:S(2)}) %collective-permute-start.8) | collective-permute-done | bytes 409632 | tf_op jit(solution)/shard_map/ppermute | solution.py:54
  34.2 0.0 collective-permute-start.9
  34.2 0.0 collective-permute-done.10
  34.2 2.1 %collective-permute-done.11 = bf16[384,128]{1,0:T(8,128)(2,1)S(1)} collective-permute-done((bf16[384,128]{1,0:T(8,128)(2,1)S(1)}, bf16[384,128]{1,0:T(8,128)(2,1)S(1)}, u32[]{:S(2)}, u32[]{:S(2)}) %collective-permute-start.11) | collective-permute-done | bytes 98336 | tf_op jit(solution)/shard_map/ppermute | solution.py:54
  36.3 0.1 collective-permute-start.12
  36.4 0.1 convert_element_type.21
  36.5 0.0 collective-permute-done.6.far_ref
  36.5 0.0 collective-permute-done.7.pair_ref
  36.5 0.4 %shard_map.90.base_ref = f32[384,256]{1,0:T(8,128)S(1)} custom-call(f32[384,256]{1,0:T(8,128)S(1)} %get-tuple-element.42.own_ref, bf16[384,256]{1,0:T(8,128)(2,1)S(1)} %collective-permute-done.6.far_ref, bf16[384,256]{1,0:T(8,128)(2,1)S(1)} %collective-permute-done.3.three_ref, bf16[768,256]{1,0:T(8,128)(2,1)S(1)} %collective-permute-done.7.pair_ref, ...), custom_call_target="tpu_custom_call" | custom-call | tf_op jit(solution)/shard_map/pallas_call | solution.py:286
  37.0 0.0 collective-permute-done.9
  37.0 0.1 convert_element_type.22
  37.1 0.2 fusion.1.two_ref
  37.3 0.0 copy-start.5
  37.3 0.0 copy-start.7
  37.3 0.4 %shard_map.91.base_ref = f32[384,256]{1,0:T(8,128)S(1)} custom-call(f32[384,256]{1,0:T(8,128)S(1)} %shard_map.90.base_ref, bf16[384,512]{1,0:T(8,128)(2,1)S(1)} %fusion.1.two_ref, bf16[3,2,256,512]{3,2,1,0:T(8,128)(2,1)S(1)} %copy-done), custom_call_target="tpu_custom_call" | custom-call | tf_op jit(solution)/shard_map/pallas_call | solution.py:289
  37.7 0.1 collective-permute-done.12.got_ref
  37.8 0.4 %copy-done.5 = bf16[2,192,256]{2,1,0:T(8,128)(2,1)S(1)} copy-done((bf16[2,192,256]{2,1,0:T(8,128)(2,1)S(1)}, bf16[2,192,256]{2,1,0:T(8,128)(2,1)}, u32[]{:S(2)}) %copy-start.5) | copy-done | bytes 196632
  38.2 1.7 %shard_map.92 = (f32[2,192,256]{2,1,0:T(8,128)}, f32[1,256]{1,0:T(1,128)}) custom-call(s32[1,256]{1,0:T(1,128)S(1)} %bitcast.5, f32[384,256]{1,0:T(8,128)S(1)} %shard_map.91.base_ref, bf16[768,128]{1,0:T(8,128)(2,1)S(1)} %constant_dynamic-update-slice_fusion.mine_ref, bf16[768,128]{1,0:T(8,128)(2,1)S(1)} %collective-permute-done.12.got_ref, ...), custom_call_target="tpu_custom_call" | custom-call | tf_op jit(solution)/shard_map/pallas_call | solution.py:291
  (15 shorter events, 0.1 us)
Async XLA Ops:
  0.6 4.6 %copy-start.1 = (bf16[2,2,8,128,128]{4,3,2,1,0:T(8,128)(2,1)S(1)}, bf16[2,2,8,128,128]{4,3,2,1,0:T(8,128)(2,1)}, u32[]{:S(2)}) copy-start(bf16[2,2,8,128,128]{4,3,2,1,0:T(8,128)(2,1)} %near_ref.1) | copy-start | bytes 3145732
  0.6 4.6 %copy-start.8 = (s32[2,8]{1,0:T(2,128)S(1)}, s32[2,8]{1,0:T(2,128)}, u32[]{:S(2)}) copy-start(s32[2,8]{1,0:T(2,128)} %index_ref.1) | copy-start | bytes 196
  4.2 9.3 %copy-start.2 = (f32[384,512]{1,0:T(8,128)S(1)}, f32[384,512]{1,0:T(8,128)}, u32[]{:S(2)}) copy-start(f32[384,512]{1,0:T(8,128)} %get-tuple-element.26.part_2_ref) | copy-start | bytes 2359300
  4.2 9.3 %copy-start.3 = (f32[384,256]{1,0:T(8,128)S(1)}, f32[384,256]{1,0:T(8,128)}, u32[]{:S(2)}) copy-start(f32[384,256]{1,0:T(8,128)} %get-tuple-element.27.keep_3_ref) | copy-start | bytes 1179652
  4.2 9.3 %collective-permute-start = (f32[384,512]{1,0:T(8,128)}, f32[384,512]{1,0:T(8,128)S(1)}, u32[]{:S(2)}, u32[]{:S(2)}) collective-permute-start(f32[384,512]{1,0:T(8,128)} %get-tuple-element.26.part_2_ref), channel_id=1, source_target_pairs={{0,1},{1,0},{2,3},{3,2},{4,5},{5,4},{6,7},{7,6},{8,9},{9,8},{10,11... | collective-permute-start | bytes 2359304 | tf_op jit(solution)/shard_map/ppermute | solution.py:45
  4.7 3.1 %collective-permute-start.2 = (f32[384,256]{1,0:T(8,128)}, f32[384,256]{1,0:T(8,128)S(1)}, u32[]{:S(2)}, u32[]{:S(2)}) collective-permute-start(f32[384,256]{1,0:T(8,128)} %get-tuple-element.30), channel_id=1, source_target_pairs={{0,1},{1,0},{2,3},{3,2},{4,5},{5,4},{6,7},{7,6},{8,9},{9,8},{10,11... | collective-permute-start | bytes 1179656 | tf_op jit(solution)/shard_map/ppermute | solution.py:45
  4.8 8.0 %collective-permute-start.1 = (f32[384,256]{1,0:T(8,128)}, f32[384,256]{1,0:T(8,128)S(1)}, u32[]{:S(2)}, u32[]{:S(2)}) collective-permute-start(f32[384,256]{1,0:T(8,128)} %get-tuple-element.28), channel_id=1, source_target_pairs={{0,1},{1,0},{2,3},{3,2},{4,5},{5,4},{6,7},{7,6},{8,9},{9,8},{10,11... | collective-permute-start | bytes 1179656 | tf_op jit(solution)/shard_map/ppermute | solution.py:45
  5.2 0.9 %copy-start.6 = (bf16[384,256]{1,0:T(8,128)(2,1)S(1)}, bf16[384,256]{1,0:T(8,128)(2,1)}, u32[]{:S(2)}) copy-start(bf16[384,256]{1,0:T(8,128)(2,1)} %get-tuple-element.31.tree_ref) | copy-start | bytes 589828
  7.8 1.0 %copy-start.4 = (f32[384,256]{1,0:T(8,128)S(1)}, f32[384,256]{1,0:T(8,128)}, u32[]{:S(2)}) copy-start(f32[384,256]{1,0:T(8,128)} %get-tuple-element.29.keep_ref) | copy-start | bytes 1179652
  8.9 9.7 %collective-permute-start.4 = (f32[384,128]{1,0:T(8,128)S(1)}, f32[384,128]{1,0:T(8,128)}, u32[]{:S(2)}, u32[]{:S(2)}) collective-permute-start(f32[384,128]{1,0:T(8,128)S(1)} %get-tuple-element.34), channel_id=1, source_target_pairs={{0,2},{1,5},{2,0},{3,7},{4,6},{5,1},{6,4},{7,3},{8,10},{9,13},{10,... | collective-permute-start | bytes 589832 | tf_op jit(solution)/shard_map/ppermute | solution.py:54
  11.5 7.1 %collective-permute-start.5 = (f32[384,128]{1,0:T(8,128)S(1)}, f32[384,128]{1,0:T(8,128)}, u32[]{:S(2)}, u32[]{:S(2)}) collective-permute-start(f32[384,128]{1,0:T(8,128)S(1)} %get-tuple-element.38), channel_id=1, source_target_pairs={{1,7},{3,5},{5,3},{7,1},{9,15},{11,13},{13,11},{15,9},{17,23},{19,... | collective-permute-start | bytes 589832 | tf_op jit(solution)/shard_map/ppermute | solution.py:54
  12.8 23.7 %collective-permute-start.6 = (bf16[384,256]{1,0:T(8,128)(2,1)S(1)}, bf16[384,256]{1,0:T(8,128)(2,1)S(1)}, u32[]{:S(2)}, u32[]{:S(2)}) collective-permute-start(bf16[384,256]{1,0:T(8,128)(2,1)S(1)} %get-tuple-element.44), channel_id=1, source_target_pairs={{1,2},{3,4},{5,6},{7,8},{9,10},{11,12},{13,14},{2,1},{4,3},{6,5},{... | collective-permute-start | bytes 589832 | tf_op jit(solution)/shard_map/ppermute | solution.py:275
  13.9 20.3 %collective-permute-start.8 = (f16[400,512]{1,0:T(8,128)(2,1)S(1)}, f16[400,512]{1,0:T(8,128)(2,1)S(1)}, u32[]{:S(2)}, u32[]{:S(2)}) collective-permute-start(f16[400,512]{1,0:T(8,128)(2,1)S(1)} %convert_element_type.18), channel_id=1, source_target_pairs={{0,4},{1,7},{2,6},{3,5},{4,0},{5,3},{6,2},{7,1},{8,12},{9,15},{10,... | collective-permute-start | bytes 1228808 | tf_op jit(solution)/shard_map/ppermute | solution.py:54
  18.6 11.9 %collective-permute-start.3 = (bf16[384,256]{1,0:T(8,128)(2,1)S(1)}, bf16[384,256]{1,0:T(8,128)(2,1)S(1)}, u32[]{:S(2)}, u32[]{:S(2)}) collective-permute-start(bf16[384,256]{1,0:T(8,128)(2,1)S(1)} %get-tuple-element.36), channel_id=1, source_target_pairs={{0,2},{1,3},{2,0},{3,1},{4,6},{5,7},{6,4},{7,5},{8,10},{9,11},{10,... | collective-permute-start | bytes 589832 | tf_op jit(solution)/shard_map/ppermute | solution.py:45
  23.4 13.2 %copy-start = (bf16[3,2,256,512]{3,2,1,0:T(8,128)(2,1)S(1)}, bf16[3,2,256,512]{3,2,1,0:T(8,128)(2,1)}, u32[]{:S(2)}) copy-start(bf16[3,2,256,512]{3,2,1,0:T(8,128)(2,1)} %basis_ref.5) | copy-start | bytes 4718596
  23.4 10.8 %collective-permute-start.10 = (bf16[384,128]{1,0:T(8,128)(2,1)S(1)}, bf16[384,128]{1,0:T(8,128)(2,1)S(1)}, u32[]{:S(2)}, u32[]{:S(2)}) collective-permute-start(bf16[384,128]{1,0:T(8,128)(2,1)S(1)} %fusion.2), channel_id=1, source_target_pairs={{0,8},{1,13},{2,10},{3,15},{4,12},{5,9},{6,14},{7,11},{8,0},{9,5},... | collective-permute-start | bytes 294920 | tf_op jit(solution)/shard_map/ppermute | solution.py:54
  26.1 10.2 %collective-permute-start.11 = (bf16[384,128]{1,0:T(8,128)(2,1)S(1)}, bf16[384,128]{1,0:T(8,128)(2,1)S(1)}, u32[]{:S(2)}, u32[]{:S(2)}) collective-permute-start(bf16[384,128]{1,0:T(8,128)(2,1)S(1)} %fusion.2), channel_id=1, source_target_pairs={{0,10},{1,15},{2,8},{3,13},{4,14},{5,11},{6,12},{7,9},{8,2},{9,7},... | collective-permute-start | bytes 294920 | tf_op jit(solution)/shard_map/ppermute | solution.py:54
  30.6 6.0 %collective-permute-start.7 = (bf16[768,256]{1,0:T(8,128)(2,1)S(1)}, bf16[768,256]{1,0:T(8,128)(2,1)S(1)}, u32[]{:S(2)}, u32[]{:S(2)}) collective-permute-start(bf16[768,256]{1,0:T(8,128)(2,1)S(1)} %pad_maximum_fusion), channel_id=1, source_target_pairs={{0,1},{1,0},{2,3},{3,2},{4,5},{5,4},{6,7},{7,6},{8,9},{9,8},{10,11... | collective-permute-start | bytes 1179656 | tf_op jit(solution)/shard_map/ppermute | solution.py:45
  34.2 2.8 %collective-permute-start.9 = (f16[400,512]{1,0:T(8,128)(2,1)S(1)}, f16[400,512]{1,0:T(8,128)(2,1)S(1)}, u32[]{:S(2)}, u32[]{:S(2)}) collective-permute-start(f16[400,512]{1,0:T(8,128)(2,1)S(1)} %collective-permute-done.8), channel_id=1, source_target_pairs={{0,1},{1,0},{2,3},{3,2},{4,5},{5,4},{6,7},{7,6},{8,9},{9,8},{10,11... | collective-permute-start | bytes 1228808 | tf_op jit(solution)/shard_map/ppermute | solution.py:45
  36.3 1.5 %collective-permute-start.12 = (bf16[768,128]{1,0:T(8,128)(2,1)S(1)}, bf16[768,128]{1,0:T(8,128)(2,1)S(1)}, u32[]{:S(2)}, u32[]{:S(2)}) collective-permute-start(bf16[768,128]{1,0:T(8,128)(2,1)S(1)} %constant_dynamic-update-slice_fusion.mine_ref), channel_id=1, source_target_pairs={{0,1},{1,0},{2,3},{3,2},{4,5},{5,4},{6,7},{7,6},{8,9},{9,8},{10,11... | collective-permute-start | bytes 589832 | tf_op jit(solution)/shard_map/ppermute | solution.py:45
  37.3 0.9 %copy-start.5 = (bf16[2,192,256]{2,1,0:T(8,128)(2,1)S(1)}, bf16[2,192,256]{2,1,0:T(8,128)(2,1)}, u32[]{:S(2)}) copy-start(bf16[2,192,256]{2,1,0:T(8,128)(2,1)} %forward_ref.1) | copy-start | bytes 589828
  37.3 0.9 %copy-start.7 = (s32[256]{0:T(256)S(1)}, s32[256]{0:T(256)}, u32[]{:S(2)}) copy-start(s32[256]{0:T(256)} %param.13) | copy-start | bytes 3076

commit v3 on v2

--- a/solution.py
+++ b/solution.py
@@ -21,7 +21,7 @@
     return lax.dot_general(a, b, (((1,), (1,)), ((), ())), preferred_element_type=F32)
 
 
-def call(kernel, out_shape, inputs, scratch_shapes=(), smem=(), far=(), vmem=VMEM_BYTES):
+def call(kernel, out_shape, inputs, scratch_shapes=(), smem=(), far=(), vmem=VMEM_BYTES, cost=0):
     def place(i):
         if i in far:
             return pl.BlockSpec(memory_space=pltpu.HBM)
@@ -34,6 +34,7 @@
         out_specs=jax.tree.map(lambda _: pl.BlockSpec(memory_space=pltpu.VMEM), out_shape),
         scratch_shapes=list(scratch_shapes),
         compiler_params=pltpu.CompilerParams(vmem_limit_bytes=vmem),
+        cost_estimate=pl.CostEstimate(flops=0, bytes_accessed=cost, transcendentals=0) if cost else None,
     )
 
 
@@ -59,21 +60,26 @@
 
 
 EXTRA = 16
+FACTORS = 8
 TOP = 14.0
 
 
 def scaled_to(out_ref, values):
-    rows = values.shape[0]
+    rows, width = values.shape
     largest = jnp.max(jnp.max(jnp.abs(values), axis=0, keepdims=True), axis=1, keepdims=True)
-    power = jnp.clip(jnp.ceil(jnp.log2(jnp.maximum(largest, 1e-30))), -100.0, 100.0)
-    out_ref[:rows] = values * jnp.exp2(TOP - power)
-    out_ref[rows:] = jnp.broadcast_to(power, (EXTRA, values.shape[1]))
+    power = jnp.ceil(jnp.log2(jnp.maximum(largest, 1e-30))) - TOP
+    power = jnp.clip(power, -112.0, 112.0)
+    out_ref[:rows] = values * jnp.exp2(-power)
+    row = lax.broadcasted_iota(jnp.int32, (EXTRA, width), 0).astype(F32)
+    out_ref[rows:] = jnp.where(row < FACTORS, jnp.exp2(jnp.floor((power + row) / FACTORS)), 0.0)
 
 
 def unscaled(packed):
-    packed = packed.astype(F32)
     rows = packed.shape[0] - EXTRA
-    return packed[:rows] * jnp.exp2(packed[rows : rows + 1] - TOP)
+    values = packed[:rows].astype(F32)
+    for factor in range(rows, rows + FACTORS):
+        values = values * packed[factor : factor + 1].astype(F32)
+    return values
 
 
 def one_hot_of(order_ref, panels):
@@ -96,65 +102,58 @@
 
 
 def first_kernel(
-    order_hbm,
-    src_hbm,
+    tree_ref,
     basis_hbm,
-    tree_ref,
+    stack_ref,
     send_1_ref,
     keep_1_ref,
     part_2_ref,
     send_3_ref,
     keep_3_ref,
-    order,
-    source,
     basis,
     sems,
 ):
     core, _, low = position()
-    two, rows, panels = source.shape
-    rank = basis.shape[3]
+    levels, _, panels, rank = basis.shape
     half = rank // 2
     copies = [
-        pltpu.make_async_copy(order_hbm, order, sems.at[0]),
-        pltpu.make_async_copy(src_hbm, source, sems.at[1]),
-    ] + [
-        pltpu.make_async_copy(basis_hbm.at[level], basis.at[level], sems.at[2 + level])
-        for level in range(3)
+        pltpu.make_async_copy(basis_hbm.at[level], basis.at[level], sems.at[level])
+        for level in range(levels)
     ]
     for copy in copies:
         copy.start()
-    copies[0].wait()
-    one_hot = one_hot_of(order, panels)
-    copies[1].wait()
-    tree = dot(source[...].reshape(two * rows, panels), one_hot).astype(BF16)
-    tree_ref[...] = tree
-    stack = signed_stack(tree)
+    stack = signed_stack(tree_ref[...])
+    stack_ref[...] = stack
 
     def product(level, start, width):
         columns = basis[level, :, :, pl.ds(start, width)].reshape(2 * panels, width)
         return dot(stack, columns)
 
-    copies[2].wait()
+    copies[0].wait()
     send_1_ref[...] = product(0, pl.multiple_of((low ^ core ^ 1) * half, half), half)
     keep_1_ref[...] = product(0, pl.multiple_of((low ^ core) * half, half), half)
-    copies[3].wait()
+    copies[1].wait()
     part_2_ref[...] = product(1, 0, rank)
-    copies[4].wait()
+    copies[2].wait()
     send_3_ref[...] = product(2, pl.multiple_of((core ^ 1) * half, half), half)
     keep_3_ref[...] = product(2, pl.multiple_of(core * half, half), half)
 
 
-def near_kernel(index_ref, tree_ref, near_ref, core_ref, far_ref, own_ref, sums):
+def near_kernel(index_ref, stack_ref, near_ref, core_ref, far_ref, own_ref, sums):
     core, _, _ = position()
     _, block_count, neighbours, size, _ = near_ref.shape
     sums[...] = jnp.zeros_like(sums)
     base = index_ref[0, 0] - block_count
     for i in range(block_count):
-        stack = signed_stack(tree_ref[:, i * size : (i + 1) * size])
-        for k in range(neighbours):
-            block = near_ref[:, i, k].reshape(2 * size, size)
-            target = jnp.clip(index_ref[i, k] - base, 0, 3 * block_count - 1)
-            sums[target] += dot(stack, block)
+        stack = jnp.concatenate(
+            [stack_ref[:, j * size : (j + 1) * size] for j in (i, block_count + i)], axis=1
+        )
+        for k in range(0, neighbours, 2):
+            pair = jnp.concatenate([near_ref[:, i, k], near_ref[:, i, k + 1]], axis=2)
+            terms = dot(stack, pair.reshape(2 * size, 2 * size))
+            for j in range(2):
+                target = jnp.clip(index_ref[i, k + j] - base, 0, 3 * block_count - 1)
+                sums[target] += terms[:, j * size : (j + 1) * size]
     for j in range(block_count):
         lanes = pl.ds(j * size, size)
         own_ref[:, lanes] = sums[block_count + j]
@@ -162,13 +161,12 @@
         core_ref[:, lanes] = sums[(1 - core) * 2 * block_count + j].astype(BF16)
 
 
-def spread_kernel(keep_ref, got_ref, out_ref, other_ref):
-    core, across, _ = position()
-    width = out_ref.shape[1]
-    out_lanes = pl.ds(pl.multiple_of((across ^ 1 ^ core) * width, width), width)
-    other_lanes = pl.ds(pl.multiple_of((across ^ core) * width, width), width)
-    out_ref[...] = keep_ref[:, out_lanes] + got_ref[:, out_lanes]
-    other_ref[...] = keep_ref[:, other_lanes] + got_ref[:, other_lanes]
+def spread_kernel(keep_ref, got_ref, near_ref, far_ref):
+    _, across, _ = position()
+    width = near_ref.shape[1]
+    for out, place in ((near_ref, across), (far_ref, across ^ 1)):
+        lanes = pl.ds(pl.multiple_of(place * width, width), width)
+        scaled_to(out, keep_ref[:, lanes] + got_ref[:, lanes])
 
 
 def sums_kernel(part_2_ref, got_2_ref, keep_3_ref, got_3_ref, two_ref, three_ref):
@@ -194,31 +192,46 @@
     out_ref[...] = total
 
 
-def second_kernel(base_ref, two_ref, basis_ref, out_ref):
-    out_ref[...] = base_ref[...] + expanded(two_ref[...], basis_ref, 1, 0, two_ref.shape[1])
-
-
-def last_kernel(
-    order_ref, base_ref, mine_ref, got_ref, basis_ref, forward_ref, field_ref, grad_ref, full
-):
-    core, across, low = position()
-    both = base_ref.shape[0]
-    width = mine_ref.shape[1]
-    mine = low ^ core
-    for half, part in ((mine, mine_ref), (mine ^ 1, got_ref)):
-        full[:, pl.ds(pl.multiple_of((2 * half + across) * width, width), width)] = part[:both]
-        full[:, pl.ds(pl.multiple_of((2 * half + (across ^ 1)) * width, width), width)] = part[both:]
-    total = base_ref[...] + expanded(full[...], basis_ref, 0, 0, 4 * width)
-    two, rows, panels = field_ref.shape
+def prepare_kernel(order_ref, basis_ref, forward_ref, moved_ref, ahead_ref, hot_ref):
+    panels = hot_ref.shape[0]
     one_hot = one_hot_of(order_ref, panels)
+    hot_ref[...] = one_hot
+    for part in range(2):
+        moved_ref[0, part] = dot(one_hot, basis_ref[0, part]).astype(BF16)
+    ahead_ref[...] = forward_ref[...].reshape(ahead_ref.shape)
+
+
+def second_kernel(hot_ref, base_ref, two_ref, basis_ref, ahead_ref, out_ref, grad_ref):
+    total = base_ref[...] + expanded(two_ref[...], basis_ref, 1, 0, two_ref.shape[1])
+    one_hot = hot_ref[...]
     field = jnp.zeros_like(total)
     for _ in range(3):
         piece = total.astype(BF16)
         total = total - piece.astype(F32)
         field += dot_t(piece, one_hot)
-    field_ref[...] = field.reshape(two, rows, panels)
-    forward = forward_ref[...].reshape(two * rows, panels).astype(F32)
-    grad_ref[...] = -jnp.sum(field * forward, axis=0, keepdims=True) / math.sqrt(rows)
+    out_ref[...] = field
+    grad_ref[...] = jnp.sum(field * ahead_ref[...].astype(F32), axis=0, keepdims=True)
+
+
+def last_kernel(
+    base_ref, first_grad_ref, own_ref, mine_ref, got_ref, basis_ref, ahead_ref, field_ref, grad_ref, full
+):
+    core, across, low = position()
+    both, width = own_ref.shape
+
+    def put(flip, value):
+        place = (2 * low + across) ^ flip
+        full[:, pl.ds(pl.multiple_of(place * width, width), width)] = value
+
+    put(0, own_ref[...])
+    put(1, jnp.where(core == 0, mine_ref[:both], got_ref[:both]))
+    put(2, jnp.where(core == 0, got_ref[:both], mine_ref[:both]))
+    put(3, jnp.where(core == 0, got_ref[both:], mine_ref[both:]))
+    two, rows, panels = field_ref.shape
+    added = expanded(full[...], basis_ref, 0, 0, 4 * width)
+    field_ref[...] = (base_ref[...] + added).reshape(two, rows, panels)
+    total = first_grad_ref[...] + jnp.sum(added * ahead_ref[...].astype(F32), axis=0, keepdims=True)
+    grad_ref[...] = -total / math.sqrt(rows)
 
 
 def fast_body(sources, forward_field, row_bases, col_bases, near_blocks, near_index, cluster_order):
@@ -227,25 +240,18 @@
     both = two * rows
     half, quarter = rank // 2, rank // 4
     order = cluster_order.reshape(1, panels)
-    core = lax.axis_index(TREE) & 1
     halves = array((both, half), F32)
-
-    tree, send_1, keep_1, part_2, send_3, keep_3 = call(
+    one_hot = (lax.rem(cluster_order, panels)[None, :] == jnp.arange(panels)[:, None]).astype(BF16)
+    tree = dot(sources.reshape(both, panels), one_hot).astype(BF16)
+    stack, send_1, keep_1, part_2, send_3, keep_3 = call(
         first_kernel,
-        (array((both, panels), BF16), halves, halves, array((both, rank), F32), halves, halves),
-        3,
-        scratch_shapes=[
-            pltpu.VMEM((1, panels), jnp.int32),
-            pltpu.VMEM((two, rows, panels), BF16),
-            pltpu.VMEM((3, 2, panels, rank), BF16),
-            pltpu.SemaphoreType.DMA((5,)),
-        ],
-        far=(0, 1, 2),
-        vmem=56 * 1024 * 1024,
-    )(order, sources, row_bases)
+        (array((both, 2 * panels), BF16), halves, halves, array((both, rank), F32), halves, halves),
+        2,
+        scratch_shapes=[pltpu.VMEM((3, 2, panels, rank), BF16), pltpu.SemaphoreType.DMA((3,))],
+        far=(1,),
+        vmem=50 * 1024 * 1024,
+    )(tree, row_bases)
     got_1 = swapped(send_1, 1)
-    got_3 = swapped(send_3, 1)
-    got_2 = swapped(part_2, 1)
 
     blocks = near_blocks.shape[1]
     size = near_blocks.shape[3]
@@ -255,45 +261,56 @@
         3,
         scratch_shapes=[pltpu.VMEM((3 * blocks, both, size), F32)],
         smem=(0,),
-    )(near_index, tree, near_blocks)
-
-    got_1, own = lax.optimization_barrier((got_1, own))
-    to_a, to_b = call(
-        spread_kernel, (array((both, quarter), F32), array((both, quarter), F32)), 2
-    )(keep_1, got_1)
-    got_a = by_core(to_a, 2, 4)
-    got_b = by_core(to_b, None, 6)
+    )(near_index, stack, near_blocks)
+
+    packed = array((both + EXTRA, quarter), F32)
+    got_1, own, send_3, part_2 = lax.optimization_barrier((got_1, own, send_3, part_2))
+    got_3 = swapped(send_3, 1)
+    got_2 = swapped(part_2, 1)
+    to_f, to_g = call(spread_kernel, (packed, packed), 2)(keep_1, got_1)
+    got_f = by_core(to_f.astype(jnp.float16), 8, 12)
+    got_g = by_core(to_g.astype(jnp.float16), 10, 14)
 
     two_sent, three_sent = call(
         sums_kernel, (array((both + EXTRA, rank), F32), array((both, half), BF16)), 4
-    )(part_2, got_2, keep_3, after(got_3, to_a))
+    )(part_2, got_2, keep_3, after(got_3, to_f))
     mine_3 = swapped(three_sent, 2)
     two_sent = two_sent.astype(jnp.float16)
     got_cd = by_core(two_sent, 4, 6)
     peers = lax.axis_size(TREE)
     joints = [(i, i + 1) for i in range(1, peers - 1, 2)]
-    far_halo = lax.ppermute(after(to_far, to_a), TREE, joints + [(b, a) for a, b in joints])
-
-    got_a, got_b, _ = lax.optimization_barrier((got_a, got_b, two_sent))
-    middle = got_a + jnp.where(core == 0, to_b, got_b)
-    parts = lax.all_gather(middle, "rhs", axis=0)
+    far_halo = lax.ppermute(to_far, TREE, joints + [(b, a) for a, b in joints])
+
+    got_f, got_g, _ = lax.optimization_barrier((got_f, got_g, two_sent))
+    parts = lax.all_gather(unscaled(got_f) + unscaled(got_g), "rhs", axis=0)
     quarter_sum = (parts[0] + parts[1]).astype(BF16)
-    got_f = by_core(quarter_sum, 8, 12)
-    got_g = by_core(quarter_sum, 10, 14)
-
-    mine_3, own, _ = lax.optimization_barrier((mine_3, own, quarter_sum))
+    got_a = by_core(quarter_sum, 2, 4)
+    got_b = by_core(quarter_sum, None, 6)
+
+    moved, ahead, hot = call(
+        prepare_kernel,
+        (
+            array((1, 2, panels, rank), BF16),
+            array((both, panels), BF16),
+            array((panels, panels), BF16),
+        ),
+        3,
+    )(after(order, quarter_sum), col_bases, forward_field)
+    mine_3, own, _, _ = lax.optimization_barrier((mine_3, own, quarter_sum, moved))
     pair_3 = swapped(jnp.concatenate([mine_3, to_core], axis=0), 1)
     base = call(halo_kernel, array((both, panels), F32), 5)(own, far_halo, mine_3, pair_3, col_bases)
     got_cd = after(got_cd, quarter_sum)
     all_2 = (unscaled(got_cd) + unscaled(swapped(got_cd, 1))).astype(BF16)
-    base = call(second_kernel, array((both, panels), F32), 3)(base, all_2, col_bases)
-    mine_1 = jnp.concatenate([got_f, got_g], axis=0)
+    base, first_grad = call(
+        second_kernel, (array((both, panels), F32), array((1, panels), F32)), 5
+    )(hot, base, all_2, col_bases, ahead)
+    mine_1 = jnp.concatenate([got_a, got_b], axis=0)
     field, grad = call(
         last_kernel,
         (array((two, rows, panels), F32), array((1, panels), F32)),
-        6,
+        7,
         scratch_shapes=[pltpu.VMEM((both, rank), BF16)],
-    )(order, base, mine_1, swapped(mine_1, 1), col_bases, forward_field)
+    )(base, first_grad, quarter_sum, mine_1, swapped(mine_1, 1), moved, ahead)
     return field, grad.reshape(panels)
 
 

time: 40.2 us -> 36.7 us (0.913)
  starting transfers between devices: 17 us -> 14 us
  waiting for transfers between devices: 8.12 us -> 10.5 us
  local copies, waits for them, and re-layouts: 2.37 us -> 0.17 us
  Pallas kernels: 7.95 us -> 6.76 us
    ppermute x7, starting transfers between devices: 4.59 us -> 2.35 us  [swapped(): lax.ppermute(x, TREE, [(i, i ^ distance) for i in range(lax.axis_size(TRE...]
    unnamed x19 -> x13, local copies, waits for them, and re-layouts: 2.36 us -> 0.16 us
    ppermute x5, waiting for transfers between devices: 3.97 us -> 5.62 us  [by_core(): return lax.ppermute(x, TREE, pairs)]
    add x1, other arithmetic: 0.96 us -> 0.05 us  [fast_body(): parts = lax.all_gather(unscaled(got_f) + unscaled(got_g), 'rhs', axis=0)]
    rem x0 -> x1, other arithmetic: none -> 0.78 us  [fast_body(): lax.rem(cluster_order, panels)[None, :] == jnp.arange(panels)[:, None]]
    ppermute x7, waiting for transfers between devices: 4.15 us -> 4.88 us  [swapped(): lax.ppermute(x, TREE, [(i, i ^ distance) for i in range(lax.axis_size(TRE...]
    ppermute x5, starting transfers between devices: 11.7 us -> 11 us  [by_core(): return lax.ppermute(x, TREE, pairs)]
    pallas_call x1, Pallas kernels: 1.66 us -> 1.2 us  [fast_body(): call(last_kernel, (array((two, rows, panels), F32), array((1, panels), F3...]
  transfers between devices with their start and end apart: 13 -> 13, of which waited for: 4 -> 5; matrix products, arithmetic and copies ran while one was open for 4% -> 2% of each run, Pallas kernels for 7% -> 9%
where the time goes in v3:
time: 36.7 us; the launch traced here: 36.1 us
  starting transfers between devices  14 us (38%)
  waiting for transfers between devices  10.5 us (29%)
  Pallas kernels  6.76 us (18%)
  blocking collectives  2.09 us (6%)
  other arithmetic  1.45 us (4%)
  between operations  0.87 us (2%)
    ppermute x5, starting transfers between devices, by_core(): return lax.ppermute(x, TREE, pairs)  11 us
    ppermute x5, waiting for transfers between devices, by_core(): return lax.ppermute(x, TREE, pairs)  5.62 us
    ppermute x7, waiting for transfers between devices, swapped(): lax.ppermute(x, TREE, [(i, i ^ distance) for i in range(lax.axis_size(TRE...  4.88 us
    ppermute x7, starting transfers between devices, swapped(): lax.ppermute(x, TREE, [(i, i ^ distance) for i in range(lax.axis_size(TRE...  2.35 us
    pallas_call x1, Pallas kernels, fast_body(): call(first_kernel, (array((both, 2 * panels), BF16), halves, halves, arra...  2.19 us
    all_gather x1, blocking collectives, fast_body(): parts = lax.all_gather(unscaled(got_f) + unscaled(got_g), 'rhs', axis=0)  2.09 us
    pallas_call x1, Pallas kernels, fast_body(): call(near_kernel, (array((both, panels), BF16), array((both, panels), BF1...  1.32 us
    pallas_call x1, Pallas kernels, fast_body(): call(last_kernel, (array((two, rows, panels), F32), array((1, panels), F3...  1.2 us
  transfers between devices with their start and end apart: 13, of which 5 were waited for; matrix products, arithmetic and copies ran while one was open for 2% of the time, Pallas kernels for 9%

profile of v3, /device:TPU:0, one launch (start us, length us, event | category | flops | bytes accessed | tf_op | source)
XLA Modules:
  0.0 36.1 jit_solution(4795348443372472808)
XLA Ops:
  0.6 0.0 copy-start
  0.6 0.0 copy-start.5
  0.7 0.0 copy-start.2
  0.7 0.8 %compare_select_fusion = s32[256]{0:T(256)S(1)} fusion(s32[256]{0:T(256)} %param.13), kind=kLoop, calls=%fused_computation.11 | loop fusion | flops 1536 | bytes 2048 | tf_op jit(solution)/shard_map/rem | solution.py:244
  1.4 0.1 copy-done
  1.6 0.2 fusion.tree_ref
  1.8 2.2 %shard_map.86 = (bf16[384,512]{1,0:T(8,128)(2,1)S(1)}, f32[384,256]{1,0:T(8,128)S(1)}, f32[384,256]{1,0:T(8,128)S(1)}, f32[384,512]{1,0:T(8,128)S(1)}, f32[384,256]{1,0:T(8,128)S(1)}, /*index=5*/f32[384,256]{1,0:T(8,128)S(1)}) custom-call(bf16[384,256]{1,0:T(8,128)(2,1)S(1)} %fusion.tree_ref, bf16[3,2,256,512]{3,2,1,0:T(8,128)(2,1)} %basis_hbm.1), custom_call_target="tpu_custom_call" | custom-call | tf_op jit(solution)/shard_map/pallas_call | solution.py:246
  4.0 0.5 %collective-permute-start = (f32[384,256]{1,0:T(8,128)S(1)}, f32[384,256]{1,0:T(8,128)S(1)}, u32[]{:S(2)}, u32[]{:S(2)}) collective-permute-start(f32[384,256]{1,0:T(8,128)S(1)} %get-tuple-element.34), channel_id=1, source_target_pairs={{0,1},{1,0},{2,3},{3,2},{4,5},{5,4},{6,7},{7,6},{8,9},{9,8},{10,11... | collective-permute-start | bytes 1179656 | tf_op jit(solution)/shard_map/ppermute | solution.py:46
  4.5 0.0 copy-done.5
  4.5 1.3 %shard_map.87 = (bf16[384,256]{1,0:T(8,128)(2,1)S(1)}, bf16[384,256]{1,0:T(8,128)(2,1)S(1)}, f32[384,256]{1,0:T(8,128)S(1)}) custom-call(s32[2,8]{1,0:T(2,128)S(1)} %copy-done.5, bf16[384,512]{1,0:T(8,128)(2,1)S(1)} %get-tuple-element.35.stack_ref, bf16[2,2,8,128,128]{4,3,2,1,0:T(8,128)(2,1)S(1)} %copy-done.2), custom_call_target="tpu_custom_call" | custom-call | tf_op jit(solution)/shard_map/pallas_call | solution.py:258
  5.8 0.0 collective-permute-done.got_ref
  5.9 0.4 %collective-permute-start.3 = (f32[384,512]{1,0:T(8,128)S(1)}, f32[384,512]{1,0:T(8,128)S(1)}, u32[]{:S(2)}, u32[]{:S(2)}) collective-permute-start(f32[384,512]{1,0:T(8,128)S(1)} %get-tuple-element.42.part_2_ref), channel_id=1, source_target_pairs={{0,1},{1,0},{2,3},{3,2},{4,5},{5,4},{6,7},{7,6},{8,9},{9,8},{10,11... | collective-permute-start | bytes 2359304 | tf_op jit(solution)/shard_map/ppermute | solution.py:46
  6.2 0.2 collective-permute-start.4
  6.4 0.2 shard_map.88
  6.7 4.0 %collective-permute-start.1 = (f16[400,128]{1,0:T(8,128)(2,1)S(1)}, f16[400,128]{1,0:T(8,128)(2,1)S(1)}, u32[]{:S(2)}, u32[]{:S(2)}) collective-permute-start(f16[400,128]{1,0:T(8,128)(2,1)S(1)} %convert_element_type.26), channel_id=1, source_target_pairs={{0,8},{1,13},{2,10},{3,15},{4,12},{5,9},{6,14},{7,11},{8,0},{9,5},... | collective-permute-start | bytes 307208 | tf_op jit(solution)/shard_map/ppermute | solution.py:55
  10.6 1.3 %collective-permute-start.2 = (f16[400,128]{1,0:T(8,128)(2,1)S(1)}, f16[400,128]{1,0:T(8,128)(2,1)S(1)}, u32[]{:S(2)}, u32[]{:S(2)}) collective-permute-start(f16[400,128]{1,0:T(8,128)(2,1)S(1)} %convert_element_type.27), channel_id=1, source_target_pairs={{0,10},{1,15},{2,8},{3,13},{4,14},{5,11},{6,12},{7,9},{8,2},{9,7},... | collective-permute-start | bytes 307208 | tf_op jit(solution)/shard_map/ppermute | solution.py:55
  11.9 0.7 %collective-permute-start.6 = (bf16[384,256]{1,0:T(8,128)(2,1)S(1)}, bf16[384,256]{1,0:T(8,128)(2,1)S(1)}, u32[]{:S(2)}, u32[]{:S(2)}) collective-permute-start(bf16[384,256]{1,0:T(8,128)(2,1)S(1)} %get-tuple-element.55), channel_id=1, source_target_pairs={{1,2},{3,4},{5,6},{7,8},{9,10},{11,12},{13,14},{2,1},{4,3},{6,5},{... | collective-permute-start | bytes 589832 | tf_op jit(solution)/shard_map/ppermute | solution.py:282
  12.5 0.0 collective-permute-done.4.got_3_ref
  12.6 0.0 collective-permute-done.3.got_2_ref
  12.6 0.3 shard_map.89
  12.8 0.0 copy-start.1
  12.9 0.0 copy-start.3
  12.9 0.0 copy-start.4
  12.9 0.1 convert_element_type.28
  13.0 3.6 %collective-permute-start.8 = (f16[400,512]{1,0:T(8,128)(2,1)S(1)}, f16[400,512]{1,0:T(8,128)(2,1)S(1)}, u32[]{:S(2)}, u32[]{:S(2)}) collective-permute-start(f16[400,512]{1,0:T(8,128)(2,1)S(1)} %convert_element_type.28), channel_id=1, source_target_pairs={{0,4},{1,7},{2,6},{3,5},{4,0},{5,3},{6,2},{7,1},{8,12},{9,15},{10,... | collective-permute-start | bytes 1228808 | tf_op jit(solution)/shard_map/ppermute | solution.py:55
  16.5 0.0 collective-permute-done.1
  16.5 5.2 %collective-permute-done.2 = f16[400,128]{1,0:T(8,128)(2,1)S(1)} collective-permute-done((f16[400,128]{1,0:T(8,128)(2,1)S(1)}, f16[400,128]{1,0:T(8,128)(2,1)S(1)}, u32[]{:S(2)}, u32[]{:S(2)}) %collective-permute-start.2) | collective-permute-done | bytes 102432 | tf_op jit(solution)/shard_map/ppermute | solution.py:55
  21.7 0.5 %collective-permute-start.5 = (bf16[384,256]{1,0:T(8,128)(2,1)S(1)}, bf16[384,256]{1,0:T(8,128)(2,1)S(1)}, u32[]{:S(2)}, u32[]{:S(2)}) collective-permute-start(bf16[384,256]{1,0:T(8,128)(2,1)S(1)} %get-tuple-element.51), channel_id=1, source_target_pairs={{0,2},{1,3},{2,0},{3,1},{4,6},{5,7},{6,4},{7,5},{8,10},{9,11},{10,... | collective-permute-start | bytes 589832 | tf_op jit(solution)/shard_map/ppermute | solution.py:46
  22.2 0.1 multiply_add_fusion
  22.3 2.1 %all-gather = f32[768,128]{1,0:T(8,128)S(1)} all-gather(f32[384,128]{1,0:T(8,128)S(1)} %multiply_add_fusion), channel_id=2, replica_groups=mesh['groups'=2,'leaf'=8,'rhs'=2] {'rhs'}, dimensions={0}, use_global_device_ids=true | all-gather | bytes 589824 | tf_op jit(solution)/shard_map/all_gather | solution.py:285
  24.4 0.7 %collective-permute-start.11 = (bf16[384,128]{1,0:T(8,128)(2,1)S(1)}, bf16[384,128]{1,0:T(8,128)(2,1)S(1)}, u32[]{:S(2)}, u32[]{:S(2)}) collective-permute-start(bf16[384,128]{1,0:T(8,128)(2,1)S(1)} %fusion.1.own_ref), channel_id=1, source_target_pairs={{1,7},{3,5},{5,3},{7,1},{9,15},{11,13},{13,11},{15,9},{17,23},{19,... | collective-permute-start | bytes 294920 | tf_op jit(solution)/shard_map/ppermute | solution.py:55
  25.1 1.6 %collective-permute-start.10 = (bf16[384,128]{1,0:T(8,128)(2,1)S(1)}, bf16[384,128]{1,0:T(8,128)(2,1)S(1)}, u32[]{:S(2)}, u32[]{:S(2)}) collective-permute-start(bf16[384,128]{1,0:T(8,128)(2,1)S(1)} %fusion.1.own_ref), channel_id=1, source_target_pairs={{0,2},{1,5},{2,0},{3,7},{4,6},{5,1},{6,4},{7,3},{8,10},{9,13},{10,... | collective-permute-start | bytes 294920 | tf_op jit(solution)/shard_map/ppermute | solution.py:55
  26.7 0.3 shard_map.90
  27.0 4.2 %collective-permute-done.5.three_ref = bf16[384,256]{1,0:T(8,128)(2,1)S(1)} collective-permute-done((bf16[384,256]{1,0:T(8,128)(2,1)S(1)}, bf16[384,256]{1,0:T(8,128)(2,1)S(1)}, u32[]{:S(2)}, u32[]{:S(2)}) %collective-permute-start.5) | collective-permute-done | bytes 196640 | tf_op jit(solution)/shard_map/ppermute | solution.py:46
  31.2 0.1 collective-permute-start.7
  31.3 0.0 collective-permute-done.8
  31.3 0.5 %collective-permute-start.9 = (f16[400,512]{1,0:T(8,128)(2,1)S(1)}, f16[400,512]{1,0:T(8,128)(2,1)S(1)}, u32[]{:S(2)}, u32[]{:S(2)}) collective-permute-start(f16[400,512]{1,0:T(8,128)(2,1)S(1)} %collective-permute-done.8), channel_id=1, source_target_pairs={{0,1},{1,0},{2,3},{3,2},{4,5},{5,4},{6,7},{7,6},{8,9},{9,8},{10,11... | collective-permute-start | bytes 1228808 | tf_op jit(solution)/shard_map/ppermute | solution.py:46
  31.8 0.4 %collective-permute-done.10 = bf16[384,128]{1,0:T(8,128)(2,1)S(1)} collective-permute-done((bf16[384,128]{1,0:T(8,128)(2,1)S(1)}, bf16[384,128]{1,0:T(8,128)(2,1)S(1)}, u32[]{:S(2)}, u32[]{:S(2)}) %collective-permute-start.10) | collective-permute-done | bytes 98336 | tf_op jit(solution)/shard_map/ppermute | solution.py:55
  32.2 0.0 collective-permute-done.11
  32.2 0.2 collective-permute-start.12
  32.4 0.0 collective-permute-done.6.far_ref
  32.5 0.5 %collective-permute-done.7.pair_ref = bf16[768,256]{1,0:T(8,128)(2,1)S(1)} collective-permute-done((bf16[768,256]{1,0:T(8,128)(2,1)S(1)}, bf16[768,256]{1,0:T(8,128)(2,1)S(1)}, u32[]{:S(2)}, u32[]{:S(2)}) %collective-permute-start.7) | collective-permute-done | bytes 393248 | tf_op jit(solution)/shard_map/ppermute | solution.py:46
  33.0 0.4 %shard_map.91.base_ref = f32[384,256]{1,0:T(8,128)S(1)} custom-call(f32[384,256]{1,0:T(8,128)S(1)} %get-tuple-element.54.own_ref, bf16[384,256]{1,0:T(8,128)(2,1)S(1)} %collective-permute-done.6.far_ref, bf16[384,256]{1,0:T(8,128)(2,1)S(1)} %collective-permute-done.5.three_ref, bf16[768,256]{1,0:T(8,128)(2,1)S(1)} %collective-permute-done.7.pair_ref, ...), custom_call_target="tpu_custom_call" | custom-call | tf_op jit(solution)/shard_map/pallas_call | solution.py:301
  33.4 0.2 collective-permute-done.9
  33.6 0.4 %add_convert_fusion.two_ref = bf16[384,512]{1,0:T(8,128)(2,1)S(1)} fusion(f16[400,512]{1,0:T(8,128)(2,1)S(1)} %collective-permute-done.9, f32[512]{0:T(512)S(1)} %bitcast.81, f32[512]{0:T(512)S(1)} %bitcast.82, f32[512]{0:T(512)S(1)} %bitcast.83, f32[512]{0:T(512)S(1)} %bitcast.84, f32[512]{0:T(512)S(1)} %bitcast.85, f32[512]{0:T(512)S(1)} %bitcast.86, ...), kind=kLoop, calls=%fused_computation.2 | loop fusion | flops 3932160 | bytes 1212416 | tf_op jit(solution)/shard_map/convert_element_type | solution.py:303
  34.0 0.9 %shard_map.92 = (f32[384,256]{1,0:T(8,128)S(1)}, f32[1,256]{1,0:T(1,128)S(1)}) custom-call(bf16[256,256]{1,0:T(8,128)(2,1)S(1)} %get-tuple-element.50.hot_ref, f32[384,256]{1,0:T(8,128)S(1)} %shard_map.91.base_ref, bf16[384,512]{1,0:T(8,128)(2,1)S(1)} %add_convert_fusion.two_ref, bf16[3,2,256,512]{3,2,1,0:T(8,128)(2,1)S(1)} %copy-done.1, ...), custom_call_target="tpu_custom_call" | custom-call | tf_op jit(solution)/shard_map/pallas_call | solution.py:304
  34.9 0.0 collective-permute-done.12.got_ref
  34.9 1.2 %shard_map.93 = (f32[2,192,256]{2,1,0:T(8,128)}, f32[1,256]{1,0:T(1,128)}) custom-call(f32[384,256]{1,0:T(8,128)S(1)} %get-tuple-element.60.base_ref, f32[1,256]{1,0:T(1,128)S(1)} %get-tuple-element.61.first_grad_ref, bf16[384,128]{1,0:T(8,128)(2,1)S(1)} %fusion.1.own_ref, bf16[768,128]{1,0:T(8,128)(2,1)S(1)} %constant_dynamic-update-slice_fusion.mine_ref, ...), custom_call_target="tpu_custom_call" | custom-call | tf_op jit(solution)/shard_map/pallas_call | solution.py:308
  (13 shorter events, 0.1 us)
Async XLA Ops:
  0.6 0.9 %copy-start = (bf16[2,192,256]{2,1,0:T(8,128)(2,1)S(1)}, bf16[2,192,256]{2,1,0:T(8,128)(2,1)}, u32[]{:S(2)}) copy-start(bf16[2,192,256]{2,1,0:T(8,128)(2,1)} %param.7) | copy-start | bytes 589828
  0.6 3.9 %copy-start.5 = (s32[2,8]{1,0:T(2,128)S(1)}, s32[2,8]{1,0:T(2,128)}, u32[]{:S(2)}) copy-start(s32[2,8]{1,0:T(2,128)} %index_ref.1) | copy-start | bytes 196
  0.7 3.9 %copy-start.2 = (bf16[2,2,8,128,128]{4,3,2,1,0:T(8,128)(2,1)S(1)}, bf16[2,2,8,128,128]{4,3,2,1,0:T(8,128)(2,1)}, u32[]{:S(2)}) copy-start(bf16[2,2,8,128,128]{4,3,2,1,0:T(8,128)(2,1)} %near_ref.1) | copy-start | bytes 3145732
  4.0 1.9 %collective-permute-start = (f32[384,256]{1,0:T(8,128)S(1)}, f32[384,256]{1,0:T(8,128)S(1)}, u32[]{:S(2)}, u32[]{:S(2)}) collective-permute-start(f32[384,256]{1,0:T(8,128)S(1)} %get-tuple-element.34), channel_id=1, source_target_pairs={{0,1},{1,0},{2,3},{3,2},{4,5},{5,4},{6,7},{7,6},{8,9},{9,8},{10,11... | collective-permute-start | bytes 1179656 | tf_op jit(solution)/shard_map/ppermute | solution.py:46
  5.9 6.7 %collective-permute-start.3 = (f32[384,512]{1,0:T(8,128)S(1)}, f32[384,512]{1,0:T(8,128)S(1)}, u32[]{:S(2)}, u32[]{:S(2)}) collective-permute-start(f32[384,512]{1,0:T(8,128)S(1)} %get-tuple-element.42.part_2_ref), channel_id=1, source_target_pairs={{0,1},{1,0},{2,3},{3,2},{4,5},{5,4},{6,7},{7,6},{8,9},{9,8},{10,11... | collective-permute-start | bytes 2359304 | tf_op jit(solution)/shard_map/ppermute | solution.py:46
  6.2 6.3 %collective-permute-start.4 = (f32[384,256]{1,0:T(8,128)S(1)}, f32[384,256]{1,0:T(8,128)S(1)}, u32[]{:S(2)}, u32[]{:S(2)}) collective-permute-start(f32[384,256]{1,0:T(8,128)S(1)} %get-tuple-element.44), channel_id=1, source_target_pairs={{0,1},{1,0},{2,3},{3,2},{4,5},{5,4},{6,7},{7,6},{8,9},{9,8},{10,11... | collective-permute-start | bytes 1179656 | tf_op jit(solution)/shard_map/ppermute | solution.py:46
  6.7 9.9 %collective-permute-start.1 = (f16[400,128]{1,0:T(8,128)(2,1)S(1)}, f16[400,128]{1,0:T(8,128)(2,1)S(1)}, u32[]{:S(2)}, u32[]{:S(2)}) collective-permute-start(f16[400,128]{1,0:T(8,128)(2,1)S(1)} %convert_element_type.26), channel_id=1, source_target_pairs={{0,8},{1,13},{2,10},{3,15},{4,12},{5,9},{6,14},{7,11},{8,0},{9,5},... | collective-permute-start | bytes 307208 | tf_op jit(solution)/shard_map/ppermute | solution.py:55
  10.6 11.1 %collective-permute-start.2 = (f16[400,128]{1,0:T(8,128)(2,1)S(1)}, f16[400,128]{1,0:T(8,128)(2,1)S(1)}, u32[]{:S(2)}, u32[]{:S(2)}) collective-permute-start(f16[400,128]{1,0:T(8,128)(2,1)S(1)} %convert_element_type.27), channel_id=1, source_target_pairs={{0,10},{1,15},{2,8},{3,13},{4,14},{5,11},{6,12},{7,9},{8,2},{9,7},... | collective-permute-start | bytes 307208 | tf_op jit(solution)/shard_map/ppermute | solution.py:55
  11.9 20.6 %collective-permute-start.6 = (bf16[384,256]{1,0:T(8,128)(2,1)S(1)}, bf16[384,256]{1,0:T(8,128)(2,1)S(1)}, u32[]{:S(2)}, u32[]{:S(2)}) collective-permute-start(bf16[384,256]{1,0:T(8,128)(2,1)S(1)} %get-tuple-element.55), channel_id=1, source_target_pairs={{1,2},{3,4},{5,6},{7,8},{9,10},{11,12},{13,14},{2,1},{4,3},{6,5},{... | collective-permute-start | bytes 589832 | tf_op jit(solution)/shard_map/ppermute | solution.py:282
  12.8 13.8 %copy-start.1 = (bf16[3,2,256,512]{3,2,1,0:T(8,128)(2,1)S(1)}, bf16[3,2,256,512]{3,2,1,0:T(8,128)(2,1)}, u32[]{:S(2)}) copy-start(bf16[3,2,256,512]{3,2,1,0:T(8,128)(2,1)} %basis_ref.5) | copy-start | bytes 4718596
  12.9 13.8 %copy-start.3 = (bf16[2,192,256]{2,1,0:T(8,128)(2,1)S(1)}, bf16[2,192,256]{2,1,0:T(8,128)(2,1)}, u32[]{:S(2)}) copy-start(bf16[2,192,256]{2,1,0:T(8,128)(2,1)} %forward_ref.1) | copy-start | bytes 589828
  12.9 13.8 %copy-start.4 = (s32[256]{0:T(256)S(1)}, s32[256]{0:T(256)}, u32[]{:S(2)}) copy-start(s32[256]{0:T(256)} %param.13) | copy-start | bytes 3076
  13.0 18.3 %collective-permute-start.8 = (f16[400,512]{1,0:T(8,128)(2,1)S(1)}, f16[400,512]{1,0:T(8,128)(2,1)S(1)}, u32[]{:S(2)}, u32[]{:S(2)}) collective-permute-start(f16[400,512]{1,0:T(8,128)(2,1)S(1)} %convert_element_type.28), channel_id=1, source_target_pairs={{0,4},{1,7},{2,6},{3,5},{4,0},{5,3},{6,2},{7,1},{8,12},{9,15},{10,... | collective-permute-start | bytes 1228808 | tf_op jit(solution)/shard_map/ppermute | solution.py:55
  21.7 9.5 %collective-permute-start.5 = (bf16[384,256]{1,0:T(8,128)(2,1)S(1)}, bf16[384,256]{1,0:T(8,128)(2,1)S(1)}, u32[]{:S(2)}, u32[]{:S(2)}) collective-permute-start(bf16[384,256]{1,0:T(8,128)(2,1)S(1)} %get-tuple-element.51), channel_id=1, source_target_pairs={{0,2},{1,3},{2,0},{3,1},{4,6},{5,7},{6,4},{7,5},{8,10},{9,11},{10,... | collective-permute-start | bytes 589832 | tf_op jit(solution)/shard_map/ppermute | solution.py:46
  24.4 7.8 %collective-permute-start.11 = (bf16[384,128]{1,0:T(8,128)(2,1)S(1)}, bf16[384,128]{1,0:T(8,128)(2,1)S(1)}, u32[]{:S(2)}, u32[]{:S(2)}) collective-permute-start(bf16[384,128]{1,0:T(8,128)(2,1)S(1)} %fusion.1.own_ref), channel_id=1, source_target_pairs={{1,7},{3,5},{5,3},{7,1},{9,15},{11,13},{13,11},{15,9},{17,23},{19,... | collective-permute-start | bytes 294920 | tf_op jit(solution)/shard_map/ppermute | solution.py:55
  25.1 7.1 %collective-permute-start.10 = (bf16[384,128]{1,0:T(8,128)(2,1)S(1)}, bf16[384,128]{1,0:T(8,128)(2,1)S(1)}, u32[]{:S(2)}, u32[]{:S(2)}) collective-permute-start(bf16[384,128]{1,0:T(8,128)(2,1)S(1)} %fusion.1.own_ref), channel_id=1, source_target_pairs={{0,2},{1,5},{2,0},{3,7},{4,6},{5,1},{6,4},{7,3},{8,10},{9,13},{10,... | collective-permute-start | bytes 294920 | tf_op jit(solution)/shard_map/ppermute | solution.py:55
  31.2 1.8 %collective-permute-start.7 = (bf16[768,256]{1,0:T(8,128)(2,1)S(1)}, bf16[768,256]{1,0:T(8,128)(2,1)S(1)}, u32[]{:S(2)}, u32[]{:S(2)}) collective-permute-start(bf16[768,256]{1,0:T(8,128)(2,1)S(1)} %pad_maximum_fusion), channel_id=1, source_target_pairs={{0,1},{1,0},{2,3},{3,2},{4,5},{5,4},{6,7},{7,6},{8,9},{9,8},{10,11... | collective-permute-start | bytes 1179656 | tf_op jit(solution)/shard_map/ppermute | solution.py:46
  31.3 2.3 %collective-permute-start.9 = (f16[400,512]{1,0:T(8,128)(2,1)S(1)}, f16[400,512]{1,0:T(8,128)(2,1)S(1)}, u32[]{:S(2)}, u32[]{:S(2)}) collective-permute-start(f16[400,512]{1,0:T(8,128)(2,1)S(1)} %collective-permute-done.8), channel_id=1, source_target_pairs={{0,1},{1,0},{2,3},{3,2},{4,5},{5,4},{6,7},{7,6},{8,9},{9,8},{10,11... | collective-permute-start | bytes 1228808 | tf_op jit(solution)/shard_map/ppermute | solution.py:46
  32.2 2.7 %collective-permute-start.12 = (bf16[768,128]{1,0:T(8,128)(2,1)S(1)}, bf16[768,128]{1,0:T(8,128)(2,1)S(1)}, u32[]{:S(2)}, u32[]{:S(2)}) collective-permute-start(bf16[768,128]{1,0:T(8,128)(2,1)S(1)} %constant_dynamic-update-slice_fusion.mine_ref), channel_id=1, source_target_pairs={{0,1},{1,0},{2,3},{3,2},{4,5},{5,4},{6,7},{7,6},{8,9},{9,8},{10,11... | collective-permute-start | bytes 589832 | tf_op jit(solution)/shard_map/ppermute | solution.py:46

commit v4 on v3

--- a/solution.py
+++ b/solution.py
@@ -82,6 +82,14 @@
     return values
 
 
+def unscaled_in_kernel(ref):
+    rows = ref.shape[0] - EXTRA
+    scale = ref[rows : rows + 1]
+    for factor in range(rows + 1, rows + FACTORS):
+        scale = scale * ref[factor : factor + 1]
+    return ref[:rows] * scale
+
+
 def one_hot_of(order_ref, panels):
     local = lax.rem(order_ref[...], panels)
     rows = lax.broadcasted_iota(jnp.int32, (panels, panels), 0)
@@ -101,42 +109,38 @@
     return place & 1, (place >> 1) & 1, (place >> 2) & 1
 
 
-def first_kernel(
-    tree_ref,
-    basis_hbm,
-    stack_ref,
-    send_1_ref,
-    keep_1_ref,
-    part_2_ref,
-    send_3_ref,
-    keep_3_ref,
-    basis,
-    sems,
-):
+def product(stack, basis, i, start, width):
+    panels = basis.shape[2]
+    return dot(stack, basis[i, :, :, pl.ds(start, width)].reshape(2 * panels, width))
+
+
+def first_kernel(tree_ref, basis_hbm, stack_ref, send_ref, keep_ref, basis, sems):
     core, _, low = position()
-    levels, _, panels, rank = basis.shape
+    half = basis.shape[3] // 2
+    copy = pltpu.make_async_copy(basis_hbm.at[0], basis.at[0], sems.at[0])
+    copy.start()
+    stack = signed_stack(tree_ref[...])
+    stack_ref[...] = stack
+    copy.wait()
+    send_ref[...] = product(stack, basis, 0, pl.multiple_of((low ^ core ^ 1) * half, half), half)
+    keep_ref[...] = product(stack, basis, 0, pl.multiple_of((low ^ core) * half, half), half)
+
+
+def others_kernel(stack_ref, basis_hbm, part_2_ref, send_3_ref, keep_3_ref, basis, sems):
+    core, _, _ = position()
+    rank = basis.shape[3]
     half = rank // 2
     copies = [
-        pltpu.make_async_copy(basis_hbm.at[level], basis.at[level], sems.at[level])
-        for level in range(levels)
+        pltpu.make_async_copy(basis_hbm.at[1 + i], basis.at[i], sems.at[i]) for i in range(2)
     ]
     for copy in copies:
         copy.start()
-    stack = signed_stack(tree_ref[...])
-    stack_ref[...] = stack
-
-    def product(level, start, width):
-        columns = basis[level, :, :, pl.ds(start, width)].reshape(2 * panels, width)
-        return dot(stack, columns)
-
+    stack = stack_ref[...]
     copies[0].wait()
-    send_1_ref[...] = product(0, pl.multiple_of((low ^ core ^ 1) * half, half), half)
-    keep_1_ref[...] = product(0, pl.multiple_of((low ^ core) * half, half), half)
+    part_2_ref[...] = product(stack, basis, 0, 0, rank)
     copies[1].wait()
-    part_2_ref[...] = product(1, 0, rank)
-    copies[2].wait()
-    send_3_ref[...] = product(2, pl.multiple_of((core ^ 1) * half, half), half)
-    keep_3_ref[...] = product(2, pl.multiple_of(core * half, half), half)
+    send_3_ref[...] = product(stack, basis, 1, pl.multiple_of((core ^ 1) * half, half), half)
+    keep_3_ref[...] = product(stack, basis, 1, pl.multiple_of(core * half, half), half)
 
 
 def near_kernel(index_ref, stack_ref, near_ref, core_ref, far_ref, own_ref, sums):
@@ -169,8 +173,11 @@
         scaled_to(out, keep_ref[:, lanes] + got_ref[:, lanes])
 
 
-def sums_kernel(part_2_ref, got_2_ref, keep_3_ref, got_3_ref, two_ref, three_ref):
-    three_ref[...] = (keep_3_ref[...] + got_3_ref[...]).astype(BF16)
+def sums_kernel(part_2_ref, got_2_ref, keep_3_ref, got_3_ref, two_ref, *three_refs):
+    for part, out in enumerate(three_refs):
+        width = out.shape[1]
+        lanes = pl.ds(part * width, width)
+        out[...] = (keep_3_ref[:, lanes] + got_3_ref[:, lanes]).astype(BF16)
     scaled_to(two_ref, part_2_ref[...] + got_2_ref[...])
 
 
@@ -201,11 +208,14 @@
     ahead_ref[...] = forward_ref[...].reshape(ahead_ref.shape)
 
 
-def second_kernel(hot_ref, base_ref, two_ref, basis_ref, ahead_ref, out_ref, grad_ref):
-    total = base_ref[...] + expanded(two_ref[...], basis_ref, 1, 0, two_ref.shape[1])
+def second_kernel(
+    hot_ref, base_ref, two_ref, two_got_ref, basis_ref, ahead_ref, out_ref, grad_ref
+):
+    two = (unscaled_in_kernel(two_ref) + unscaled_in_kernel(two_got_ref)).astype(BF16)
+    total = base_ref[...] + expanded(two, basis_ref, 1, 0, two.shape[1])
     one_hot = hot_ref[...]
     field = jnp.zeros_like(total)
-    for _ in range(3):
+    for _ in range(2):
         piece = total.astype(BF16)
         total = total - piece.astype(F32)
         field += dot_t(piece, one_hot)
@@ -243,15 +253,31 @@
     halves = array((both, half), F32)
     one_hot = (lax.rem(cluster_order, panels)[None, :] == jnp.arange(panels)[:, None]).astype(BF16)
     tree = dot(sources.reshape(both, panels), one_hot).astype(BF16)
-    stack, send_1, keep_1, part_2, send_3, keep_3 = call(
+    stack, send_1, keep_1 = call(
         first_kernel,
-        (array((both, 2 * panels), BF16), halves, halves, array((both, rank), F32), halves, halves),
+        (array((both, 2 * panels), BF16), halves, halves),
         2,
-        scratch_shapes=[pltpu.VMEM((3, 2, panels, rank), BF16), pltpu.SemaphoreType.DMA((3,))],
+        scratch_shapes=[pltpu.VMEM((1, 2, panels, rank), BF16), pltpu.SemaphoreType.DMA((1,))],
+        far=(1,),
+        vmem=52 * 1024 * 1024,
+    )(tree, row_bases)
+    got_1 = swapped(send_1, 1)
+    part_2, send_3, keep_3 = call(
+        others_kernel,
+        (array((both, rank), F32), halves, halves),
+        2,
+        scratch_shapes=[pltpu.VMEM((2, 2, panels, rank), BF16), pltpu.SemaphoreType.DMA((2,))],
         far=(1,),
         vmem=50 * 1024 * 1024,
-    )(tree, row_bases)
-    got_1 = swapped(send_1, 1)
+    )(stack, row_bases)
+
+    got_1, send_3, part_2 = lax.optimization_barrier((got_1, send_3, part_2))
+    got_3 = swapped(send_3, 1)
+    got_2 = swapped(part_2, 1)
+    packed = array((both + EXTRA, quarter), F32)
+    to_f, to_g = call(spread_kernel, (packed, packed), 2)(keep_1, got_1)
+    got_f = by_core(to_f.astype(jnp.float16), 8, 12)
+    got_g = by_core(to_g.astype(jnp.float16), 10, 14)
 
     blocks = near_blocks.shape[1]
     size = near_blocks.shape[3]
@@ -261,28 +287,22 @@
         3,
         scratch_shapes=[pltpu.VMEM((3 * blocks, both, size), F32)],
         smem=(0,),
-    )(near_index, stack, near_blocks)
-
-    packed = array((both + EXTRA, quarter), F32)
-    got_1, own, send_3, part_2 = lax.optimization_barrier((got_1, own, send_3, part_2))
-    got_3 = swapped(send_3, 1)
-    got_2 = swapped(part_2, 1)
-    to_f, to_g = call(spread_kernel, (packed, packed), 2)(keep_1, got_1)
-    got_f = by_core(to_f.astype(jnp.float16), 8, 12)
-    got_g = by_core(to_g.astype(jnp.float16), 10, 14)
-
-    two_sent, three_sent = call(
-        sums_kernel, (array((both + EXTRA, rank), F32), array((both, half), BF16)), 4
+    )(near_index, after(stack, to_f), near_blocks)
+
+    quarters = array((both, quarter), BF16)
+    two_sent, *three_sent = call(
+        sums_kernel, (array((both + EXTRA, rank), F32), quarters, quarters), 4
     )(part_2, got_2, keep_3, after(got_3, to_f))
-    mine_3 = swapped(three_sent, 2)
+    mine_3 = [swapped(part, 2) for part in three_sent]
     two_sent = two_sent.astype(jnp.float16)
     got_cd = by_core(two_sent, 4, 6)
     peers = lax.axis_size(TREE)
     joints = [(i, i + 1) for i in range(1, peers - 1, 2)]
     far_halo = lax.ppermute(to_far, TREE, joints + [(b, a) for a, b in joints])
 
-    got_f, got_g, _ = lax.optimization_barrier((got_f, got_g, two_sent))
-    parts = lax.all_gather(unscaled(got_f) + unscaled(got_g), "rhs", axis=0)
+    got_f, got_g, _, *mine_3 = lax.optimization_barrier((got_f, got_g, two_sent, *mine_3))
+    middle = unscaled(got_f) + unscaled(got_g)
+    parts = lax.all_gather(middle, "rhs", axis=0)
     quarter_sum = (parts[0] + parts[1]).astype(BF16)
     got_a = by_core(quarter_sum, 2, 4)
     got_b = by_core(quarter_sum, None, 6)
@@ -296,14 +316,15 @@
         ),
         3,
     )(after(order, quarter_sum), col_bases, forward_field)
+    mine_3 = jnp.concatenate(mine_3, axis=1)
     mine_3, own, _, _ = lax.optimization_barrier((mine_3, own, quarter_sum, moved))
     pair_3 = swapped(jnp.concatenate([mine_3, to_core], axis=0), 1)
     base = call(halo_kernel, array((both, panels), F32), 5)(own, far_halo, mine_3, pair_3, col_bases)
     got_cd = after(got_cd, quarter_sum)
-    all_2 = (unscaled(got_cd) + unscaled(swapped(got_cd, 1))).astype(BF16)
+    other_cd = swapped(got_cd, 1)
     base, first_grad = call(
-        second_kernel, (array((both, panels), F32), array((1, panels), F32)), 5
-    )(hot, base, all_2, col_bases, ahead)
+        second_kernel, (array((both, panels), F32), array((1, panels), F32)), 6
+    )(hot, base, got_cd.astype(F32), other_cd.astype(F32), col_bases, ahead)
     mine_1 = jnp.concatenate([got_a, got_b], axis=0)
     field, grad = call(
         last_kernel,

time: 36.7 us -> 35.8 us (0.975); the launches traced: 36.1 us -> 35.6 us
  waiting for transfers between devices: 10.5 us -> 4.15 us
  starting transfers between devices: 14 us -> 20.1 us
    ppermute x7 -> x8, starting transfers between devices: 2.35 us -> 7.47 us  [swapped(): lax.ppermute(x, TREE, [(i, i ^ distance) for i in range(lax.axis_size(TRE...]
    ppermute x7 -> x8, waiting for transfers between devices: 4.88 us -> 0.8 us  [swapped(): lax.ppermute(x, TREE, [(i, i ^ distance) for i in range(lax.axis_size(TRE...]
    ppermute x5, waiting for transfers between devices: 5.62 us -> 3.34 us  [by_core(): return lax.ppermute(x, TREE, pairs)]
    ppermute x5, starting transfers between devices: 11 us -> 11.8 us  [by_core(): return lax.ppermute(x, TREE, pairs)]
    pallas_call x2 -> x3, Pallas kernels: 2.46 us -> 2.56 us  [the longest x1 1.42 us: fast_body(): call(first_kernel, (array((both, 2 * panels), BF16), halves, halves), 2,...]
  transfers between devices with their start and end apart: 13 -> 14, of which waited for: 5 -> 4; matrix products, arithmetic and copies ran while one was open for 2% -> 1% of each run, Pallas kernels for 9% -> 12%
where the time goes in v4:
time: 35.8 us; the launch traced here: 35.6 us
  starting transfers between devices  20.1 us (56%)
  Pallas kernels  6.76 us (19%)
  waiting for transfers between devices  4.15 us (12%)
  blocking collectives  2.09 us (6%)
  other arithmetic  1.23 us (3%)
  between operations  0.92 us (3%)
    ppermute x5, starting transfers between devices, by_core(): return lax.ppermute(x, TREE, pairs)  11.8 us
    ppermute x8, starting transfers between devices, swapped(): lax.ppermute(x, TREE, [(i, i ^ distance) for i in range(lax.axis_size(TRE...  7.47 us
    ppermute x5, waiting for transfers between devices, by_core(): return lax.ppermute(x, TREE, pairs)  3.34 us
    all_gather x1, blocking collectives, fast_body(): parts = lax.all_gather(middle, 'rhs', axis=0)  2.09 us
    pallas_call x1, Pallas kernels, fast_body(): call(first_kernel, (array((both, 2 * panels), BF16), halves, halves), 2,...  1.42 us
    pallas_call x1, Pallas kernels, fast_body(): call(near_kernel, (array((both, panels), BF16), array((both, panels), BF1...  1.32 us
    pallas_call x1, Pallas kernels, fast_body(): call(last_kernel, (array((two, rows, panels), F32), array((1, panels), F3...  1.2 us
    pallas_call x1, Pallas kernels, fast_body(): call(others_kernel, (array((both, rank), F32), halves, halves), 2, scratc...  0.85 us
  transfers between devices with their start and end apart: 14, of which 4 were waited for; matrix products, arithmetic and copies ran while one was open for 1% of the time, Pallas kernels for 12%

profile of v4, /device:TPU:0, one launch (start us, length us, event | category | flops | bytes accessed | tf_op | source)
XLA Modules:
  0.0 35.6 jit_solution(3148087224941272882)
XLA Ops:
  0.6 0.0 copy-start
  0.6 0.0 copy-start.2
  0.7 0.8 %compare_select_fusion = s32[256]{0:T(256)S(1)} fusion(s32[256]{0:T(256)} %param.13), kind=kLoop, calls=%fused_computation.11 | loop fusion | flops 1536 | bytes 2048 | tf_op jit(solution)/shard_map/rem | solution.py:254
  1.5 0.1 copy-done
  1.6 0.2 fusion.tree_ref
  1.8 1.4 %shard_map.86 = (bf16[384,512]{1,0:T(8,128)(2,1)S(1)}, f32[384,256]{1,0:T(8,128)S(1)}, f32[384,256]{1,0:T(8,128)S(1)}) custom-call(bf16[384,256]{1,0:T(8,128)(2,1)S(1)} %fusion.tree_ref, bf16[3,2,256,512]{3,2,1,0:T(8,128)(2,1)} %basis_hbm.3), custom_call_target="tpu_custom_call" | custom-call | tf_op jit(solution)/shard_map/pallas_call | solution.py:256
  3.2 0.5 %collective-permute-start = (f32[384,256]{1,0:T(8,128)S(1)}, f32[384,256]{1,0:T(8,128)S(1)}, u32[]{:S(2)}, u32[]{:S(2)}) collective-permute-start(f32[384,256]{1,0:T(8,128)S(1)} %get-tuple-element.37), channel_id=1, source_target_pairs={{0,1},{1,0},{2,3},{3,2},{4,5},{5,4},{6,7},{7,6},{8,9},{9,8},{10,11... | collective-permute-start | bytes 1179656 | tf_op jit(solution)/shard_map/ppermute | solution.py:46
  3.7 0.9 %shard_map.87 = (f32[384,512]{1,0:T(8,128)S(1)}, f32[384,256]{1,0:T(8,128)S(1)}, f32[384,256]{1,0:T(8,128)S(1)}) custom-call(bf16[384,512]{1,0:T(8,128)(2,1)S(1)} %get-tuple-element.57.stack_ref, bf16[3,2,256,512]{3,2,1,0:T(8,128)(2,1)S(1)} %copy-done.2), custom_call_target="tpu_custom_call" | custom-call | tf_op jit(solution)/shard_map/pallas_call | solution.py:265
  4.6 0.5 %collective-permute-done.got_ref = f32[384,256]{1,0:T(8,128)S(1)} collective-permute-done((f32[384,256]{1,0:T(8,128)S(1)}, f32[384,256]{1,0:T(8,128)S(1)}, u32[]{:S(2)}, u32[]{:S(2)}) %collective-permute-start) | collective-permute-done | bytes 393248 | tf_op jit(solution)/shard_map/ppermute | solution.py:46
  5.1 0.4 %collective-permute-start.3 = (f32[384,512]{1,0:T(8,128)S(1)}, f32[384,512]{1,0:T(8,128)S(1)}, u32[]{:S(2)}, u32[]{:S(2)}) collective-permute-start(f32[384,512]{1,0:T(8,128)S(1)} %get-tuple-element.44.part_2_ref), channel_id=1, source_target_pairs={{0,1},{1,0},{2,3},{3,2},{4,5},{5,4},{6,7},{7,6},{8,9},{9,8},{10,11... | collective-permute-start | bytes 2359304 | tf_op jit(solution)/shard_map/ppermute | solution.py:46
  5.5 0.1 collective-permute-start.4
  5.6 0.2 shard_map.88
  5.8 0.0 copy-start.3
  5.8 0.0 copy-start.6
  5.8 4.0 %collective-permute-start.1 = (f16[400,128]{1,0:T(8,128)(2,1)S(1)}, f16[400,128]{1,0:T(8,128)(2,1)S(1)}, u32[]{:S(2)}, u32[]{:S(2)}) collective-permute-start(f16[400,128]{1,0:T(8,128)(2,1)S(1)} %convert_element_type.24), channel_id=1, source_target_pairs={{0,8},{1,13},{2,10},{3,15},{4,12},{5,9},{6,14},{7,11},{8,0},{9,5},... | collective-permute-start | bytes 307208 | tf_op jit(solution)/shard_map/ppermute | solution.py:55
  9.9 1.3 %collective-permute-start.2 = (f16[400,128]{1,0:T(8,128)(2,1)S(1)}, f16[400,128]{1,0:T(8,128)(2,1)S(1)}, u32[]{:S(2)}, u32[]{:S(2)}) collective-permute-start(f16[400,128]{1,0:T(8,128)(2,1)S(1)} %convert_element_type.25), channel_id=1, source_target_pairs={{0,10},{1,15},{2,8},{3,13},{4,14},{5,11},{6,12},{7,9},{8,2},{9,7},... | collective-permute-start | bytes 307208 | tf_op jit(solution)/shard_map/ppermute | solution.py:55
  11.2 0.0 collective-permute-done.4.got_3_ref
  11.2 0.0 collective-permute-done.3.got_2_ref
  11.2 0.3 shard_map.89
  11.5 0.3 collective-permute-start.5
  11.8 1.8 %collective-permute-start.6 = (bf16[384,128]{1,0:T(8,128)(2,1)S(1)}, bf16[384,128]{1,0:T(8,128)(2,1)S(1)}, u32[]{:S(2)}, u32[]{:S(2)}) collective-permute-start(bf16[384,128]{1,0:T(8,128)(2,1)S(1)} %get-tuple-element.50), channel_id=1, source_target_pairs={{0,2},{1,3},{2,0},{3,1},{4,6},{5,7},{6,4},{7,5},{8,10},{9,11},{10,... | collective-permute-start | bytes 294920 | tf_op jit(solution)/shard_map/ppermute | solution.py:46
  13.6 1.3 %shard_map.91 = (bf16[384,256]{1,0:T(8,128)(2,1)S(1)}, bf16[384,256]{1,0:T(8,128)(2,1)S(1)}, f32[384,256]{1,0:T(8,128)S(1)}) custom-call(s32[2,8]{1,0:T(2,128)S(1)} %copy-done.6, bf16[384,512]{1,0:T(8,128)(2,1)S(1)} %get-tuple-element.57.stack_ref, bf16[2,2,8,128,128]{4,3,2,1,0:T(8,128)(2,1)S(1)} %copy-done.3), custom_call_target="tpu_custom_call" | custom-call | tf_op jit(solution)/shard_map/pallas_call | solution.py:284
  14.9 0.0 copy-start.1
  14.9 0.0 copy-start.4
  15.0 0.0 copy-start.5
  15.0 0.8 %collective-permute-start.7 = (bf16[384,256]{1,0:T(8,128)(2,1)S(1)}, bf16[384,256]{1,0:T(8,128)(2,1)S(1)}, u32[]{:S(2)}, u32[]{:S(2)}) collective-permute-start(bf16[384,256]{1,0:T(8,128)(2,1)S(1)} %get-tuple-element.61), channel_id=1, source_target_pairs={{1,2},{3,4},{5,6},{7,8},{9,10},{11,12},{13,14},{2,1},{4,3},{6,5},{... | collective-permute-start | bytes 589832 | tf_op jit(solution)/shard_map/ppermute | solution.py:301
  15.8 0.1 convert_element_type.52
  15.9 2.9 %collective-permute-start.9 = (f16[400,512]{1,0:T(8,128)(2,1)S(1)}, f16[400,512]{1,0:T(8,128)(2,1)S(1)}, u32[]{:S(2)}, u32[]{:S(2)}) collective-permute-start(f16[400,512]{1,0:T(8,128)(2,1)S(1)} %convert_element_type.52), channel_id=1, source_target_pairs={{0,4},{1,7},{2,6},{3,5},{4,0},{5,3},{6,2},{7,1},{8,12},{9,15},{10,... | collective-permute-start | bytes 1228808 | tf_op jit(solution)/shard_map/ppermute | solution.py:55
  18.8 2.0 %collective-permute-done.2 = f16[400,128]{1,0:T(8,128)(2,1)S(1)} collective-permute-done((f16[400,128]{1,0:T(8,128)(2,1)S(1)}, f16[400,128]{1,0:T(8,128)(2,1)S(1)}, u32[]{:S(2)}, u32[]{:S(2)}) %collective-permute-start.2) | collective-permute-done | bytes 102432 | tf_op jit(solution)/shard_map/ppermute | solution.py:55
  20.8 0.3 collective-permute-done.6
  21.1 0.1 multiply_add_fusion
  21.2 2.1 %all-gather = f32[768,128]{1,0:T(8,128)S(1)} all-gather(f32[384,128]{1,0:T(8,128)S(1)} %multiply_add_fusion), channel_id=2, replica_groups=mesh['groups'=2,'leaf'=8,'rhs'=2] {'rhs'}, dimensions={0}, use_global_device_ids=true | all-gather | bytes 589824 | tf_op jit(solution)/shard_map/all_gather | solution.py:305
  23.3 2.9 %collective-permute-start.11 = (bf16[384,128]{1,0:T(8,128)(2,1)S(1)}, bf16[384,128]{1,0:T(8,128)(2,1)S(1)}, u32[]{:S(2)}, u32[]{:S(2)}) collective-permute-start(bf16[384,128]{1,0:T(8,128)(2,1)S(1)} %fusion.1.own_ref), channel_id=1, source_target_pairs={{0,2},{1,5},{2,0},{3,7},{4,6},{5,1},{6,4},{7,3},{8,10},{9,13},{10,... | collective-permute-start | bytes 294920 | tf_op jit(solution)/shard_map/ppermute | solution.py:55
  26.2 0.7 %collective-permute-start.12 = (bf16[384,128]{1,0:T(8,128)(2,1)S(1)}, bf16[384,128]{1,0:T(8,128)(2,1)S(1)}, u32[]{:S(2)}, u32[]{:S(2)}) collective-permute-start(bf16[384,128]{1,0:T(8,128)(2,1)S(1)} %fusion.1.own_ref), channel_id=1, source_target_pairs={{1,7},{3,5},{5,3},{7,1},{9,15},{11,13},{13,11},{15,9},{17,23},{19,... | collective-permute-start | bytes 294920 | tf_op jit(solution)/shard_map/ppermute | solution.py:55
  26.9 0.3 shard_map.90
  27.3 2.3 %collective-permute-start.8 = (bf16[768,256]{1,0:T(8,128)(2,1)S(1)}, bf16[768,256]{1,0:T(8,128)(2,1)S(1)}, u32[]{:S(2)}, u32[]{:S(2)}) collective-permute-start(bf16[768,256]{1,0:T(8,128)(2,1)S(1)} %pad_maximum_fusion), channel_id=1, source_target_pairs={{0,1},{1,0},{2,3},{3,2},{4,5},{5,4},{6,7},{7,6},{8,9},{9,8},{10,11... | collective-permute-start | bytes 1179656 | tf_op jit(solution)/shard_map/ppermute | solution.py:46
  29.6 1.3 %collective-permute-done.9 = f16[400,512]{1,0:T(8,128)(2,1)S(1)} collective-permute-done((f16[400,512]{1,0:T(8,128)(2,1)S(1)}, f16[400,512]{1,0:T(8,128)(2,1)S(1)}, u32[]{:S(2)}, u32[]{:S(2)}) %collective-permute-start.9) | collective-permute-done | bytes 409632 | tf_op jit(solution)/shard_map/ppermute | solution.py:55
  30.9 0.0 collective-permute-start.10
  30.9 0.0 collective-permute-done.11
  30.9 0.0 collective-permute-done.12
  31.0 2.0 %collective-permute-start.13 = (bf16[768,128]{1,0:T(8,128)(2,1)S(1)}, bf16[768,128]{1,0:T(8,128)(2,1)S(1)}, u32[]{:S(2)}, u32[]{:S(2)}) collective-permute-start(bf16[768,128]{1,0:T(8,128)(2,1)S(1)} %constant_dynamic-update-slice_fusion.mine_ref), channel_id=1, source_target_pairs={{0,1},{1,0},{2,3},{3,2},{4,5},{5,4},{6,7},{7,6},{8,9},{9,8},{10,11... | collective-permute-start | bytes 589832 | tf_op jit(solution)/shard_map/ppermute | solution.py:46
  33.0 0.1 convert_element_type.57.two_ref
  33.1 0.0 collective-permute-done.7.far_ref
  33.1 0.4 %shard_map.92.base_ref = f32[384,256]{1,0:T(8,128)S(1)} custom-call(f32[384,256]{1,0:T(8,128)S(1)} %get-tuple-element.60.own_ref, bf16[384,256]{1,0:T(8,128)(2,1)S(1)} %collective-permute-done.7.far_ref, bf16[384,256]{1,0:T(8,128)(2,1)S(1)} %pad_maximum_fusion.1.three_ref, bf16[768,256]{1,0:T(8,128)(2,1)S(1)} %collective-permute-done.8.pair_ref, ...), custom_call_target="tpu_custom_call" | custom-call | tf_op jit(solution)/shard_map/pallas_call | solution.py:322
  33.5 0.0 collective-permute-done.10
  33.5 0.1 convert_element_type.58.two_got_ref
  33.6 0.8 %shard_map.93 = (f32[384,256]{1,0:T(8,128)S(1)}, f32[1,256]{1,0:T(1,128)S(1)}) custom-call(bf16[256,256]{1,0:T(8,128)(2,1)S(1)} %get-tuple-element.54.hot_ref, f32[384,256]{1,0:T(8,128)S(1)} %shard_map.92.base_ref, f32[400,512]{1,0:T(8,128)S(1)} %convert_element_type.57.two_ref, f32[400,512]{1,0:T(8,128)S(1)} %convert_element_type.58.two_got_ref, ...), custom_call_target="tpu_custom_call" | custom-call | tf_op jit(solution)/shard_map/pallas_call | solution.py:325
  34.4 1.2 %shard_map.94 = (f32[2,192,256]{2,1,0:T(8,128)}, f32[1,256]{1,0:T(1,128)}) custom-call(f32[384,256]{1,0:T(8,128)S(1)} %get-tuple-element.66.base_ref, f32[1,256]{1,0:T(1,128)S(1)} %get-tuple-element.67.first_grad_ref, bf16[384,128]{1,0:T(8,128)(2,1)S(1)} %fusion.1.own_ref, bf16[768,128]{1,0:T(8,128)(2,1)S(1)} %constant_dynamic-update-slice_fusion.mine_ref, ...), custom_call_target="tpu_custom_call" | custom-call | tf_op jit(solution)/shard_map/pallas_call | solution.py:329
  (18 shorter events, 0.2 us)
Async XLA Ops:
  0.6 0.9 %copy-start = (bf16[2,192,256]{2,1,0:T(8,128)(2,1)S(1)}, bf16[2,192,256]{2,1,0:T(8,128)(2,1)}, u32[]{:S(2)}) copy-start(bf16[2,192,256]{2,1,0:T(8,128)(2,1)} %param.7) | copy-start | bytes 589828
  0.6 3.1 %copy-start.2 = (bf16[3,2,256,512]{3,2,1,0:T(8,128)(2,1)S(1)}, bf16[3,2,256,512]{3,2,1,0:T(8,128)(2,1)}, u32[]{:S(2)}) copy-start(bf16[3,2,256,512]{3,2,1,0:T(8,128)(2,1)} %basis_hbm.3) | copy-start | bytes 4718596
  3.2 1.9 %collective-permute-start = (f32[384,256]{1,0:T(8,128)S(1)}, f32[384,256]{1,0:T(8,128)S(1)}, u32[]{:S(2)}, u32[]{:S(2)}) collective-permute-start(f32[384,256]{1,0:T(8,128)S(1)} %get-tuple-element.37), channel_id=1, source_target_pairs={{0,1},{1,0},{2,3},{3,2},{4,5},{5,4},{6,7},{7,6},{8,9},{9,8},{10,11... | collective-permute-start | bytes 1179656 | tf_op jit(solution)/shard_map/ppermute | solution.py:46
  5.1 6.1 %collective-permute-start.3 = (f32[384,512]{1,0:T(8,128)S(1)}, f32[384,512]{1,0:T(8,128)S(1)}, u32[]{:S(2)}, u32[]{:S(2)}) collective-permute-start(f32[384,512]{1,0:T(8,128)S(1)} %get-tuple-element.44.part_2_ref), channel_id=1, source_target_pairs={{0,1},{1,0},{2,3},{3,2},{4,5},{5,4},{6,7},{7,6},{8,9},{9,8},{10,11... | collective-permute-start | bytes 2359304 | tf_op jit(solution)/shard_map/ppermute | solution.py:46
  5.5 5.7 %collective-permute-start.4 = (f32[384,256]{1,0:T(8,128)S(1)}, f32[384,256]{1,0:T(8,128)S(1)}, u32[]{:S(2)}, u32[]{:S(2)}) collective-permute-start(f32[384,256]{1,0:T(8,128)S(1)} %get-tuple-element.46), channel_id=1, source_target_pairs={{0,1},{1,0},{2,3},{3,2},{4,5},{5,4},{6,7},{7,6},{8,9},{9,8},{10,11... | collective-permute-start | bytes 1179656 | tf_op jit(solution)/shard_map/ppermute | solution.py:46
  5.8 7.8 %copy-start.3 = (bf16[2,2,8,128,128]{4,3,2,1,0:T(8,128)(2,1)S(1)}, bf16[2,2,8,128,128]{4,3,2,1,0:T(8,128)(2,1)}, u32[]{:S(2)}) copy-start(bf16[2,2,8,128,128]{4,3,2,1,0:T(8,128)(2,1)} %near_ref.1) | copy-start | bytes 3145732
  5.8 7.8 %copy-start.6 = (s32[2,8]{1,0:T(2,128)S(1)}, s32[2,8]{1,0:T(2,128)}, u32[]{:S(2)}) copy-start(s32[2,8]{1,0:T(2,128)} %index_ref.1) | copy-start | bytes 196
  5.8 10.0 %collective-permute-start.1 = (f16[400,128]{1,0:T(8,128)(2,1)S(1)}, f16[400,128]{1,0:T(8,128)(2,1)S(1)}, u32[]{:S(2)}, u32[]{:S(2)}) collective-permute-start(f16[400,128]{1,0:T(8,128)(2,1)S(1)} %convert_element_type.24), channel_id=1, source_target_pairs={{0,8},{1,13},{2,10},{3,15},{4,12},{5,9},{6,14},{7,11},{8,0},{9,5},... | collective-permute-start | bytes 307208 | tf_op jit(solution)/shard_map/ppermute | solution.py:55
  9.9 10.9 %collective-permute-start.2 = (f16[400,128]{1,0:T(8,128)(2,1)S(1)}, f16[400,128]{1,0:T(8,128)(2,1)S(1)}, u32[]{:S(2)}, u32[]{:S(2)}) collective-permute-start(f16[400,128]{1,0:T(8,128)(2,1)S(1)} %convert_element_type.25), channel_id=1, source_target_pairs={{0,10},{1,15},{2,8},{3,13},{4,14},{5,11},{6,12},{7,9},{8,2},{9,7},... | collective-permute-start | bytes 307208 | tf_op jit(solution)/shard_map/ppermute | solution.py:55
  11.5 9.3 %collective-permute-start.5 = (bf16[384,128]{1,0:T(8,128)(2,1)S(1)}, bf16[384,128]{1,0:T(8,128)(2,1)S(1)}, u32[]{:S(2)}, u32[]{:S(2)}) collective-permute-start(bf16[384,128]{1,0:T(8,128)(2,1)S(1)} %get-tuple-element.49), channel_id=1, source_target_pairs={{0,2},{1,3},{2,0},{3,1},{4,6},{5,7},{6,4},{7,5},{8,10},{9,11},{10,... | collective-permute-start | bytes 294920 | tf_op jit(solution)/shard_map/ppermute | solution.py:46
  11.8 9.3 %collective-permute-start.6 = (bf16[384,128]{1,0:T(8,128)(2,1)S(1)}, bf16[384,128]{1,0:T(8,128)(2,1)S(1)}, u32[]{:S(2)}, u32[]{:S(2)}) collective-permute-start(bf16[384,128]{1,0:T(8,128)(2,1)S(1)} %get-tuple-element.50), channel_id=1, source_target_pairs={{0,2},{1,3},{2,0},{3,1},{4,6},{5,7},{6,4},{7,5},{8,10},{9,11},{10,... | collective-permute-start | bytes 294920 | tf_op jit(solution)/shard_map/ppermute | solution.py:46
  14.9 11.9 %copy-start.1 = (bf16[3,2,256,512]{3,2,1,0:T(8,128)(2,1)S(1)}, bf16[3,2,256,512]{3,2,1,0:T(8,128)(2,1)}, u32[]{:S(2)}) copy-start(bf16[3,2,256,512]{3,2,1,0:T(8,128)(2,1)} %basis_ref.5) | copy-start | bytes 4718596
  14.9 11.9 %copy-start.4 = (bf16[2,192,256]{2,1,0:T(8,128)(2,1)S(1)}, bf16[2,192,256]{2,1,0:T(8,128)(2,1)}, u32[]{:S(2)}) copy-start(bf16[2,192,256]{2,1,0:T(8,128)(2,1)} %forward_ref.1) | copy-start | bytes 589828
  15.0 11.9 %copy-start.5 = (s32[256]{0:T(256)S(1)}, s32[256]{0:T(256)}, u32[]{:S(2)}) copy-start(s32[256]{0:T(256)} %param.13) | copy-start | bytes 3076
  15.0 18.1 %collective-permute-start.7 = (bf16[384,256]{1,0:T(8,128)(2,1)S(1)}, bf16[384,256]{1,0:T(8,128)(2,1)S(1)}, u32[]{:S(2)}, u32[]{:S(2)}) collective-permute-start(bf16[384,256]{1,0:T(8,128)(2,1)S(1)} %get-tuple-element.61), channel_id=1, source_target_pairs={{1,2},{3,4},{5,6},{7,8},{9,10},{11,12},{13,14},{2,1},{4,3},{6,5},{... | collective-permute-start | bytes 589832 | tf_op jit(solution)/shard_map/ppermute | solution.py:301
  15.9 15.0 %collective-permute-start.9 = (f16[400,512]{1,0:T(8,128)(2,1)S(1)}, f16[400,512]{1,0:T(8,128)(2,1)S(1)}, u32[]{:S(2)}, u32[]{:S(2)}) collective-permute-start(f16[400,512]{1,0:T(8,128)(2,1)S(1)} %convert_element_type.52), channel_id=1, source_target_pairs={{0,4},{1,7},{2,6},{3,5},{4,0},{5,3},{6,2},{7,1},{8,12},{9,15},{10,... | collective-permute-start | bytes 1228808 | tf_op jit(solution)/shard_map/ppermute | solution.py:55
  23.3 7.6 %collective-permute-start.11 = (bf16[384,128]{1,0:T(8,128)(2,1)S(1)}, bf16[384,128]{1,0:T(8,128)(2,1)S(1)}, u32[]{:S(2)}, u32[]{:S(2)}) collective-permute-start(bf16[384,128]{1,0:T(8,128)(2,1)S(1)} %fusion.1.own_ref), channel_id=1, source_target_pairs={{0,2},{1,5},{2,0},{3,7},{4,6},{5,1},{6,4},{7,3},{8,10},{9,13},{10,... | collective-permute-start | bytes 294920 | tf_op jit(solution)/shard_map/ppermute | solution.py:55
  26.2 4.7 %collective-permute-start.12 = (bf16[384,128]{1,0:T(8,128)(2,1)S(1)}, bf16[384,128]{1,0:T(8,128)(2,1)S(1)}, u32[]{:S(2)}, u32[]{:S(2)}) collective-permute-start(bf16[384,128]{1,0:T(8,128)(2,1)S(1)} %fusion.1.own_ref), channel_id=1, source_target_pairs={{1,7},{3,5},{5,3},{7,1},{9,15},{11,13},{13,11},{15,9},{17,23},{19,... | collective-permute-start | bytes 294920 | tf_op jit(solution)/shard_map/ppermute | solution.py:55
  27.3 5.8 %collective-permute-start.8 = (bf16[768,256]{1,0:T(8,128)(2,1)S(1)}, bf16[768,256]{1,0:T(8,128)(2,1)S(1)}, u32[]{:S(2)}, u32[]{:S(2)}) collective-permute-start(bf16[768,256]{1,0:T(8,128)(2,1)S(1)} %pad_maximum_fusion), channel_id=1, source_target_pairs={{0,1},{1,0},{2,3},{3,2},{4,5},{5,4},{6,7},{7,6},{8,9},{9,8},{10,11... | collective-permute-start | bytes 1179656 | tf_op jit(solution)/shard_map/ppermute | solution.py:46
  30.9 2.6 %collective-permute-start.10 = (f16[400,512]{1,0:T(8,128)(2,1)S(1)}, f16[400,512]{1,0:T(8,128)(2,1)S(1)}, u32[]{:S(2)}, u32[]{:S(2)}) collective-permute-start(f16[400,512]{1,0:T(8,128)(2,1)S(1)} %collective-permute-done.9), channel_id=1, source_target_pairs={{0,1},{1,0},{2,3},{3,2},{4,5},{5,4},{6,7},{7,6},{8,9},{9,8},{10,11... | collective-permute-start | bytes 1228808 | tf_op jit(solution)/shard_map/ppermute | solution.py:46
  31.0 3.4 %collective-permute-start.13 = (bf16[768,128]{1,0:T(8,128)(2,1)S(1)}, bf16[768,128]{1,0:T(8,128)(2,1)S(1)}, u32[]{:S(2)}, u32[]{:S(2)}) collective-permute-start(bf16[768,128]{1,0:T(8,128)(2,1)S(1)} %constant_dynamic-update-slice_fusion.mine_ref), channel_id=1, source_target_pairs={{0,1},{1,0},{2,3},{3,2},{4,5},{5,4},{6,7},{7,6},{8,9},{9,8},{10,11... | collective-permute-start | bytes 589832 | tf_op jit(solution)/shard_map/ppermute | solution.py:46

commit v5 on v4

--- a/solution.py
+++ b/solution.py
@@ -21,7 +21,7 @@
     return lax.dot_general(a, b, (((1,), (1,)), ((), ())), preferred_element_type=F32)
 
 
-def call(kernel, out_shape, inputs, scratch_shapes=(), smem=(), far=(), vmem=VMEM_BYTES, cost=0):
+def call(kernel, out_shape, inputs, scratch_shapes=(), smem=(), far=(), vmem=VMEM_BYTES):
     def place(i):
         if i in far:
             return pl.BlockSpec(memory_space=pltpu.HBM)
@@ -34,7 +34,6 @@
         out_specs=jax.tree.map(lambda _: pl.BlockSpec(memory_space=pltpu.VMEM), out_shape),
         scratch_shapes=list(scratch_shapes),
         compiler_params=pltpu.CompilerParams(vmem_limit_bytes=vmem),
-        cost_estimate=pl.CostEstimate(flops=0, bytes_accessed=cost, transcendentals=0) if cost else None,
     )
 
 
@@ -126,7 +125,7 @@
     keep_ref[...] = product(stack, basis, 0, pl.multiple_of((low ^ core) * half, half), half)
 
 
-def others_kernel(stack_ref, basis_hbm, part_2_ref, send_3_ref, keep_3_ref, basis, sems):
+def others_kernel(stack_ref, basis_hbm, send_ref, keep_3_ref, basis, sems):
     core, _, _ = position()
     rank = basis.shape[3]
     half = rank // 2
@@ -137,9 +136,9 @@
         copy.start()
     stack = stack_ref[...]
     copies[0].wait()
-    part_2_ref[...] = product(stack, basis, 0, 0, rank)
+    send_ref[:, :rank] = product(stack, basis, 0, 0, rank)
     copies[1].wait()
-    send_3_ref[...] = product(stack, basis, 1, pl.multiple_of((core ^ 1) * half, half), half)
+    send_ref[:, rank:] = product(stack, basis, 1, pl.multiple_of((core ^ 1) * half, half), half)
     keep_3_ref[...] = product(stack, basis, 1, pl.multiple_of(core * half, half), half)
 
 
@@ -173,30 +172,21 @@
         scaled_to(out, keep_ref[:, lanes] + got_ref[:, lanes])
 
 
-def sums_kernel(part_2_ref, got_2_ref, keep_3_ref, got_3_ref, two_ref, *three_refs):
+def sums_kernel(sent_ref, got_ref, keep_3_ref, two_ref, *three_refs):
+    rank = two_ref.shape[1]
     for part, out in enumerate(three_refs):
         width = out.shape[1]
-        lanes = pl.ds(part * width, width)
-        out[...] = (keep_3_ref[:, lanes] + got_3_ref[:, lanes]).astype(BF16)
-    scaled_to(two_ref, part_2_ref[...] + got_2_ref[...])
+        lanes, got_lanes = pl.ds(part * width, width), pl.ds(rank + part * width, width)
+        out[...] = (keep_3_ref[:, lanes] + got_ref[:, got_lanes]).astype(BF16)
+    scaled_to(two_ref, sent_ref[:, :rank] + got_ref[:, :rank])
 
 
 def expanded(coefficient, basis_ref, level, start, width):
     half = coefficient.shape[0] // 2
-    turned = jnp.concatenate([-coefficient[half:], coefficient[:half]], axis=0)
     lanes = pl.ds(start, width)
-    return dot_t(coefficient, basis_ref[level, 0, :, lanes]) + dot_t(
-        turned, basis_ref[level, 1, :, lanes]
-    )
-
-
-def halo_kernel(own_ref, far_ref, three_ref, pair_ref, basis_ref, out_ref):
-    core, _, _ = position()
-    rows, half = three_ref.shape
-    total = own_ref[...] + far_ref[...].astype(F32) + pair_ref[rows:].astype(F32)
-    total += expanded(three_ref[...], basis_ref, 2, pl.multiple_of(core * half, half), half)
-    total += expanded(pair_ref[:rows], basis_ref, 2, pl.multiple_of((1 - core) * half, half), half)
-    out_ref[...] = total
+    by_real = dot_t(coefficient, basis_ref[level, 0, :, lanes])
+    by_imag = dot_t(coefficient, basis_ref[level, 1, :, lanes])
+    return jnp.concatenate([by_real[:half] - by_imag[half:], by_imag[:half] + by_real[half:]], axis=0)
 
 
 def prepare_kernel(order_ref, basis_ref, forward_ref, moved_ref, ahead_ref, hot_ref):
@@ -209,10 +199,25 @@
 
 
 def second_kernel(
-    hot_ref, base_ref, two_ref, two_got_ref, basis_ref, ahead_ref, out_ref, grad_ref
+    hot_ref,
+    own_ref,
+    far_ref,
+    three_ref,
+    pair_ref,
+    two_ref,
+    two_got_ref,
+    basis_ref,
+    ahead_ref,
+    out_ref,
+    grad_ref,
 ):
+    core, _, _ = position()
+    rows, half = three_ref.shape
+    total = own_ref[...] + far_ref[...].astype(F32) + pair_ref[rows:].astype(F32)
+    total += expanded(three_ref[...], basis_ref, 2, pl.multiple_of(core * half, half), half)
+    total += expanded(pair_ref[:rows], basis_ref, 2, pl.multiple_of((1 - core) * half, half), half)
     two = (unscaled_in_kernel(two_ref) + unscaled_in_kernel(two_got_ref)).astype(BF16)
-    total = base_ref[...] + expanded(two, basis_ref, 1, 0, two.shape[1])
+    total += expanded(two, basis_ref, 1, 0, two.shape[1])
     one_hot = hot_ref[...]
     field = jnp.zeros_like(total)
     for _ in range(2):
@@ -262,23 +267,29 @@
         vmem=52 * 1024 * 1024,
     )(tree, row_bases)
     got_1 = swapped(send_1, 1)
-    part_2, send_3, keep_3 = call(
+    send_23, keep_3 = call(
         others_kernel,
-        (array((both, rank), F32), halves, halves),
+        (array((both, rank + half), F32), halves),
         2,
         scratch_shapes=[pltpu.VMEM((2, 2, panels, rank), BF16), pltpu.SemaphoreType.DMA((2,))],
         far=(1,),
         vmem=50 * 1024 * 1024,
     )(stack, row_bases)
 
-    got_1, send_3, part_2 = lax.optimization_barrier((got_1, send_3, part_2))
-    got_3 = swapped(send_3, 1)
-    got_2 = swapped(part_2, 1)
+    got_1, send_23 = lax.optimization_barrier((got_1, send_23))
+    got_23 = swapped(send_23, 1)
     packed = array((both + EXTRA, quarter), F32)
     to_f, to_g = call(spread_kernel, (packed, packed), 2)(keep_1, got_1)
     got_f = by_core(to_f.astype(jnp.float16), 8, 12)
     got_g = by_core(to_g.astype(jnp.float16), 10, 14)
 
+    quarters = array((both, quarter), BF16)
+    two_sent, *three_sent = call(
+        sums_kernel, (array((both + EXTRA, rank), F32), quarters, quarters), 3
+    )(send_23, after(got_23, to_f), keep_3)
+    mine_3 = [swapped(part, 2) for part in three_sent]
+    two_sent = two_sent.astype(jnp.float16)
+    got_cd = by_core(two_sent, 4, 6)
     blocks = near_blocks.shape[1]
     size = near_blocks.shape[3]
     to_core, to_far, own = call(
@@ -287,20 +298,13 @@
         3,
         scratch_shapes=[pltpu.VMEM((3 * blocks, both, size), F32)],
         smem=(0,),
-    )(near_index, after(stack, to_f), near_blocks)
-
-    quarters = array((both, quarter), BF16)
-    two_sent, *three_sent = call(
-        sums_kernel, (array((both + EXTRA, rank), F32), quarters, quarters), 4
-    )(part_2, got_2, keep_3, after(got_3, to_f))
-    mine_3 = [swapped(part, 2) for part in three_sent]
-    two_sent = two_sent.astype(jnp.float16)
-    got_cd = by_core(two_sent, 4, 6)
+    )(near_index, after(stack, two_sent), near_blocks)
+
     peers = lax.axis_size(TREE)
     joints = [(i, i + 1) for i in range(1, peers - 1, 2)]
     far_halo = lax.ppermute(to_far, TREE, joints + [(b, a) for a, b in joints])
 
-    got_f, got_g, _, *mine_3 = lax.optimization_barrier((got_f, got_g, two_sent, *mine_3))
+    got_f, got_g, _, mine_3[0] = lax.optimization_barrier((got_f, got_g, two_sent, mine_3[0]))
     middle = unscaled(got_f) + unscaled(got_g)
     parts = lax.all_gather(middle, "rhs", axis=0)
     quarter_sum = (parts[0] + parts[1]).astype(BF16)
@@ -319,12 +323,21 @@
     mine_3 = jnp.concatenate(mine_3, axis=1)
     mine_3, own, _, _ = lax.optimization_barrier((mine_3, own, quarter_sum, moved))
     pair_3 = swapped(jnp.concatenate([mine_3, to_core], axis=0), 1)
-    base = call(halo_kernel, array((both, panels), F32), 5)(own, far_halo, mine_3, pair_3, col_bases)
     got_cd = after(got_cd, quarter_sum)
     other_cd = swapped(got_cd, 1)
     base, first_grad = call(
-        second_kernel, (array((both, panels), F32), array((1, panels), F32)), 6
-    )(hot, base, got_cd.astype(F32), other_cd.astype(F32), col_bases, ahead)
+        second_kernel, (array((both, panels), F32), array((1, panels), F32)), 9
+    )(
+        hot,
+        own,
+        far_halo,
+        mine_3,
+        pair_3,
+        got_cd.astype(F32),
+        other_cd.astype(F32),
+        col_bases,
+        ahead,
+    )
     mine_1 = jnp.concatenate([got_a, got_b], axis=0)
     field, grad = call(
         last_kernel,

time: 35.8 us -> 33.1 us (0.925)
  starting transfers between devices: 20.1 us -> 14.3 us
  waiting for transfers between devices: 4.15 us -> 6.85 us
  blocking collectives: 2.09 us -> 2.49 us
    ppermute x5, starting transfers between devices: 11.8 us -> 8.15 us  [by_core(): return lax.ppermute(x, TREE, pairs)]
    ppermute x5, waiting for transfers between devices: 3.34 us -> 6.23 us  [by_core(): return lax.ppermute(x, TREE, pairs)]
    ppermute x8 -> x7, starting transfers between devices: 7.47 us -> 5.45 us  [swapped(): lax.ppermute(x, TREE, [(i, i ^ distance) for i in range(lax.axis_size(TRE...]
    pallas_call x3 -> x2, Pallas kernels: 1.57 us -> 1.13 us  [the longest x1 0.85 us: fast_body(): call(others_kernel, (array((both, rank + half), F32), halves), 2, scratch...]
    all_gather x1, blocking collectives: 2.09 us -> 2.49 us  [fast_body(): parts = lax.all_gather(middle, 'rhs', axis=0)]
    ppermute x8 -> x7, waiting for transfers between devices: 0.8 us -> 0.62 us  [swapped(): lax.ppermute(x, TREE, [(i, i ^ distance) for i in range(lax.axis_size(TRE...]
  transfers between devices with their start and end apart: 14 -> 13, of which waited for: 4 -> 4; matrix products, arithmetic and copies ran while one was open for 1% -> 1% of each run, Pallas kernels for 12% -> 12%
where the time goes in v5:
time: 33.1 us; the launch traced here: 32.8 us
  starting transfers between devices  14.3 us (43%)
  waiting for transfers between devices  6.85 us (21%)
  Pallas kernels  6.63 us (20%)
  blocking collectives  2.49 us (8%)
  other arithmetic  1.23 us (4%)
  between operations  0.89 us (3%)
    ppermute x5, starting transfers between devices, by_core(): return lax.ppermute(x, TREE, pairs)  8.15 us
    ppermute x5, waiting for transfers between devices, by_core(): return lax.ppermute(x, TREE, pairs)  6.23 us
    ppermute x7, starting transfers between devices, swapped(): lax.ppermute(x, TREE, [(i, i ^ distance) for i in range(lax.axis_size(TRE...  5.45 us
    all_gather x1, blocking collectives, fast_body(): parts = lax.all_gather(middle, 'rhs', axis=0)  2.49 us
    pallas_call x1, Pallas kernels, fast_body(): call(first_kernel, (array((both, 2 * panels), BF16), halves, halves), 2,...  1.42 us
    pallas_call x1, Pallas kernels, fast_body(): call(near_kernel, (array((both, panels), BF16), array((both, panels), BF1...  1.32 us
    pallas_call x1, Pallas kernels, fast_body(): call(last_kernel, (array((two, rows, panels), F32), array((1, panels), F3...  1.22 us
    pallas_call x1, Pallas kernels, fast_body(): call(second_kernel, (array((both, panels), F32), array((1, panels), F32))...  1.06 us
  transfers between devices with their start and end apart: 13, of which 4 were waited for; matrix products, arithmetic and copies ran while one was open for 1% of the time, Pallas kernels for 12%

profile of v5, /device:TPU:0, one launch (start us, length us, event | category | flops | bytes accessed | tf_op | source)
XLA Modules:
  0.0 32.8 jit_solution(16584788160924920156)
XLA Ops:
  0.6 0.0 copy-start
  0.6 0.0 copy-start.1
  0.7 0.8 %compare_select_fusion = s32[256]{0:T(256)S(1)} fusion(s32[256]{0:T(256)} %param.13), kind=kLoop, calls=%fused_computation.11 | loop fusion | flops 1536 | bytes 2048 | tf_op jit(solution)/shard_map/rem | solution.py:259
  1.5 0.1 copy-done
  1.6 0.2 fusion.tree_ref
  1.8 1.4 %shard_map.86 = (bf16[384,512]{1,0:T(8,128)(2,1)S(1)}, f32[384,256]{1,0:T(8,128)S(1)}, f32[384,256]{1,0:T(8,128)S(1)}) custom-call(bf16[384,256]{1,0:T(8,128)(2,1)S(1)} %fusion.tree_ref, bf16[3,2,256,512]{3,2,1,0:T(8,128)(2,1)} %basis_hbm.3), custom_call_target="tpu_custom_call" | custom-call | tf_op jit(solution)/shard_map/pallas_call | solution.py:261
  3.2 0.5 %collective-permute-start = (f32[384,256]{1,0:T(8,128)S(1)}, f32[384,256]{1,0:T(8,128)S(1)}, u32[]{:S(2)}, u32[]{:S(2)}) collective-permute-start(f32[384,256]{1,0:T(8,128)S(1)} %get-tuple-element.34), channel_id=1, source_target_pairs={{0,1},{1,0},{2,3},{3,2},{4,5},{5,4},{6,7},{7,6},{8,9},{9,8},{10,11... | collective-permute-start | bytes 1179656 | tf_op jit(solution)/shard_map/ppermute | solution.py:45
  3.7 0.9 %shard_map.87 = (f32[384,768]{1,0:T(8,128)S(1)}, f32[384,256]{1,0:T(8,128)S(1)}) custom-call(bf16[384,512]{1,0:T(8,128)(2,1)S(1)} %get-tuple-element.51.stack_ref, bf16[3,2,256,512]{3,2,1,0:T(8,128)(2,1)S(1)} %copy-done.1), custom_call_target="tpu_custom_call" | custom-call | tf_op jit(solution)/shard_map/pallas_call | solution.py:270
  4.6 0.5 %collective-permute-done.got_ref = f32[384,256]{1,0:T(8,128)S(1)} collective-permute-done((f32[384,256]{1,0:T(8,128)S(1)}, f32[384,256]{1,0:T(8,128)S(1)}, u32[]{:S(2)}, u32[]{:S(2)}) %collective-permute-start) | collective-permute-done | bytes 393248 | tf_op jit(solution)/shard_map/ppermute | solution.py:45
  5.1 0.4 %collective-permute-start.3 = (f32[384,768]{1,0:T(8,128)S(1)}, f32[384,768]{1,0:T(8,128)S(1)}, u32[]{:S(2)}, u32[]{:S(2)}) collective-permute-start(f32[384,768]{1,0:T(8,128)S(1)} %get-tuple-element.40.sent_ref), channel_id=1, source_target_pairs={{0,1},{1,0},{2,3},{3,2},{4,5},{5,4},{6,7},{7,6},{8,9},{9,8},{10,11... | collective-permute-start | bytes 3538952 | tf_op jit(solution)/shard_map/ppermute | solution.py:45
  5.5 0.2 shard_map.88
  5.7 3.8 %collective-permute-start.1 = (f16[400,128]{1,0:T(8,128)(2,1)S(1)}, f16[400,128]{1,0:T(8,128)(2,1)S(1)}, u32[]{:S(2)}, u32[]{:S(2)}) collective-permute-start(f16[400,128]{1,0:T(8,128)(2,1)S(1)} %convert_element_type.24), channel_id=1, source_target_pairs={{0,8},{1,13},{2,10},{3,15},{4,12},{5,9},{6,14},{7,11},{8,0},{9,5},... | collective-permute-start | bytes 307208 | tf_op jit(solution)/shard_map/ppermute | solution.py:54
  9.5 1.3 %collective-permute-start.2 = (f16[400,128]{1,0:T(8,128)(2,1)S(1)}, f16[400,128]{1,0:T(8,128)(2,1)S(1)}, u32[]{:S(2)}, u32[]{:S(2)}) collective-permute-start(f16[400,128]{1,0:T(8,128)(2,1)S(1)} %convert_element_type.25), channel_id=1, source_target_pairs={{0,10},{1,15},{2,8},{3,13},{4,14},{5,11},{6,12},{7,9},{8,2},{9,7},... | collective-permute-start | bytes 307208 | tf_op jit(solution)/shard_map/ppermute | solution.py:54
  10.8 0.0 collective-permute-done.3.got_ref
  10.8 0.3 shard_map.89
  11.1 0.3 %collective-permute-start.4 = (bf16[384,128]{1,0:T(8,128)(2,1)S(1)}, bf16[384,128]{1,0:T(8,128)(2,1)S(1)}, u32[]{:S(2)}, u32[]{:S(2)}) collective-permute-start(bf16[384,128]{1,0:T(8,128)(2,1)S(1)} %get-tuple-element.44), channel_id=1, source_target_pairs={{0,2},{1,3},{2,0},{3,1},{4,6},{5,7},{6,4},{7,5},{8,10},{9,11},{10,... | collective-permute-start | bytes 294920 | tf_op jit(solution)/shard_map/ppermute | solution.py:45
  11.4 0.1 convert_element_type.52
  11.5 0.0 copy-start.2
  11.5 0.0 copy-start.4
  11.5 0.0 copy-start.5
  11.5 1.9 %collective-permute-start.8 = (f16[400,512]{1,0:T(8,128)(2,1)S(1)}, f16[400,512]{1,0:T(8,128)(2,1)S(1)}, u32[]{:S(2)}, u32[]{:S(2)}) collective-permute-start(f16[400,512]{1,0:T(8,128)(2,1)S(1)} %convert_element_type.52), channel_id=1, source_target_pairs={{0,4},{1,7},{2,6},{3,5},{4,0},{5,3},{6,2},{7,1},{8,12},{9,15},{10,... | collective-permute-start | bytes 1228808 | tf_op jit(solution)/shard_map/ppermute | solution.py:54
  13.4 1.5 %collective-permute-start.5 = (bf16[384,128]{1,0:T(8,128)(2,1)S(1)}, bf16[384,128]{1,0:T(8,128)(2,1)S(1)}, u32[]{:S(2)}, u32[]{:S(2)}) collective-permute-start(bf16[384,128]{1,0:T(8,128)(2,1)S(1)} %get-tuple-element.50), channel_id=1, source_target_pairs={{0,2},{1,3},{2,0},{3,1},{4,6},{5,7},{6,4},{7,5},{8,10},{9,11},{10,... | collective-permute-start | bytes 294920 | tf_op jit(solution)/shard_map/ppermute | solution.py:45
  14.9 0.0 copy-done.6
  14.9 1.3 %shard_map.91 = (bf16[384,256]{1,0:T(8,128)(2,1)S(1)}, bf16[384,256]{1,0:T(8,128)(2,1)S(1)}, f32[384,256]{1,0:T(8,128)S(1)}) custom-call(s32[2,8]{1,0:T(2,128)S(1)} %copy-done.6, bf16[384,512]{1,0:T(8,128)(2,1)S(1)} %get-tuple-element.51.stack_ref, bf16[2,2,8,128,128]{4,3,2,1,0:T(8,128)(2,1)S(1)} %copy-done.3), custom_call_target="tpu_custom_call" | custom-call | tf_op jit(solution)/shard_map/pallas_call | solution.py:295
  16.3 0.0 collective-permute-done.1
  16.3 0.7 %collective-permute-start.6 = (bf16[384,256]{1,0:T(8,128)(2,1)S(1)}, bf16[384,256]{1,0:T(8,128)(2,1)S(1)}, u32[]{:S(2)}, u32[]{:S(2)}) collective-permute-start(bf16[384,256]{1,0:T(8,128)(2,1)S(1)} %get-tuple-element.55), channel_id=1, source_target_pairs={{1,2},{3,4},{5,6},{7,8},{9,10},{11,12},{13,14},{2,1},{4,3},{6,5},{... | collective-permute-start | bytes 589832 | tf_op jit(solution)/shard_map/ppermute | solution.py:305
  16.9 3.7 %collective-permute-done.2 = f16[400,128]{1,0:T(8,128)(2,1)S(1)} collective-permute-done((f16[400,128]{1,0:T(8,128)(2,1)S(1)}, f16[400,128]{1,0:T(8,128)(2,1)S(1)}, u32[]{:S(2)}, u32[]{:S(2)}) %collective-permute-start.2) | collective-permute-done | bytes 102432 | tf_op jit(solution)/shard_map/ppermute | solution.py:54
  20.6 0.0 collective-permute-done.4
  20.6 0.1 multiply_add_fusion
  20.7 2.5 %all-gather = f32[768,128]{1,0:T(8,128)S(1)} all-gather(f32[384,128]{1,0:T(8,128)S(1)} %multiply_add_fusion), channel_id=2, replica_groups=mesh['groups'=2,'leaf'=8,'rhs'=2] {'rhs'}, dimensions={0}, use_global_device_ids=true | all-gather | bytes 589824 | tf_op jit(solution)/shard_map/all_gather | solution.py:309
  23.2 0.5 %collective-permute-start.10 = (bf16[384,128]{1,0:T(8,128)(2,1)S(1)}, bf16[384,128]{1,0:T(8,128)(2,1)S(1)}, u32[]{:S(2)}, u32[]{:S(2)}) collective-permute-start(bf16[384,128]{1,0:T(8,128)(2,1)S(1)} %fusion.1.own_ref), channel_id=1, source_target_pairs={{0,2},{1,5},{2,0},{3,7},{4,6},{5,1},{6,4},{7,3},{8,10},{9,13},{10,... | collective-permute-start | bytes 294920 | tf_op jit(solution)/shard_map/ppermute | solution.py:54
  23.7 0.7 %collective-permute-start.11 = (bf16[384,128]{1,0:T(8,128)(2,1)S(1)}, bf16[384,128]{1,0:T(8,128)(2,1)S(1)}, u32[]{:S(2)}, u32[]{:S(2)}) collective-permute-start(bf16[384,128]{1,0:T(8,128)(2,1)S(1)} %fusion.1.own_ref), channel_id=1, source_target_pairs={{1,7},{3,5},{5,3},{7,1},{9,15},{11,13},{13,11},{15,9},{17,23},{19,... | collective-permute-start | bytes 294920 | tf_op jit(solution)/shard_map/ppermute | solution.py:54
  24.4 0.3 shard_map.90
  24.7 0.0 collective-permute-done.5
  24.7 2.6 %collective-permute-start.7 = (bf16[768,256]{1,0:T(8,128)(2,1)S(1)}, bf16[768,256]{1,0:T(8,128)(2,1)S(1)}, u32[]{:S(2)}, u32[]{:S(2)}) collective-permute-start(bf16[768,256]{1,0:T(8,128)(2,1)S(1)} %pad_maximum_fusion), channel_id=1, source_target_pairs={{0,1},{1,0},{2,3},{3,2},{4,5},{5,4},{6,7},{7,6},{8,9},{9,8},{10,11... | collective-permute-start | bytes 1179656 | tf_op jit(solution)/shard_map/ppermute | solution.py:45
  27.3 0.0 collective-permute-done.8
  27.3 0.1 collective-permute-start.9
  27.4 2.6 %collective-permute-done.10 = bf16[384,128]{1,0:T(8,128)(2,1)S(1)} collective-permute-done((bf16[384,128]{1,0:T(8,128)(2,1)S(1)}, bf16[384,128]{1,0:T(8,128)(2,1)S(1)}, u32[]{:S(2)}, u32[]{:S(2)}) %collective-permute-start.10) | collective-permute-done | bytes 98336 | tf_op jit(solution)/shard_map/ppermute | solution.py:54
  30.0 0.0 collective-permute-done.11
  30.0 0.1 collective-permute-start.12
  30.1 0.1 convert_element_type.57.two_ref
  30.2 0.0 collective-permute-done.9
  30.2 0.1 convert_element_type.58.two_got_ref
  30.3 0.0 collective-permute-done.6.far_ref
  30.3 0.0 collective-permute-done.7.pair_ref
  30.3 1.1 %shard_map.92 = (f32[384,256]{1,0:T(8,128)S(1)}, f32[1,256]{1,0:T(1,128)S(1)}) custom-call(bf16[256,256]{1,0:T(8,128)(2,1)S(1)} %get-tuple-element.48.hot_ref, f32[384,256]{1,0:T(8,128)S(1)} %get-tuple-element.54.own_ref, bf16[384,256]{1,0:T(8,128)(2,1)S(1)} %collective-permute-done.6.far_ref, bf16[384,256]{1,0:T(8,128)(2,1)S(1)} %pad_maximum_fusion.1.three_ref, ...), custom_call_target="tpu_custom_call" | custom-call | tf_op jit(solution)/shard_map/pallas_call | solution.py:328
  31.4 0.1 collective-permute-done.12.got_ref
  31.5 1.2 %shard_map.93 = (f32[2,192,256]{2,1,0:T(8,128)}, f32[1,256]{1,0:T(1,128)}) custom-call(f32[384,256]{1,0:T(8,128)S(1)} %get-tuple-element.60.base_ref, f32[1,256]{1,0:T(1,128)S(1)} %get-tuple-element.61.first_grad_ref, bf16[384,128]{1,0:T(8,128)(2,1)S(1)} %fusion.1.own_ref, bf16[768,128]{1,0:T(8,128)(2,1)S(1)} %constant_dynamic-update-slice_fusion.mine_ref, ...), custom_call_target="tpu_custom_call" | custom-call | tf_op jit(solution)/shard_map/pallas_call | solution.py:342
  (15 shorter events, 0.2 us)
Async XLA Ops:
  0.6 0.9 %copy-start = (bf16[2,192,256]{2,1,0:T(8,128)(2,1)S(1)}, bf16[2,192,256]{2,1,0:T(8,128)(2,1)}, u32[]{:S(2)}) copy-start(bf16[2,192,256]{2,1,0:T(8,128)(2,1)} %param.7) | copy-start | bytes 589828
  0.6 3.1 %copy-start.1 = (bf16[3,2,256,512]{3,2,1,0:T(8,128)(2,1)S(1)}, bf16[3,2,256,512]{3,2,1,0:T(8,128)(2,1)}, u32[]{:S(2)}) copy-start(bf16[3,2,256,512]{3,2,1,0:T(8,128)(2,1)} %basis_hbm.3) | copy-start | bytes 4718596
  3.2 1.9 %collective-permute-start = (f32[384,256]{1,0:T(8,128)S(1)}, f32[384,256]{1,0:T(8,128)S(1)}, u32[]{:S(2)}, u32[]{:S(2)}) collective-permute-start(f32[384,256]{1,0:T(8,128)S(1)} %get-tuple-element.34), channel_id=1, source_target_pairs={{0,1},{1,0},{2,3},{3,2},{4,5},{5,4},{6,7},{7,6},{8,9},{9,8},{10,11... | collective-permute-start | bytes 1179656 | tf_op jit(solution)/shard_map/ppermute | solution.py:45
  5.1 5.7 %collective-permute-start.3 = (f32[384,768]{1,0:T(8,128)S(1)}, f32[384,768]{1,0:T(8,128)S(1)}, u32[]{:S(2)}, u32[]{:S(2)}) collective-permute-start(f32[384,768]{1,0:T(8,128)S(1)} %get-tuple-element.40.sent_ref), channel_id=1, source_target_pairs={{0,1},{1,0},{2,3},{3,2},{4,5},{5,4},{6,7},{7,6},{8,9},{9,8},{10,11... | collective-permute-start | bytes 3538952 | tf_op jit(solution)/shard_map/ppermute | solution.py:45
  5.7 10.6 %collective-permute-start.1 = (f16[400,128]{1,0:T(8,128)(2,1)S(1)}, f16[400,128]{1,0:T(8,128)(2,1)S(1)}, u32[]{:S(2)}, u32[]{:S(2)}) collective-permute-start(f16[400,128]{1,0:T(8,128)(2,1)S(1)} %convert_element_type.24), channel_id=1, source_target_pairs={{0,8},{1,13},{2,10},{3,15},{4,12},{5,9},{6,14},{7,11},{8,0},{9,5},... | collective-permute-start | bytes 307208 | tf_op jit(solution)/shard_map/ppermute | solution.py:54
  9.5 11.1 %collective-permute-start.2 = (f16[400,128]{1,0:T(8,128)(2,1)S(1)}, f16[400,128]{1,0:T(8,128)(2,1)S(1)}, u32[]{:S(2)}, u32[]{:S(2)}) collective-permute-start(f16[400,128]{1,0:T(8,128)(2,1)S(1)} %convert_element_type.25), channel_id=1, source_target_pairs={{0,10},{1,15},{2,8},{3,13},{4,14},{5,11},{6,12},{7,9},{8,2},{9,7},... | collective-permute-start | bytes 307208 | tf_op jit(solution)/shard_map/ppermute | solution.py:54
  10.8 4.1 %copy-start.3 = (bf16[2,2,8,128,128]{4,3,2,1,0:T(8,128)(2,1)S(1)}, bf16[2,2,8,128,128]{4,3,2,1,0:T(8,128)(2,1)}, u32[]{:S(2)}) copy-start(bf16[2,2,8,128,128]{4,3,2,1,0:T(8,128)(2,1)} %near_ref.1) | copy-start | bytes 3145732
  10.8 4.1 %copy-start.6 = (s32[2,8]{1,0:T(2,128)S(1)}, s32[2,8]{1,0:T(2,128)}, u32[]{:S(2)}) copy-start(s32[2,8]{1,0:T(2,128)} %index_ref.1) | copy-start | bytes 196
  11.1 9.5 %collective-permute-start.4 = (bf16[384,128]{1,0:T(8,128)(2,1)S(1)}, bf16[384,128]{1,0:T(8,128)(2,1)S(1)}, u32[]{:S(2)}, u32[]{:S(2)}) collective-permute-start(bf16[384,128]{1,0:T(8,128)(2,1)S(1)} %get-tuple-element.44), channel_id=1, source_target_pairs={{0,2},{1,3},{2,0},{3,1},{4,6},{5,7},{6,4},{7,5},{8,10},{9,11},{10,... | collective-permute-start | bytes 294920 | tf_op jit(solution)/shard_map/ppermute | solution.py:45
  11.5 12.8 %copy-start.2 = (bf16[3,2,256,512]{3,2,1,0:T(8,128)(2,1)S(1)}, bf16[3,2,256,512]{3,2,1,0:T(8,128)(2,1)}, u32[]{:S(2)}) copy-start(bf16[3,2,256,512]{3,2,1,0:T(8,128)(2,1)} %basis_ref.3) | copy-start | bytes 4718596
  11.5 12.8 %copy-start.4 = (bf16[2,192,256]{2,1,0:T(8,128)(2,1)S(1)}, bf16[2,192,256]{2,1,0:T(8,128)(2,1)}, u32[]{:S(2)}) copy-start(bf16[2,192,256]{2,1,0:T(8,128)(2,1)} %forward_ref.1) | copy-start | bytes 589828
  11.5 12.8 %copy-start.5 = (s32[256]{0:T(256)S(1)}, s32[256]{0:T(256)}, u32[]{:S(2)}) copy-start(s32[256]{0:T(256)} %param.13) | copy-start | bytes 3076
  11.5 15.8 %collective-permute-start.8 = (f16[400,512]{1,0:T(8,128)(2,1)S(1)}, f16[400,512]{1,0:T(8,128)(2,1)S(1)}, u32[]{:S(2)}, u32[]{:S(2)}) collective-permute-start(f16[400,512]{1,0:T(8,128)(2,1)S(1)} %convert_element_type.52), channel_id=1, source_target_pairs={{0,4},{1,7},{2,6},{3,5},{4,0},{5,3},{6,2},{7,1},{8,12},{9,15},{10,... | collective-permute-start | bytes 1228808 | tf_op jit(solution)/shard_map/ppermute | solution.py:54
  13.4 11.2 %collective-permute-start.5 = (bf16[384,128]{1,0:T(8,128)(2,1)S(1)}, bf16[384,128]{1,0:T(8,128)(2,1)S(1)}, u32[]{:S(2)}, u32[]{:S(2)}) collective-permute-start(bf16[384,128]{1,0:T(8,128)(2,1)S(1)} %get-tuple-element.50), channel_id=1, source_target_pairs={{0,2},{1,3},{2,0},{3,1},{4,6},{5,7},{6,4},{7,5},{8,10},{9,11},{10,... | collective-permute-start | bytes 294920 | tf_op jit(solution)/shard_map/ppermute | solution.py:45
  16.3 14.1 %collective-permute-start.6 = (bf16[384,256]{1,0:T(8,128)(2,1)S(1)}, bf16[384,256]{1,0:T(8,128)(2,1)S(1)}, u32[]{:S(2)}, u32[]{:S(2)}) collective-permute-start(bf16[384,256]{1,0:T(8,128)(2,1)S(1)} %get-tuple-element.55), channel_id=1, source_target_pairs={{1,2},{3,4},{5,6},{7,8},{9,10},{11,12},{13,14},{2,1},{4,3},{6,5},{... | collective-permute-start | bytes 589832 | tf_op jit(solution)/shard_map/ppermute | solution.py:305
  23.2 6.8 %collective-permute-start.10 = (bf16[384,128]{1,0:T(8,128)(2,1)S(1)}, bf16[384,128]{1,0:T(8,128)(2,1)S(1)}, u32[]{:S(2)}, u32[]{:S(2)}) collective-permute-start(bf16[384,128]{1,0:T(8,128)(2,1)S(1)} %fusion.1.own_ref), channel_id=1, source_target_pairs={{0,2},{1,5},{2,0},{3,7},{4,6},{5,1},{6,4},{7,3},{8,10},{9,13},{10,... | collective-permute-start | bytes 294920 | tf_op jit(solution)/shard_map/ppermute | solution.py:54
  23.7 6.3 %collective-permute-start.11 = (bf16[384,128]{1,0:T(8,128)(2,1)S(1)}, bf16[384,128]{1,0:T(8,128)(2,1)S(1)}, u32[]{:S(2)}, u32[]{:S(2)}) collective-permute-start(bf16[384,128]{1,0:T(8,128)(2,1)S(1)} %fusion.1.own_ref), channel_id=1, source_target_pairs={{1,7},{3,5},{5,3},{7,1},{9,15},{11,13},{13,11},{15,9},{17,23},{19,... | collective-permute-start | bytes 294920 | tf_op jit(solution)/shard_map/ppermute | solution.py:54
  24.7 5.6 %collective-permute-start.7 = (bf16[768,256]{1,0:T(8,128)(2,1)S(1)}, bf16[768,256]{1,0:T(8,128)(2,1)S(1)}, u32[]{:S(2)}, u32[]{:S(2)}) collective-permute-start(bf16[768,256]{1,0:T(8,128)(2,1)S(1)} %pad_maximum_fusion), channel_id=1, source_target_pairs={{0,1},{1,0},{2,3},{3,2},{4,5},{5,4},{6,7},{7,6},{8,9},{9,8},{10,11... | collective-permute-start | bytes 1179656 | tf_op jit(solution)/shard_map/ppermute | solution.py:45
  27.3 2.9 %collective-permute-start.9 = (f16[400,512]{1,0:T(8,128)(2,1)S(1)}, f16[400,512]{1,0:T(8,128)(2,1)S(1)}, u32[]{:S(2)}, u32[]{:S(2)}) collective-permute-start(f16[400,512]{1,0:T(8,128)(2,1)S(1)} %collective-permute-done.8), channel_id=1, source_target_pairs={{0,1},{1,0},{2,3},{3,2},{4,5},{5,4},{6,7},{7,6},{8,9},{9,8},{10,11... | collective-permute-start | bytes 1228808 | tf_op jit(solution)/shard_map/ppermute | solution.py:45
  30.0 1.5 %collective-permute-start.12 = (bf16[768,128]{1,0:T(8,128)(2,1)S(1)}, bf16[768,128]{1,0:T(8,128)(2,1)S(1)}, u32[]{:S(2)}, u32[]{:S(2)}) collective-permute-start(bf16[768,128]{1,0:T(8,128)(2,1)S(1)} %constant_dynamic-update-slice_fusion.mine_ref), channel_id=1, source_target_pairs={{0,1},{1,0},{2,3},{3,2},{4,5},{5,4},{6,7},{7,6},{8,9},{9,8},{10,11... | collective-permute-start | bytes 589832 | tf_op jit(solution)/shard_map/ppermute | solution.py:45

commit v6 on v5

--- a/solution.py
+++ b/solution.py
@@ -151,10 +151,10 @@
         stack = jnp.concatenate(
             [stack_ref[:, j * size : (j + 1) * size] for j in (i, block_count + i)], axis=1
         )
-        for k in range(0, neighbours, 2):
-            pair = jnp.concatenate([near_ref[:, i, k], near_ref[:, i, k + 1]], axis=2)
-            terms = dot(stack, pair.reshape(2 * size, 2 * size))
-            for j in range(2):
+        for k in range(0, neighbours, 4):
+            four = jnp.concatenate([near_ref[:, i, k + j] for j in range(4)], axis=2)
+            terms = dot(stack, four.reshape(2 * size, 4 * size))
+            for j in range(4):
                 target = jnp.clip(index_ref[i, k + j] - base, 0, 3 * block_count - 1)
                 sums[target] += terms[:, j * size : (j + 1) * size]
     for j in range(block_count):

time: 33.1 us -> 33.1 us (level)
  no operation moved by 1% of the time
where the time goes in v6:
time: 33.1 us; the launch traced here: 32.8 us
  starting transfers between devices  14.3 us (43%)
  waiting for transfers between devices  6.85 us (21%)
  Pallas kernels  6.64 us (20%)
  blocking collectives  2.49 us (8%)
  other arithmetic  1.23 us (4%)
  between operations  0.89 us (3%)
    ppermute x5, starting transfers between devices, by_core(): return lax.ppermute(x, TREE, pairs)  8.15 us
    ppermute x5, waiting for transfers between devices, by_core(): return lax.ppermute(x, TREE, pairs)  6.22 us
    ppermute x7, starting transfers between devices, swapped(): lax.ppermute(x, TREE, [(i, i ^ distance) for i in range(lax.axis_size(TRE...  5.45 us
    all_gather x1, blocking collectives, fast_body(): parts = lax.all_gather(middle, 'rhs', axis=0)  2.49 us
    pallas_call x1, Pallas kernels, fast_body(): call(first_kernel, (array((both, 2 * panels), BF16), halves, halves), 2,...  1.42 us
    pallas_call x1, Pallas kernels, fast_body(): call(near_kernel, (array((both, panels), BF16), array((both, panels), BF1...  1.33 us
    pallas_call x1, Pallas kernels, fast_body(): call(last_kernel, (array((two, rows, panels), F32), array((1, panels), F3...  1.22 us
    pallas_call x1, Pallas kernels, fast_body(): call(second_kernel, (array((both, panels), F32), array((1, panels), F32))...  1.06 us
  transfers between devices with their start and end apart: 13, of which 4 were waited for; matrix products, arithmetic and copies ran while one was open for 1% of the time, Pallas kernels for 12%

profile of v6, /device:TPU:0, one launch (start us, length us, event | category | flops | bytes accessed | tf_op | source)
XLA Modules:
  0.0 32.8 jit_solution(1353603163069053421)
XLA Ops:
  0.6 0.0 copy-start
  0.6 0.0 copy-start.1
  0.7 0.8 %compare_select_fusion = s32[256]{0:T(256)S(1)} fusion(s32[256]{0:T(256)} %param.13), kind=kLoop, calls=%fused_computation.11 | loop fusion | flops 1536 | bytes 2048 | tf_op jit(solution)/shard_map/rem | solution.py:259
  1.5 0.1 copy-done
  1.6 0.2 fusion.tree_ref
  1.8 1.4 %shard_map.86 = (bf16[384,512]{1,0:T(8,128)(2,1)S(1)}, f32[384,256]{1,0:T(8,128)S(1)}, f32[384,256]{1,0:T(8,128)S(1)}) custom-call(bf16[384,256]{1,0:T(8,128)(2,1)S(1)} %fusion.tree_ref, bf16[3,2,256,512]{3,2,1,0:T(8,128)(2,1)} %basis_hbm.3), custom_call_target="tpu_custom_call" | custom-call | tf_op jit(solution)/shard_map/pallas_call | solution.py:261
  3.2 0.5 %collective-permute-start = (f32[384,256]{1,0:T(8,128)S(1)}, f32[384,256]{1,0:T(8,128)S(1)}, u32[]{:S(2)}, u32[]{:S(2)}) collective-permute-start(f32[384,256]{1,0:T(8,128)S(1)} %get-tuple-element.34), channel_id=1, source_target_pairs={{0,1},{1,0},{2,3},{3,2},{4,5},{5,4},{6,7},{7,6},{8,9},{9,8},{10,11... | collective-permute-start | bytes 1179656 | tf_op jit(solution)/shard_map/ppermute | solution.py:45
  3.7 0.9 %shard_map.87 = (f32[384,768]{1,0:T(8,128)S(1)}, f32[384,256]{1,0:T(8,128)S(1)}) custom-call(bf16[384,512]{1,0:T(8,128)(2,1)S(1)} %get-tuple-element.51.stack_ref, bf16[3,2,256,512]{3,2,1,0:T(8,128)(2,1)S(1)} %copy-done.1), custom_call_target="tpu_custom_call" | custom-call | tf_op jit(solution)/shard_map/pallas_call | solution.py:270
  4.6 0.5 %collective-permute-done.got_ref = f32[384,256]{1,0:T(8,128)S(1)} collective-permute-done((f32[384,256]{1,0:T(8,128)S(1)}, f32[384,256]{1,0:T(8,128)S(1)}, u32[]{:S(2)}, u32[]{:S(2)}) %collective-permute-start) | collective-permute-done | bytes 393248 | tf_op jit(solution)/shard_map/ppermute | solution.py:45
  5.1 0.4 %collective-permute-start.3 = (f32[384,768]{1,0:T(8,128)S(1)}, f32[384,768]{1,0:T(8,128)S(1)}, u32[]{:S(2)}, u32[]{:S(2)}) collective-permute-start(f32[384,768]{1,0:T(8,128)S(1)} %get-tuple-element.40.sent_ref), channel_id=1, source_target_pairs={{0,1},{1,0},{2,3},{3,2},{4,5},{5,4},{6,7},{7,6},{8,9},{9,8},{10,11... | collective-permute-start | bytes 3538952 | tf_op jit(solution)/shard_map/ppermute | solution.py:45
  5.5 0.2 shard_map.88
  5.7 3.8 %collective-permute-start.1 = (f16[400,128]{1,0:T(8,128)(2,1)S(1)}, f16[400,128]{1,0:T(8,128)(2,1)S(1)}, u32[]{:S(2)}, u32[]{:S(2)}) collective-permute-start(f16[400,128]{1,0:T(8,128)(2,1)S(1)} %convert_element_type.24), channel_id=1, source_target_pairs={{0,8},{1,13},{2,10},{3,15},{4,12},{5,9},{6,14},{7,11},{8,0},{9,5},... | collective-permute-start | bytes 307208 | tf_op jit(solution)/shard_map/ppermute | solution.py:54
  9.5 1.3 %collective-permute-start.2 = (f16[400,128]{1,0:T(8,128)(2,1)S(1)}, f16[400,128]{1,0:T(8,128)(2,1)S(1)}, u32[]{:S(2)}, u32[]{:S(2)}) collective-permute-start(f16[400,128]{1,0:T(8,128)(2,1)S(1)} %convert_element_type.25), channel_id=1, source_target_pairs={{0,10},{1,15},{2,8},{3,13},{4,14},{5,11},{6,12},{7,9},{8,2},{9,7},... | collective-permute-start | bytes 307208 | tf_op jit(solution)/shard_map/ppermute | solution.py:54
  10.8 0.0 collective-permute-done.3.got_ref
  10.8 0.3 shard_map.89
  11.1 0.3 %collective-permute-start.4 = (bf16[384,128]{1,0:T(8,128)(2,1)S(1)}, bf16[384,128]{1,0:T(8,128)(2,1)S(1)}, u32[]{:S(2)}, u32[]{:S(2)}) collective-permute-start(bf16[384,128]{1,0:T(8,128)(2,1)S(1)} %get-tuple-element.44), channel_id=1, source_target_pairs={{0,2},{1,3},{2,0},{3,1},{4,6},{5,7},{6,4},{7,5},{8,10},{9,11},{10,... | collective-permute-start | bytes 294920 | tf_op jit(solution)/shard_map/ppermute | solution.py:45
  11.4 0.1 convert_element_type.52
  11.5 0.0 copy-start.2
  11.5 0.0 copy-start.4
  11.5 0.0 copy-start.5
  11.5 1.9 %collective-permute-start.8 = (f16[400,512]{1,0:T(8,128)(2,1)S(1)}, f16[400,512]{1,0:T(8,128)(2,1)S(1)}, u32[]{:S(2)}, u32[]{:S(2)}) collective-permute-start(f16[400,512]{1,0:T(8,128)(2,1)S(1)} %convert_element_type.52), channel_id=1, source_target_pairs={{0,4},{1,7},{2,6},{3,5},{4,0},{5,3},{6,2},{7,1},{8,12},{9,15},{10,... | collective-permute-start | bytes 1228808 | tf_op jit(solution)/shard_map/ppermute | solution.py:54
  13.4 1.5 %collective-permute-start.5 = (bf16[384,128]{1,0:T(8,128)(2,1)S(1)}, bf16[384,128]{1,0:T(8,128)(2,1)S(1)}, u32[]{:S(2)}, u32[]{:S(2)}) collective-permute-start(bf16[384,128]{1,0:T(8,128)(2,1)S(1)} %get-tuple-element.50), channel_id=1, source_target_pairs={{0,2},{1,3},{2,0},{3,1},{4,6},{5,7},{6,4},{7,5},{8,10},{9,11},{10,... | collective-permute-start | bytes 294920 | tf_op jit(solution)/shard_map/ppermute | solution.py:45
  14.9 0.0 copy-done.6
  14.9 1.3 %shard_map.91 = (bf16[384,256]{1,0:T(8,128)(2,1)S(1)}, bf16[384,256]{1,0:T(8,128)(2,1)S(1)}, f32[384,256]{1,0:T(8,128)S(1)}) custom-call(s32[2,8]{1,0:T(2,128)S(1)} %copy-done.6, bf16[384,512]{1,0:T(8,128)(2,1)S(1)} %get-tuple-element.51.stack_ref, bf16[2,2,8,128,128]{4,3,2,1,0:T(8,128)(2,1)S(1)} %copy-done.3), custom_call_target="tpu_custom_call" | custom-call | tf_op jit(solution)/shard_map/pallas_call | solution.py:295
  16.3 0.0 collective-permute-done.1
  16.3 0.7 %collective-permute-start.6 = (bf16[384,256]{1,0:T(8,128)(2,1)S(1)}, bf16[384,256]{1,0:T(8,128)(2,1)S(1)}, u32[]{:S(2)}, u32[]{:S(2)}) collective-permute-start(bf16[384,256]{1,0:T(8,128)(2,1)S(1)} %get-tuple-element.55), channel_id=1, source_target_pairs={{1,2},{3,4},{5,6},{7,8},{9,10},{11,12},{13,14},{2,1},{4,3},{6,5},{... | collective-permute-start | bytes 589832 | tf_op jit(solution)/shard_map/ppermute | solution.py:305
  17.0 3.6 %collective-permute-done.2 = f16[400,128]{1,0:T(8,128)(2,1)S(1)} collective-permute-done((f16[400,128]{1,0:T(8,128)(2,1)S(1)}, f16[400,128]{1,0:T(8,128)(2,1)S(1)}, u32[]{:S(2)}, u32[]{:S(2)}) %collective-permute-start.2) | collective-permute-done | bytes 102432 | tf_op jit(solution)/shard_map/ppermute | solution.py:54
  20.6 0.0 collective-permute-done.4
  20.6 0.1 multiply_add_fusion
  20.7 2.5 %all-gather = f32[768,128]{1,0:T(8,128)S(1)} all-gather(f32[384,128]{1,0:T(8,128)S(1)} %multiply_add_fusion), channel_id=2, replica_groups=mesh['groups'=2,'leaf'=8,'rhs'=2] {'rhs'}, dimensions={0}, use_global_device_ids=true | all-gather | bytes 589824 | tf_op jit(solution)/shard_map/all_gather | solution.py:309
  23.2 0.5 %collective-permute-start.10 = (bf16[384,128]{1,0:T(8,128)(2,1)S(1)}, bf16[384,128]{1,0:T(8,128)(2,1)S(1)}, u32[]{:S(2)}, u32[]{:S(2)}) collective-permute-start(bf16[384,128]{1,0:T(8,128)(2,1)S(1)} %fusion.1.own_ref), channel_id=1, source_target_pairs={{0,2},{1,5},{2,0},{3,7},{4,6},{5,1},{6,4},{7,3},{8,10},{9,13},{10,... | collective-permute-start | bytes 294920 | tf_op jit(solution)/shard_map/ppermute | solution.py:54
  23.7 0.7 %collective-permute-start.11 = (bf16[384,128]{1,0:T(8,128)(2,1)S(1)}, bf16[384,128]{1,0:T(8,128)(2,1)S(1)}, u32[]{:S(2)}, u32[]{:S(2)}) collective-permute-start(bf16[384,128]{1,0:T(8,128)(2,1)S(1)} %fusion.1.own_ref), channel_id=1, source_target_pairs={{1,7},{3,5},{5,3},{7,1},{9,15},{11,13},{13,11},{15,9},{17,23},{19,... | collective-permute-start | bytes 294920 | tf_op jit(solution)/shard_map/ppermute | solution.py:54
  24.4 0.3 shard_map.90
  24.7 0.0 collective-permute-done.5
  24.7 2.6 %collective-permute-start.7 = (bf16[768,256]{1,0:T(8,128)(2,1)S(1)}, bf16[768,256]{1,0:T(8,128)(2,1)S(1)}, u32[]{:S(2)}, u32[]{:S(2)}) collective-permute-start(bf16[768,256]{1,0:T(8,128)(2,1)S(1)} %pad_maximum_fusion), channel_id=1, source_target_pairs={{0,1},{1,0},{2,3},{3,2},{4,5},{5,4},{6,7},{7,6},{8,9},{9,8},{10,11... | collective-permute-start | bytes 1179656 | tf_op jit(solution)/shard_map/ppermute | solution.py:45
  27.3 0.0 collective-permute-done.8
  27.3 0.1 collective-permute-start.9
  27.4 2.6 %collective-permute-done.10 = bf16[384,128]{1,0:T(8,128)(2,1)S(1)} collective-permute-done((bf16[384,128]{1,0:T(8,128)(2,1)S(1)}, bf16[384,128]{1,0:T(8,128)(2,1)S(1)}, u32[]{:S(2)}, u32[]{:S(2)}) %collective-permute-start.10) | collective-permute-done | bytes 98336 | tf_op jit(solution)/shard_map/ppermute | solution.py:54
  30.0 0.0 collective-permute-done.11
  30.0 0.1 collective-permute-start.12
  30.1 0.1 convert_element_type.57.two_ref
  30.2 0.0 collective-permute-done.9
  30.2 0.1 convert_element_type.58.two_got_ref
  30.3 0.0 collective-permute-done.6.far_ref
  30.3 0.0 collective-permute-done.7.pair_ref
  30.3 1.1 %shard_map.92 = (f32[384,256]{1,0:T(8,128)S(1)}, f32[1,256]{1,0:T(1,128)S(1)}) custom-call(bf16[256,256]{1,0:T(8,128)(2,1)S(1)} %get-tuple-element.48.hot_ref, f32[384,256]{1,0:T(8,128)S(1)} %get-tuple-element.54.own_ref, bf16[384,256]{1,0:T(8,128)(2,1)S(1)} %collective-permute-done.6.far_ref, bf16[384,256]{1,0:T(8,128)(2,1)S(1)} %pad_maximum_fusion.1.three_ref, ...), custom_call_target="tpu_custom_call" | custom-call | tf_op jit(solution)/shard_map/pallas_call | solution.py:328
  31.4 0.1 collective-permute-done.12.got_ref
  31.5 1.2 %shard_map.93 = (f32[2,192,256]{2,1,0:T(8,128)}, f32[1,256]{1,0:T(1,128)}) custom-call(f32[384,256]{1,0:T(8,128)S(1)} %get-tuple-element.60.base_ref, f32[1,256]{1,0:T(1,128)S(1)} %get-tuple-element.61.first_grad_ref, bf16[384,128]{1,0:T(8,128)(2,1)S(1)} %fusion.1.own_ref, bf16[768,128]{1,0:T(8,128)(2,1)S(1)} %constant_dynamic-update-slice_fusion.mine_ref, ...), custom_call_target="tpu_custom_call" | custom-call | tf_op jit(solution)/shard_map/pallas_call | solution.py:342
  (15 shorter events, 0.2 us)
Async XLA Ops:
  0.6 0.9 %copy-start = (bf16[2,192,256]{2,1,0:T(8,128)(2,1)S(1)}, bf16[2,192,256]{2,1,0:T(8,128)(2,1)}, u32[]{:S(2)}) copy-start(bf16[2,192,256]{2,1,0:T(8,128)(2,1)} %param.7) | copy-start | bytes 589828
  0.6 3.1 %copy-start.1 = (bf16[3,2,256,512]{3,2,1,0:T(8,128)(2,1)S(1)}, bf16[3,2,256,512]{3,2,1,0:T(8,128)(2,1)}, u32[]{:S(2)}) copy-start(bf16[3,2,256,512]{3,2,1,0:T(8,128)(2,1)} %basis_hbm.3) | copy-start | bytes 4718596
  3.2 1.9 %collective-permute-start = (f32[384,256]{1,0:T(8,128)S(1)}, f32[384,256]{1,0:T(8,128)S(1)}, u32[]{:S(2)}, u32[]{:S(2)}) collective-permute-start(f32[384,256]{1,0:T(8,128)S(1)} %get-tuple-element.34), channel_id=1, source_target_pairs={{0,1},{1,0},{2,3},{3,2},{4,5},{5,4},{6,7},{7,6},{8,9},{9,8},{10,11... | collective-permute-start | bytes 1179656 | tf_op jit(solution)/shard_map/ppermute | solution.py:45
  5.1 5.7 %collective-permute-start.3 = (f32[384,768]{1,0:T(8,128)S(1)}, f32[384,768]{1,0:T(8,128)S(1)}, u32[]{:S(2)}, u32[]{:S(2)}) collective-permute-start(f32[384,768]{1,0:T(8,128)S(1)} %get-tuple-element.40.sent_ref), channel_id=1, source_target_pairs={{0,1},{1,0},{2,3},{3,2},{4,5},{5,4},{6,7},{7,6},{8,9},{9,8},{10,11... | collective-permute-start | bytes 3538952 | tf_op jit(solution)/shard_map/ppermute | solution.py:45
  5.7 10.6 %collective-permute-start.1 = (f16[400,128]{1,0:T(8,128)(2,1)S(1)}, f16[400,128]{1,0:T(8,128)(2,1)S(1)}, u32[]{:S(2)}, u32[]{:S(2)}) collective-permute-start(f16[400,128]{1,0:T(8,128)(2,1)S(1)} %convert_element_type.24), channel_id=1, source_target_pairs={{0,8},{1,13},{2,10},{3,15},{4,12},{5,9},{6,14},{7,11},{8,0},{9,5},... | collective-permute-start | bytes 307208 | tf_op jit(solution)/shard_map/ppermute | solution.py:54
  9.5 11.1 %collective-permute-start.2 = (f16[400,128]{1,0:T(8,128)(2,1)S(1)}, f16[400,128]{1,0:T(8,128)(2,1)S(1)}, u32[]{:S(2)}, u32[]{:S(2)}) collective-permute-start(f16[400,128]{1,0:T(8,128)(2,1)S(1)} %convert_element_type.25), channel_id=1, source_target_pairs={{0,10},{1,15},{2,8},{3,13},{4,14},{5,11},{6,12},{7,9},{8,2},{9,7},... | collective-permute-start | bytes 307208 | tf_op jit(solution)/shard_map/ppermute | solution.py:54
  10.8 4.1 %copy-start.3 = (bf16[2,2,8,128,128]{4,3,2,1,0:T(8,128)(2,1)S(1)}, bf16[2,2,8,128,128]{4,3,2,1,0:T(8,128)(2,1)}, u32[]{:S(2)}) copy-start(bf16[2,2,8,128,128]{4,3,2,1,0:T(8,128)(2,1)} %near_ref.1) | copy-start | bytes 3145732
  10.8 4.1 %copy-start.6 = (s32[2,8]{1,0:T(2,128)S(1)}, s32[2,8]{1,0:T(2,128)}, u32[]{:S(2)}) copy-start(s32[2,8]{1,0:T(2,128)} %index_ref.1) | copy-start | bytes 196
  11.1 9.5 %collective-permute-start.4 = (bf16[384,128]{1,0:T(8,128)(2,1)S(1)}, bf16[384,128]{1,0:T(8,128)(2,1)S(1)}, u32[]{:S(2)}, u32[]{:S(2)}) collective-permute-start(bf16[384,128]{1,0:T(8,128)(2,1)S(1)} %get-tuple-element.44), channel_id=1, source_target_pairs={{0,2},{1,3},{2,0},{3,1},{4,6},{5,7},{6,4},{7,5},{8,10},{9,11},{10,... | collective-permute-start | bytes 294920 | tf_op jit(solution)/shard_map/ppermute | solution.py:45
  11.5 12.8 %copy-start.2 = (bf16[3,2,256,512]{3,2,1,0:T(8,128)(2,1)S(1)}, bf16[3,2,256,512]{3,2,1,0:T(8,128)(2,1)}, u32[]{:S(2)}) copy-start(bf16[3,2,256,512]{3,2,1,0:T(8,128)(2,1)} %basis_ref.3) | copy-start | bytes 4718596
  11.5 12.8 %copy-start.4 = (bf16[2,192,256]{2,1,0:T(8,128)(2,1)S(1)}, bf16[2,192,256]{2,1,0:T(8,128)(2,1)}, u32[]{:S(2)}) copy-start(bf16[2,192,256]{2,1,0:T(8,128)(2,1)} %forward_ref.1) | copy-start | bytes 589828
  11.5 12.8 %copy-start.5 = (s32[256]{0:T(256)S(1)}, s32[256]{0:T(256)}, u32[]{:S(2)}) copy-start(s32[256]{0:T(256)} %param.13) | copy-start | bytes 3076
  11.5 15.8 %collective-permute-start.8 = (f16[400,512]{1,0:T(8,128)(2,1)S(1)}, f16[400,512]{1,0:T(8,128)(2,1)S(1)}, u32[]{:S(2)}, u32[]{:S(2)}) collective-permute-start(f16[400,512]{1,0:T(8,128)(2,1)S(1)} %convert_element_type.52), channel_id=1, source_target_pairs={{0,4},{1,7},{2,6},{3,5},{4,0},{5,3},{6,2},{7,1},{8,12},{9,15},{10,... | collective-permute-start | bytes 1228808 | tf_op jit(solution)/shard_map/ppermute | solution.py:54
  13.4 11.2 %collective-permute-start.5 = (bf16[384,128]{1,0:T(8,128)(2,1)S(1)}, bf16[384,128]{1,0:T(8,128)(2,1)S(1)}, u32[]{:S(2)}, u32[]{:S(2)}) collective-permute-start(bf16[384,128]{1,0:T(8,128)(2,1)S(1)} %get-tuple-element.50), channel_id=1, source_target_pairs={{0,2},{1,3},{2,0},{3,1},{4,6},{5,7},{6,4},{7,5},{8,10},{9,11},{10,... | collective-permute-start | bytes 294920 | tf_op jit(solution)/shard_map/ppermute | solution.py:45
  16.3 14.1 %collective-permute-start.6 = (bf16[384,256]{1,0:T(8,128)(2,1)S(1)}, bf16[384,256]{1,0:T(8,128)(2,1)S(1)}, u32[]{:S(2)}, u32[]{:S(2)}) collective-permute-start(bf16[384,256]{1,0:T(8,128)(2,1)S(1)} %get-tuple-element.55), channel_id=1, source_target_pairs={{1,2},{3,4},{5,6},{7,8},{9,10},{11,12},{13,14},{2,1},{4,3},{6,5},{... | collective-permute-start | bytes 589832 | tf_op jit(solution)/shard_map/ppermute | solution.py:305
  23.2 6.8 %collective-permute-start.10 = (bf16[384,128]{1,0:T(8,128)(2,1)S(1)}, bf16[384,128]{1,0:T(8,128)(2,1)S(1)}, u32[]{:S(2)}, u32[]{:S(2)}) collective-permute-start(bf16[384,128]{1,0:T(8,128)(2,1)S(1)} %fusion.1.own_ref), channel_id=1, source_target_pairs={{0,2},{1,5},{2,0},{3,7},{4,6},{5,1},{6,4},{7,3},{8,10},{9,13},{10,... | collective-permute-start | bytes 294920 | tf_op jit(solution)/shard_map/ppermute | solution.py:54
  23.7 6.3 %collective-permute-start.11 = (bf16[384,128]{1,0:T(8,128)(2,1)S(1)}, bf16[384,128]{1,0:T(8,128)(2,1)S(1)}, u32[]{:S(2)}, u32[]{:S(2)}) collective-permute-start(bf16[384,128]{1,0:T(8,128)(2,1)S(1)} %fusion.1.own_ref), channel_id=1, source_target_pairs={{1,7},{3,5},{5,3},{7,1},{9,15},{11,13},{13,11},{15,9},{17,23},{19,... | collective-permute-start | bytes 294920 | tf_op jit(solution)/shard_map/ppermute | solution.py:54
  24.7 5.6 %collective-permute-start.7 = (bf16[768,256]{1,0:T(8,128)(2,1)S(1)}, bf16[768,256]{1,0:T(8,128)(2,1)S(1)}, u32[]{:S(2)}, u32[]{:S(2)}) collective-permute-start(bf16[768,256]{1,0:T(8,128)(2,1)S(1)} %pad_maximum_fusion), channel_id=1, source_target_pairs={{0,1},{1,0},{2,3},{3,2},{4,5},{5,4},{6,7},{7,6},{8,9},{9,8},{10,11... | collective-permute-start | bytes 1179656 | tf_op jit(solution)/shard_map/ppermute | solution.py:45
  27.3 2.9 %collective-permute-start.9 = (f16[400,512]{1,0:T(8,128)(2,1)S(1)}, f16[400,512]{1,0:T(8,128)(2,1)S(1)}, u32[]{:S(2)}, u32[]{:S(2)}) collective-permute-start(f16[400,512]{1,0:T(8,128)(2,1)S(1)} %collective-permute-done.8), channel_id=1, source_target_pairs={{0,1},{1,0},{2,3},{3,2},{4,5},{5,4},{6,7},{7,6},{8,9},{9,8},{10,11... | collective-permute-start | bytes 1228808 | tf_op jit(solution)/shard_map/ppermute | solution.py:45
  30.0 1.5 %collective-permute-start.12 = (bf16[768,128]{1,0:T(8,128)(2,1)S(1)}, bf16[768,128]{1,0:T(8,128)(2,1)S(1)}, u32[]{:S(2)}, u32[]{:S(2)}) collective-permute-start(bf16[768,128]{1,0:T(8,128)(2,1)S(1)} %constant_dynamic-update-slice_fusion.mine_ref), channel_id=1, source_target_pairs={{0,1},{1,0},{2,3},{3,2},{4,5},{5,4},{6,7},{7,6},{8,9},{9,8},{10,11... | collective-permute-start | bytes 589832 | tf_op jit(solution)/shard_map/ppermute | solution.py:45

commit v7 on v5

--- a/solution.py
+++ b/solution.py
@@ -304,7 +304,7 @@
     joints = [(i, i + 1) for i in range(1, peers - 1, 2)]
     far_halo = lax.ppermute(to_far, TREE, joints + [(b, a) for a, b in joints])
 
-    got_f, got_g, _, mine_3[0] = lax.optimization_barrier((got_f, got_g, two_sent, mine_3[0]))
+    got_f, got_g, _, mine_3[1] = lax.optimization_barrier((got_f, got_g, two_sent, mine_3[1]))
     middle = unscaled(got_f) + unscaled(got_g)
     parts = lax.all_gather(middle, "rhs", axis=0)
     quarter_sum = (parts[0] + parts[1]).astype(BF16)

time: 33.1 us -> 33.1 us (level)
  no operation moved by 1% of the time
where the time goes in v7:
time: 33.1 us; the launch traced here: 32.8 us
  starting transfers between devices  14.3 us (43%)
  waiting for transfers between devices  6.85 us (21%)
  Pallas kernels  6.63 us (20%)
  blocking collectives  2.49 us (8%)
  other arithmetic  1.23 us (4%)
  between operations  0.89 us (3%)
    ppermute x5, starting transfers between devices, by_core(): return lax.ppermute(x, TREE, pairs)  8.15 us
    ppermute x5, waiting for transfers between devices, by_core(): return lax.ppermute(x, TREE, pairs)  6.23 us
    ppermute x7, starting transfers between devices, swapped(): lax.ppermute(x, TREE, [(i, i ^ distance) for i in range(lax.axis_size(TRE...  5.45 us
    all_gather x1, blocking collectives, fast_body(): parts = lax.all_gather(middle, 'rhs', axis=0)  2.49 us
    pallas_call x1, Pallas kernels, fast_body(): call(first_kernel, (array((both, 2 * panels), BF16), halves, halves), 2,...  1.42 us
    pallas_call x1, Pallas kernels, fast_body(): call(near_kernel, (array((both, panels), BF16), array((both, panels), BF1...  1.32 us
    pallas_call x1, Pallas kernels, fast_body(): call(last_kernel, (array((two, rows, panels), F32), array((1, panels), F3...  1.22 us
    pallas_call x1, Pallas kernels, fast_body(): call(second_kernel, (array((both, panels), F32), array((1, panels), F32))...  1.06 us
  transfers between devices with their start and end apart: 13, of which 4 were waited for; matrix products, arithmetic and copies ran while one was open for 1% of the time, Pallas kernels for 12%

profile of v7, /device:TPU:0, one launch (start us, length us, event | category | flops | bytes accessed | tf_op | source)
XLA Modules:
  0.0 32.8 jit_solution(1258295547850147611)
XLA Ops:
  0.6 0.0 copy-start
  0.6 0.0 copy-start.1
  0.7 0.8 %compare_select_fusion = s32[256]{0:T(256)S(1)} fusion(s32[256]{0:T(256)} %param.13), kind=kLoop, calls=%fused_computation.11 | loop fusion | flops 1536 | bytes 2048 | tf_op jit(solution)/shard_map/rem | solution.py:259
  1.5 0.1 copy-done
  1.6 0.2 fusion.tree_ref
  1.8 1.4 %shard_map.86 = (bf16[384,512]{1,0:T(8,128)(2,1)S(1)}, f32[384,256]{1,0:T(8,128)S(1)}, f32[384,256]{1,0:T(8,128)S(1)}) custom-call(bf16[384,256]{1,0:T(8,128)(2,1)S(1)} %fusion.tree_ref, bf16[3,2,256,512]{3,2,1,0:T(8,128)(2,1)} %basis_hbm.3), custom_call_target="tpu_custom_call" | custom-call | tf_op jit(solution)/shard_map/pallas_call | solution.py:261
  3.2 0.5 %collective-permute-start = (f32[384,256]{1,0:T(8,128)S(1)}, f32[384,256]{1,0:T(8,128)S(1)}, u32[]{:S(2)}, u32[]{:S(2)}) collective-permute-start(f32[384,256]{1,0:T(8,128)S(1)} %get-tuple-element.34), channel_id=1, source_target_pairs={{0,1},{1,0},{2,3},{3,2},{4,5},{5,4},{6,7},{7,6},{8,9},{9,8},{10,11... | collective-permute-start | bytes 1179656 | tf_op jit(solution)/shard_map/ppermute | solution.py:45
  3.7 0.9 %shard_map.87 = (f32[384,768]{1,0:T(8,128)S(1)}, f32[384,256]{1,0:T(8,128)S(1)}) custom-call(bf16[384,512]{1,0:T(8,128)(2,1)S(1)} %get-tuple-element.51.stack_ref, bf16[3,2,256,512]{3,2,1,0:T(8,128)(2,1)S(1)} %copy-done.1), custom_call_target="tpu_custom_call" | custom-call | tf_op jit(solution)/shard_map/pallas_call | solution.py:270
  4.6 0.5 %collective-permute-done.got_ref = f32[384,256]{1,0:T(8,128)S(1)} collective-permute-done((f32[384,256]{1,0:T(8,128)S(1)}, f32[384,256]{1,0:T(8,128)S(1)}, u32[]{:S(2)}, u32[]{:S(2)}) %collective-permute-start) | collective-permute-done | bytes 393248 | tf_op jit(solution)/shard_map/ppermute | solution.py:45
  5.1 0.4 %collective-permute-start.3 = (f32[384,768]{1,0:T(8,128)S(1)}, f32[384,768]{1,0:T(8,128)S(1)}, u32[]{:S(2)}, u32[]{:S(2)}) collective-permute-start(f32[384,768]{1,0:T(8,128)S(1)} %get-tuple-element.40.sent_ref), channel_id=1, source_target_pairs={{0,1},{1,0},{2,3},{3,2},{4,5},{5,4},{6,7},{7,6},{8,9},{9,8},{10,11... | collective-permute-start | bytes 3538952 | tf_op jit(solution)/shard_map/ppermute | solution.py:45
  5.5 0.2 shard_map.88
  5.7 3.8 %collective-permute-start.1 = (f16[400,128]{1,0:T(8,128)(2,1)S(1)}, f16[400,128]{1,0:T(8,128)(2,1)S(1)}, u32[]{:S(2)}, u32[]{:S(2)}) collective-permute-start(f16[400,128]{1,0:T(8,128)(2,1)S(1)} %convert_element_type.24), channel_id=1, source_target_pairs={{0,8},{1,13},{2,10},{3,15},{4,12},{5,9},{6,14},{7,11},{8,0},{9,5},... | collective-permute-start | bytes 307208 | tf_op jit(solution)/shard_map/ppermute | solution.py:54
  9.5 1.3 %collective-permute-start.2 = (f16[400,128]{1,0:T(8,128)(2,1)S(1)}, f16[400,128]{1,0:T(8,128)(2,1)S(1)}, u32[]{:S(2)}, u32[]{:S(2)}) collective-permute-start(f16[400,128]{1,0:T(8,128)(2,1)S(1)} %convert_element_type.25), channel_id=1, source_target_pairs={{0,10},{1,15},{2,8},{3,13},{4,14},{5,11},{6,12},{7,9},{8,2},{9,7},... | collective-permute-start | bytes 307208 | tf_op jit(solution)/shard_map/ppermute | solution.py:54
  10.8 0.0 collective-permute-done.3.got_ref
  10.8 0.3 shard_map.89
  11.1 0.3 %collective-permute-start.4 = (bf16[384,128]{1,0:T(8,128)(2,1)S(1)}, bf16[384,128]{1,0:T(8,128)(2,1)S(1)}, u32[]{:S(2)}, u32[]{:S(2)}) collective-permute-start(bf16[384,128]{1,0:T(8,128)(2,1)S(1)} %get-tuple-element.44), channel_id=1, source_target_pairs={{0,2},{1,3},{2,0},{3,1},{4,6},{5,7},{6,4},{7,5},{8,10},{9,11},{10,... | collective-permute-start | bytes 294920 | tf_op jit(solution)/shard_map/ppermute | solution.py:45
  11.4 0.1 convert_element_type.52
  11.5 0.0 copy-start.2
  11.5 0.0 copy-start.4
  11.5 0.0 copy-start.5
  11.5 1.9 %collective-permute-start.8 = (f16[400,512]{1,0:T(8,128)(2,1)S(1)}, f16[400,512]{1,0:T(8,128)(2,1)S(1)}, u32[]{:S(2)}, u32[]{:S(2)}) collective-permute-start(f16[400,512]{1,0:T(8,128)(2,1)S(1)} %convert_element_type.52), channel_id=1, source_target_pairs={{0,4},{1,7},{2,6},{3,5},{4,0},{5,3},{6,2},{7,1},{8,12},{9,15},{10,... | collective-permute-start | bytes 1228808 | tf_op jit(solution)/shard_map/ppermute | solution.py:54
  13.4 1.5 %collective-permute-start.5 = (bf16[384,128]{1,0:T(8,128)(2,1)S(1)}, bf16[384,128]{1,0:T(8,128)(2,1)S(1)}, u32[]{:S(2)}, u32[]{:S(2)}) collective-permute-start(bf16[384,128]{1,0:T(8,128)(2,1)S(1)} %get-tuple-element.49), channel_id=1, source_target_pairs={{0,2},{1,3},{2,0},{3,1},{4,6},{5,7},{6,4},{7,5},{8,10},{9,11},{10,... | collective-permute-start | bytes 294920 | tf_op jit(solution)/shard_map/ppermute | solution.py:45
  14.9 0.0 copy-done.6
  14.9 1.3 %shard_map.91 = (bf16[384,256]{1,0:T(8,128)(2,1)S(1)}, bf16[384,256]{1,0:T(8,128)(2,1)S(1)}, f32[384,256]{1,0:T(8,128)S(1)}) custom-call(s32[2,8]{1,0:T(2,128)S(1)} %copy-done.6, bf16[384,512]{1,0:T(8,128)(2,1)S(1)} %get-tuple-element.51.stack_ref, bf16[2,2,8,128,128]{4,3,2,1,0:T(8,128)(2,1)S(1)} %copy-done.3), custom_call_target="tpu_custom_call" | custom-call | tf_op jit(solution)/shard_map/pallas_call | solution.py:295
  16.3 0.0 collective-permute-done.1
  16.3 0.7 %collective-permute-start.6 = (bf16[384,256]{1,0:T(8,128)(2,1)S(1)}, bf16[384,256]{1,0:T(8,128)(2,1)S(1)}, u32[]{:S(2)}, u32[]{:S(2)}) collective-permute-start(bf16[384,256]{1,0:T(8,128)(2,1)S(1)} %get-tuple-element.55), channel_id=1, source_target_pairs={{1,2},{3,4},{5,6},{7,8},{9,10},{11,12},{13,14},{2,1},{4,3},{6,5},{... | collective-permute-start | bytes 589832 | tf_op jit(solution)/shard_map/ppermute | solution.py:305
  16.9 3.7 %collective-permute-done.2 = f16[400,128]{1,0:T(8,128)(2,1)S(1)} collective-permute-done((f16[400,128]{1,0:T(8,128)(2,1)S(1)}, f16[400,128]{1,0:T(8,128)(2,1)S(1)}, u32[]{:S(2)}, u32[]{:S(2)}) %collective-permute-start.2) | collective-permute-done | bytes 102432 | tf_op jit(solution)/shard_map/ppermute | solution.py:54
  20.6 0.0 collective-permute-done.4
  20.6 0.1 multiply_add_fusion
  20.7 2.5 %all-gather = f32[768,128]{1,0:T(8,128)S(1)} all-gather(f32[384,128]{1,0:T(8,128)S(1)} %multiply_add_fusion), channel_id=2, replica_groups=mesh['groups'=2,'leaf'=8,'rhs'=2] {'rhs'}, dimensions={0}, use_global_device_ids=true | all-gather | bytes 589824 | tf_op jit(solution)/shard_map/all_gather | solution.py:309
  23.2 0.5 %collective-permute-start.10 = (bf16[384,128]{1,0:T(8,128)(2,1)S(1)}, bf16[384,128]{1,0:T(8,128)(2,1)S(1)}, u32[]{:S(2)}, u32[]{:S(2)}) collective-permute-start(bf16[384,128]{1,0:T(8,128)(2,1)S(1)} %fusion.1.own_ref), channel_id=1, source_target_pairs={{0,2},{1,5},{2,0},{3,7},{4,6},{5,1},{6,4},{7,3},{8,10},{9,13},{10,... | collective-permute-start | bytes 294920 | tf_op jit(solution)/shard_map/ppermute | solution.py:54
  23.7 0.7 %collective-permute-start.11 = (bf16[384,128]{1,0:T(8,128)(2,1)S(1)}, bf16[384,128]{1,0:T(8,128)(2,1)S(1)}, u32[]{:S(2)}, u32[]{:S(2)}) collective-permute-start(bf16[384,128]{1,0:T(8,128)(2,1)S(1)} %fusion.1.own_ref), channel_id=1, source_target_pairs={{1,7},{3,5},{5,3},{7,1},{9,15},{11,13},{13,11},{15,9},{17,23},{19,... | collective-permute-start | bytes 294920 | tf_op jit(solution)/shard_map/ppermute | solution.py:54
  24.4 0.3 shard_map.90
  24.7 0.0 collective-permute-done.5
  24.7 2.6 %collective-permute-start.7 = (bf16[768,256]{1,0:T(8,128)(2,1)S(1)}, bf16[768,256]{1,0:T(8,128)(2,1)S(1)}, u32[]{:S(2)}, u32[]{:S(2)}) collective-permute-start(bf16[768,256]{1,0:T(8,128)(2,1)S(1)} %pad_maximum_fusion), channel_id=1, source_target_pairs={{0,1},{1,0},{2,3},{3,2},{4,5},{5,4},{6,7},{7,6},{8,9},{9,8},{10,11... | collective-permute-start | bytes 1179656 | tf_op jit(solution)/shard_map/ppermute | solution.py:45
  27.3 0.0 collective-permute-done.8
  27.3 0.1 collective-permute-start.9
  27.4 2.6 %collective-permute-done.10 = bf16[384,128]{1,0:T(8,128)(2,1)S(1)} collective-permute-done((bf16[384,128]{1,0:T(8,128)(2,1)S(1)}, bf16[384,128]{1,0:T(8,128)(2,1)S(1)}, u32[]{:S(2)}, u32[]{:S(2)}) %collective-permute-start.10) | collective-permute-done | bytes 98336 | tf_op jit(solution)/shard_map/ppermute | solution.py:54
  30.0 0.0 collective-permute-done.11
  30.0 0.1 collective-permute-start.12
  30.1 0.1 convert_element_type.57.two_ref
  30.2 0.0 collective-permute-done.9
  30.2 0.1 convert_element_type.58.two_got_ref
  30.3 0.0 collective-permute-done.6.far_ref
  30.3 0.0 collective-permute-done.7.pair_ref
  30.3 1.1 %shard_map.92 = (f32[384,256]{1,0:T(8,128)S(1)}, f32[1,256]{1,0:T(1,128)S(1)}) custom-call(bf16[256,256]{1,0:T(8,128)(2,1)S(1)} %get-tuple-element.48.hot_ref, f32[384,256]{1,0:T(8,128)S(1)} %get-tuple-element.54.own_ref, bf16[384,256]{1,0:T(8,128)(2,1)S(1)} %collective-permute-done.6.far_ref, bf16[384,256]{1,0:T(8,128)(2,1)S(1)} %pad_maximum_fusion.1.three_ref, ...), custom_call_target="tpu_custom_call" | custom-call | tf_op jit(solution)/shard_map/pallas_call | solution.py:328
  31.4 0.1 collective-permute-done.12.got_ref
  31.5 1.2 %shard_map.93 = (f32[2,192,256]{2,1,0:T(8,128)}, f32[1,256]{1,0:T(1,128)}) custom-call(f32[384,256]{1,0:T(8,128)S(1)} %get-tuple-element.60.base_ref, f32[1,256]{1,0:T(1,128)S(1)} %get-tuple-element.61.first_grad_ref, bf16[384,128]{1,0:T(8,128)(2,1)S(1)} %fusion.1.own_ref, bf16[768,128]{1,0:T(8,128)(2,1)S(1)} %constant_dynamic-update-slice_fusion.mine_ref, ...), custom_call_target="tpu_custom_call" | custom-call | tf_op jit(solution)/shard_map/pallas_call | solution.py:342
  (15 shorter events, 0.2 us)
Async XLA Ops:
  0.6 0.9 %copy-start = (bf16[2,192,256]{2,1,0:T(8,128)(2,1)S(1)}, bf16[2,192,256]{2,1,0:T(8,128)(2,1)}, u32[]{:S(2)}) copy-start(bf16[2,192,256]{2,1,0:T(8,128)(2,1)} %param.7) | copy-start | bytes 589828
  0.6 3.1 %copy-start.1 = (bf16[3,2,256,512]{3,2,1,0:T(8,128)(2,1)S(1)}, bf16[3,2,256,512]{3,2,1,0:T(8,128)(2,1)}, u32[]{:S(2)}) copy-start(bf16[3,2,256,512]{3,2,1,0:T(8,128)(2,1)} %basis_hbm.3) | copy-start | bytes 4718596
  3.2 1.9 %collective-permute-start = (f32[384,256]{1,0:T(8,128)S(1)}, f32[384,256]{1,0:T(8,128)S(1)}, u32[]{:S(2)}, u32[]{:S(2)}) collective-permute-start(f32[384,256]{1,0:T(8,128)S(1)} %get-tuple-element.34), channel_id=1, source_target_pairs={{0,1},{1,0},{2,3},{3,2},{4,5},{5,4},{6,7},{7,6},{8,9},{9,8},{10,11... | collective-permute-start | bytes 1179656 | tf_op jit(solution)/shard_map/ppermute | solution.py:45
  5.1 5.7 %collective-permute-start.3 = (f32[384,768]{1,0:T(8,128)S(1)}, f32[384,768]{1,0:T(8,128)S(1)}, u32[]{:S(2)}, u32[]{:S(2)}) collective-permute-start(f32[384,768]{1,0:T(8,128)S(1)} %get-tuple-element.40.sent_ref), channel_id=1, source_target_pairs={{0,1},{1,0},{2,3},{3,2},{4,5},{5,4},{6,7},{7,6},{8,9},{9,8},{10,11... | collective-permute-start | bytes 3538952 | tf_op jit(solution)/shard_map/ppermute | solution.py:45
  5.7 10.6 %collective-permute-start.1 = (f16[400,128]{1,0:T(8,128)(2,1)S(1)}, f16[400,128]{1,0:T(8,128)(2,1)S(1)}, u32[]{:S(2)}, u32[]{:S(2)}) collective-permute-start(f16[400,128]{1,0:T(8,128)(2,1)S(1)} %convert_element_type.24), channel_id=1, source_target_pairs={{0,8},{1,13},{2,10},{3,15},{4,12},{5,9},{6,14},{7,11},{8,0},{9,5},... | collective-permute-start | bytes 307208 | tf_op jit(solution)/shard_map/ppermute | solution.py:54
  9.5 11.1 %collective-permute-start.2 = (f16[400,128]{1,0:T(8,128)(2,1)S(1)}, f16[400,128]{1,0:T(8,128)(2,1)S(1)}, u32[]{:S(2)}, u32[]{:S(2)}) collective-permute-start(f16[400,128]{1,0:T(8,128)(2,1)S(1)} %convert_element_type.25), channel_id=1, source_target_pairs={{0,10},{1,15},{2,8},{3,13},{4,14},{5,11},{6,12},{7,9},{8,2},{9,7},... | collective-permute-start | bytes 307208 | tf_op jit(solution)/shard_map/ppermute | solution.py:54
  10.8 4.1 %copy-start.3 = (bf16[2,2,8,128,128]{4,3,2,1,0:T(8,128)(2,1)S(1)}, bf16[2,2,8,128,128]{4,3,2,1,0:T(8,128)(2,1)}, u32[]{:S(2)}) copy-start(bf16[2,2,8,128,128]{4,3,2,1,0:T(8,128)(2,1)} %near_ref.1) | copy-start | bytes 3145732
  10.8 4.1 %copy-start.6 = (s32[2,8]{1,0:T(2,128)S(1)}, s32[2,8]{1,0:T(2,128)}, u32[]{:S(2)}) copy-start(s32[2,8]{1,0:T(2,128)} %index_ref.1) | copy-start | bytes 196
  11.1 9.5 %collective-permute-start.4 = (bf16[384,128]{1,0:T(8,128)(2,1)S(1)}, bf16[384,128]{1,0:T(8,128)(2,1)S(1)}, u32[]{:S(2)}, u32[]{:S(2)}) collective-permute-start(bf16[384,128]{1,0:T(8,128)(2,1)S(1)} %get-tuple-element.44), channel_id=1, source_target_pairs={{0,2},{1,3},{2,0},{3,1},{4,6},{5,7},{6,4},{7,5},{8,10},{9,11},{10,... | collective-permute-start | bytes 294920 | tf_op jit(solution)/shard_map/ppermute | solution.py:45
  11.5 12.8 %copy-start.2 = (bf16[3,2,256,512]{3,2,1,0:T(8,128)(2,1)S(1)}, bf16[3,2,256,512]{3,2,1,0:T(8,128)(2,1)}, u32[]{:S(2)}) copy-start(bf16[3,2,256,512]{3,2,1,0:T(8,128)(2,1)} %basis_ref.3) | copy-start | bytes 4718596
  11.5 12.8 %copy-start.4 = (bf16[2,192,256]{2,1,0:T(8,128)(2,1)S(1)}, bf16[2,192,256]{2,1,0:T(8,128)(2,1)}, u32[]{:S(2)}) copy-start(bf16[2,192,256]{2,1,0:T(8,128)(2,1)} %forward_ref.1) | copy-start | bytes 589828
  11.5 12.8 %copy-start.5 = (s32[256]{0:T(256)S(1)}, s32[256]{0:T(256)}, u32[]{:S(2)}) copy-start(s32[256]{0:T(256)} %param.13) | copy-start | bytes 3076
  11.5 15.8 %collective-permute-start.8 = (f16[400,512]{1,0:T(8,128)(2,1)S(1)}, f16[400,512]{1,0:T(8,128)(2,1)S(1)}, u32[]{:S(2)}, u32[]{:S(2)}) collective-permute-start(f16[400,512]{1,0:T(8,128)(2,1)S(1)} %convert_element_type.52), channel_id=1, source_target_pairs={{0,4},{1,7},{2,6},{3,5},{4,0},{5,3},{6,2},{7,1},{8,12},{9,15},{10,... | collective-permute-start | bytes 1228808 | tf_op jit(solution)/shard_map/ppermute | solution.py:54
  13.4 11.2 %collective-permute-start.5 = (bf16[384,128]{1,0:T(8,128)(2,1)S(1)}, bf16[384,128]{1,0:T(8,128)(2,1)S(1)}, u32[]{:S(2)}, u32[]{:S(2)}) collective-permute-start(bf16[384,128]{1,0:T(8,128)(2,1)S(1)} %get-tuple-element.49), channel_id=1, source_target_pairs={{0,2},{1,3},{2,0},{3,1},{4,6},{5,7},{6,4},{7,5},{8,10},{9,11},{10,... | collective-permute-start | bytes 294920 | tf_op jit(solution)/shard_map/ppermute | solution.py:45
  16.3 14.1 %collective-permute-start.6 = (bf16[384,256]{1,0:T(8,128)(2,1)S(1)}, bf16[384,256]{1,0:T(8,128)(2,1)S(1)}, u32[]{:S(2)}, u32[]{:S(2)}) collective-permute-start(bf16[384,256]{1,0:T(8,128)(2,1)S(1)} %get-tuple-element.55), channel_id=1, source_target_pairs={{1,2},{3,4},{5,6},{7,8},{9,10},{11,12},{13,14},{2,1},{4,3},{6,5},{... | collective-permute-start | bytes 589832 | tf_op jit(solution)/shard_map/ppermute | solution.py:305
  23.2 6.8 %collective-permute-start.10 = (bf16[384,128]{1,0:T(8,128)(2,1)S(1)}, bf16[384,128]{1,0:T(8,128)(2,1)S(1)}, u32[]{:S(2)}, u32[]{:S(2)}) collective-permute-start(bf16[384,128]{1,0:T(8,128)(2,1)S(1)} %fusion.1.own_ref), channel_id=1, source_target_pairs={{0,2},{1,5},{2,0},{3,7},{4,6},{5,1},{6,4},{7,3},{8,10},{9,13},{10,... | collective-permute-start | bytes 294920 | tf_op jit(solution)/shard_map/ppermute | solution.py:54
  23.7 6.3 %collective-permute-start.11 = (bf16[384,128]{1,0:T(8,128)(2,1)S(1)}, bf16[384,128]{1,0:T(8,128)(2,1)S(1)}, u32[]{:S(2)}, u32[]{:S(2)}) collective-permute-start(bf16[384,128]{1,0:T(8,128)(2,1)S(1)} %fusion.1.own_ref), channel_id=1, source_target_pairs={{1,7},{3,5},{5,3},{7,1},{9,15},{11,13},{13,11},{15,9},{17,23},{19,... | collective-permute-start | bytes 294920 | tf_op jit(solution)/shard_map/ppermute | solution.py:54
  24.7 5.6 %collective-permute-start.7 = (bf16[768,256]{1,0:T(8,128)(2,1)S(1)}, bf16[768,256]{1,0:T(8,128)(2,1)S(1)}, u32[]{:S(2)}, u32[]{:S(2)}) collective-permute-start(bf16[768,256]{1,0:T(8,128)(2,1)S(1)} %pad_maximum_fusion), channel_id=1, source_target_pairs={{0,1},{1,0},{2,3},{3,2},{4,5},{5,4},{6,7},{7,6},{8,9},{9,8},{10,11... | collective-permute-start | bytes 1179656 | tf_op jit(solution)/shard_map/ppermute | solution.py:45
  27.3 2.9 %collective-permute-start.9 = (f16[400,512]{1,0:T(8,128)(2,1)S(1)}, f16[400,512]{1,0:T(8,128)(2,1)S(1)}, u32[]{:S(2)}, u32[]{:S(2)}) collective-permute-start(f16[400,512]{1,0:T(8,128)(2,1)S(1)} %collective-permute-done.8), channel_id=1, source_target_pairs={{0,1},{1,0},{2,3},{3,2},{4,5},{5,4},{6,7},{7,6},{8,9},{9,8},{10,11... | collective-permute-start | bytes 1228808 | tf_op jit(solution)/shard_map/ppermute | solution.py:45
  30.0 1.5 %collective-permute-start.12 = (bf16[768,128]{1,0:T(8,128)(2,1)S(1)}, bf16[768,128]{1,0:T(8,128)(2,1)S(1)}, u32[]{:S(2)}, u32[]{:S(2)}) collective-permute-start(bf16[768,128]{1,0:T(8,128)(2,1)S(1)} %constant_dynamic-update-slice_fusion.mine_ref), channel_id=1, source_target_pairs={{0,1},{1,0},{2,3},{3,2},{4,5},{5,4},{6,7},{7,6},{8,9},{9,8},{10,11... | collective-permute-start | bytes 589832 | tf_op jit(solution)/shard_map/ppermute | solution.py:45
